TPU v7x, 32 devices: a whole 2x2x4 slice. The times are simulated.
32 devices in a mesh: tm: 16 (over z, y, core), space: 2 (over x).
Axes of the slice: x: 2, y: 2, z: 4, core: 2. Of those that a mesh axis runs over, the one named last changes fastest.
Arguments:
- queries: bfloat16 [4096, 4096], P(('tm', 'space')), may hold values from -14 to 14
- keys: bfloat16 [4096, 2048], P(('tm', 'space')), may hold values from -6 to 6
- values: bfloat16 [4096, 2048], P(('tm', 'space')), may hold values from -6 to 6
- output_gradient: bfloat16 [4096, 4096], P(('tm', 'space')), may hold values from -6 to 6
- tiles: int32 [32, 6], P('tm'), may hold values from 0 to 5, as said below
- kinds: int32 [32, 6], P('tm'), may hold values from 0 to 2, as said below
Outputs:
- grad_queries: bfloat16 [4096, 4096], P(('tm', 'space'))
- grad_keys: bfloat16 [4096, 2048], P(('tm', 'space'))
- grad_values: bfloat16 [4096, 2048], P(('tm', 'space'))
Inputs may be any that keep to these rules, and one draw needn't show every extreme that they name: Row b lists the key tiles of query block b, which lies in window w = b // 2 at block b % 2 of it. A value v names kv block v % 2 of window w - v // 2; windows below 0 are never named, nor, where v // 2 = 0, blocks at or after b % 2 except in slot 0. Slot 0 holds b % 2; slots 1 to u hold distinct other values, u from 0 to 5, ragged over the blocks; the remaining slots hold 0. Every draw has rows with u = 5 and names the largest value. `kinds`: kind 0: every key of the tile is visible; kind 1: a key is visible when its position in its tile is at most the query's position in its block; kind 2: the slot is unused. Slot 0 has kind 1, used slots kind 0 or 1, unused slots kind 2.
All inputs are finite; a program needn't handle non-finite values.
Results may differ from a plain program's by a relative error of at most 0.015.
Values may be sent and summed in bfloat16 or wider, within the bound.
No kernel may reach another device: no remote copies, remote signals or barrier semaphores. Data moves between devices by JAX's collectives and lax.ppermute only.
A program may use at most 128 MiB of HBM per device.

v0:
```python
import math

import jax
import jax.numpy as jnp
from jax import lax
from jax.sharding import PartitionSpec as P

HEAD_SIZE = 128
BLOCK_TOKENS = 128
MAXT = 6
REACH = 2


def shifted_2(block, axis, distance):
    devices = range(lax.axis_size(axis))
    route = [(i - distance, i) for i in devices if i - distance in devices]
    return lax.ppermute(block, axis, route)


def block_grads(query_rows, grad_rows, key_tiles, value_tiles, tile_kinds):
    blocks, length, kv_count, head_dim = key_tiles.shape
    score_scale = 1.0 / head_dim**0.5
    key_flat = key_tiles.reshape(blocks * length, kv_count, head_dim)
    value_flat = value_tiles.reshape(blocks * length, kv_count, head_dim)
    scores = (
        jnp.einsum("qkgd,tkd->kgqt", query_rows, key_flat, preferred_element_type=jnp.float32)
        * score_scale
    )
    query_pos = jnp.arange(length)
    column_kind = jnp.repeat(tile_kinds, length)
    column_pos = jnp.tile(jnp.arange(length), blocks)
    visible = (column_kind == 0)[None, :] | (column_kind == 1)[None, :] & (
        column_pos[None, :] <= query_pos[:, None]
    )
    masked = jnp.where(visible, scores, -jnp.inf)
    row_max = jnp.max(masked, axis=-1, keepdims=True)
    weights = jnp.where(visible, jnp.exp(masked - row_max), 0.0)
    probabilities = weights / jnp.sum(weights, axis=-1, keepdims=True)
    probs_low = probabilities.astype(jnp.bfloat16)
    outputs = jnp.einsum(
        "kgqt,tkd->qkgd", probs_low, value_flat, preferred_element_type=jnp.float32
    )
    row_delta = jnp.einsum("qkgd,qkgd->kgq", grad_rows.astype(jnp.float32), outputs)
    grad_probs = jnp.einsum(
        "qkgd,tkd->kgqt", grad_rows, value_flat, preferred_element_type=jnp.float32
    )
    grad_scores = (score_scale * probabilities * (grad_probs - row_delta[..., None])).astype(
        jnp.bfloat16
    )
    grad_query = jnp.einsum(
        "kgqt,tkd->qkgd", grad_scores, key_flat, preferred_element_type=jnp.float32
    )
    grad_key = jnp.einsum(
        "kgqt,qkgd->tkd", grad_scores, query_rows, preferred_element_type=jnp.float32
    )
    grad_value = jnp.einsum(
        "kgqt,qkgd->tkd", probs_low, grad_rows, preferred_element_type=jnp.float32
    )
    return (
        grad_query.astype(jnp.bfloat16),
        grad_key.reshape(blocks, length, kv_count, head_dim),
        grad_value.reshape(blocks, length, kv_count, head_dim),
    )


def body(queries, keys, values, output_gradient, tiles, kinds):
    query_heads, grad_heads, key_heads, value_heads = (
        lax.all_to_all(queries, "space", split_axis=1, concat_axis=0, tiled=True),
        lax.all_to_all(output_gradient, "space", split_axis=1, concat_axis=0, tiled=True),
        lax.all_to_all(keys, "space", split_axis=1, concat_axis=0, tiled=True),
        lax.all_to_all(values, "space", split_axis=1, concat_axis=0, tiled=True),
    )
    window = query_heads.shape[0]
    kv_heads = key_heads.shape[1] // HEAD_SIZE
    head_groups = query_heads.shape[1] // key_heads.shape[1]
    per_window = window // BLOCK_TOKENS
    earlier = [shifted_2((key_heads, value_heads), "tm", offset) for offset in range(1, REACH + 1)]
    tile_count = (REACH + 1) * per_window
    key_tiles = jnp.concatenate([key_heads] + [shifted[0] for shifted in earlier], axis=0)
    key_tiles = key_tiles.reshape(tile_count, BLOCK_TOKENS, kv_heads, HEAD_SIZE)
    value_tiles = jnp.concatenate([value_heads] + [shifted[1] for shifted in earlier], axis=0)
    value_tiles = value_tiles.reshape(tile_count, BLOCK_TOKENS, kv_heads, HEAD_SIZE)
    group_size = math.gcd(per_window, 4)
    rounds = per_window // group_size
    query_groups = query_heads.reshape(
        rounds, group_size, BLOCK_TOKENS, kv_heads, head_groups, HEAD_SIZE
    )
    grad_groups = grad_heads.reshape(
        rounds, group_size, BLOCK_TOKENS, kv_heads, head_groups, HEAD_SIZE
    )
    tile_groups = tiles.reshape(rounds, group_size, MAXT)
    kind_groups = kinds.reshape(rounds, group_size, MAXT)

    def one_round(totals, inputs):
        summed_key_grad, summed_value_grad = totals
        query_part, grad_part, tile_part, kind_part = inputs
        flat_tiles = tile_part.reshape(group_size * MAXT)
        grad_query, grad_key, grad_value = jax.vmap(block_grads)(
            query_part, grad_part, key_tiles[tile_part], value_tiles[tile_part], kind_part
        )
        summed_key_grad = summed_key_grad.at[flat_tiles].add(
            grad_key.reshape(group_size * MAXT, BLOCK_TOKENS, kv_heads, HEAD_SIZE)
        )
        summed_value_grad = summed_value_grad.at[flat_tiles].add(
            grad_value.reshape(group_size * MAXT, BLOCK_TOKENS, kv_heads, HEAD_SIZE)
        )
        return ((summed_key_grad, summed_value_grad), grad_query)

    blank_total_sum = jnp.zeros((tile_count, BLOCK_TOKENS, kv_heads, HEAD_SIZE), jnp.float32)
    (summed_key_grad, summed_value_grad), grad_queries = lax.scan(
        one_round,
        (blank_total_sum, blank_total_sum),
        (query_groups, grad_groups, tile_groups, kind_groups),
    )
    key_parts = summed_key_grad.reshape(REACH + 1, window, kv_heads * HEAD_SIZE)
    value_parts = summed_value_grad.reshape(REACH + 1, window, kv_heads * HEAD_SIZE)
    moving_sum = (key_parts[REACH], value_parts[REACH])
    for offset in range(REACH - 1, -1, -1):
        arrived = shifted_2((moving_sum[0], moving_sum[1]), "tm", -1)
        moving_sum = (arrived[0] + key_parts[offset], arrived[1] + value_parts[offset])
    key_total, value_total = moving_sum
    grad_query_heads = grad_queries.reshape(window, head_groups * kv_heads * HEAD_SIZE)
    return (
        lax.all_to_all(grad_query_heads, "space", split_axis=0, concat_axis=1, tiled=True),
        lax.all_to_all(
            key_total.astype(jnp.bfloat16), "space", split_axis=0, concat_axis=1, tiled=True
        ),
        lax.all_to_all(
            value_total.astype(jnp.bfloat16), "space", split_axis=0, concat_axis=1, tiled=True
        ),
    )


def solution(mesh):
    in_specs = (
        P(("tm", "space"), None),
        P(("tm", "space"), None),
        P(("tm", "space"), None),
        P(("tm", "space"), None),
        P("tm", None),
        P("tm", None),
    )
    out_specs = (P(("tm", "space"), None), P(("tm", "space"), None), P(("tm", "space"), None))
    return jax.shard_map(body, mesh=mesh, in_specs=in_specs, out_specs=out_specs, check_vma=False)
```

profile of v0, /device:TPU:24, one launch (start us, length us, event | category | flops | bytes accessed | tf_op | source)
XLA Modules:
  0.0 209.1 jit_solution(6476635479993479575)
XLA Ops:
  0.7 2.1 %copy.25 = bf16[128,2048]{0,1:T(8,128)(2,1)} copy(bf16[128,2048]{1,0:T(8,128)(2,1)} %param.7) | data formatting | bytes 1048576 | tf_op args[1]
  2.8 3.5 %all-to-all-start = ((bf16[128,2,1024]{0,2,1:T(8,128)(2,1)}), bf16[128,2,1024]{0,2,1:T(8,128)(2,1)S(1)}, u32[]{:S(2)}, u32[]{:S(2)}) async-start(bf16[128,2,1024]{0,2,1:T(8,128)(2,1)} %bitcast.2), calls=%async_computation | async-start | bytes 1048576 | tf_op jit(solution)/shard_map/all_to_all | solution.py:70
  7.6 2.0 copy.30
  9.8 4.8 %all-to-all-done = bf16[128,2,1024]{0,2,1:T(8,128)(2,1)S(1)} async-done(((bf16[128,2,1024]{0,2,1:T(8,128)(2,1)}), bf16[128,2,1024]{0,2,1:T(8,128)(2,1)S(1)}, u32[]{:S(2)}, u32[]{:S(2)}) %all-to-all-start) | async-done | bytes 524320 | tf_op jit(solution)/shard_map/all_to_all | solution.py:70
  14.5 3.6 %all-to-all-start.2 = ((bf16[128,2,1024]{0,2,1:T(8,128)(2,1)}), bf16[128,2,1024]{0,2,1:T(8,128)(2,1)S(1)}, u32[]{:S(2)}, u32[]{:S(2)}) async-start(bf16[128,2,1024]{0,2,1:T(8,128)(2,1)} %bitcast.13), calls=%async_computation.2 | async-start | bytes 1048576 | tf_op jit(solution)/shard_map/all_to_all | solution.py:71
  18.3 1.3 copy.27
  20.0 1.9 collective-permute-start
  21.9 3.4 %collective-permute-start.1 = (bf16[256,1024]{1,0:T(8,128)(2,1)S(1)}, bf16[256,1024]{1,0:T(8,128)(2,1)S(1)}, u32[]{:S(2)}, u32[]{:S(2)}) collective-permute-start(bf16[256,1024]{1,0:T(8,128)(2,1)S(1)} %bitcast.163), channel_id=1, source_target_pairs={{0,4},{2,6},{4,8},{6,10},{8,12},{10,14},{12,16},{14,18},{16,20},{1... | collective-permute-start | bytes 1572872 | tf_op jit(solution)/shard_map/ppermute | solution.py:17
  25.5 4.4 %all-to-all-start.1 = ((bf16[128,2,2048]{0,2,1:T(8,128)(2,1)}), bf16[128,2,2048]{0,2,1:T(8,128)(2,1)}, u32[]{:S(2)}, u32[]{:S(2)}) async-start(bf16[128,2,2048]{0,2,1:T(8,128)(2,1)} %bitcast.9), calls=%async_computation.1 | async-start | bytes 2097152 | tf_op jit(solution)/shard_map/all_to_all | solution.py:68
  30.1 1.3 copy.32
  33.0 1.9 collective-permute-start.2
  34.9 3.4 %collective-permute-start.3 = (bf16[256,1024]{1,0:T(8,128)(2,1)}, bf16[256,1024]{1,0:T(8,128)(2,1)}, u32[]{:S(2)}, u32[]{:S(2)}) collective-permute-start(bf16[256,1024]{1,0:T(8,128)(2,1)} %bitcast.15), channel_id=1, source_target_pairs={{0,4},{2,6},{4,8},{6,10},{8,12},{10,14},{12,16},{14,18},{16,20},{1... | collective-permute-start | bytes 1572872 | tf_op jit(solution)/shard_map/ppermute | solution.py:17
  38.3 1.2 collective-permute-done.1
  40.1 2.7 %gather_fusion = bf16[12,128,8,128]{3,2,1,0:T(8,128)(2,1)} fusion(bf16[6,128,8,128]{3,2,1,0:T(8,128)(2,1)S(1)} %bitcast.144, s32[1024]{0:T(1024)S(1)} %pad_clamp_fusion), kind=kCustom, calls=%fused_computation | custom fusion | bytes 6291504 | tf_op jit(solution)/shard_map/while/body/eval_jaxpr/gather | solution.py:99
  42.8 3.8 %copy.60 = bf16[2,768,8,128,1]{1,3,4,2,0:T(8,128)(2,1)S(1)} copy(bf16[2,768,8,128,1]{3,2,1,0,4:T(8,128)(2,1)} %bitcast.146) | data formatting | bytes 6291456 | tf_op jit(solution)/shard_map/while/body/eval_jaxpr/vmap()/reshape | solution.py:23
  46.6 4.4 %all-to-all-start.3 = ((bf16[128,2,2048]{0,2,1:T(8,128)(2,1)}), bf16[128,2,2048]{0,2,1:T(8,128)(2,1)}, u32[]{:S(2)}, u32[]{:S(2)}) async-start(bf16[128,2,2048]{0,2,1:T(8,128)(2,1)} %bitcast.147), calls=%async_computation.3 | async-start | bytes 2097152 | tf_op jit(solution)/shard_map/all_to_all | solution.py:69
  51.1 10.5 %fusion.18 = (f32[2,8,2,128]{3,2,1,0:T(2,128)S(1)}, f32[2,8,2,128,768]{3,4,2,1,0:T(8,128)}) fusion(pred[2,128,768]{1,2,0:T(8,128)(4,1)S(1)} %and_or_fusion, bf16[2,768,8,128,1]{1,3,4,2,0:T(8,128)(2,1)S(1)} %copy.60, bf16[2,128,8,2,128]{1,4,3,2,0:T(8,128)(2,1)} %bitcast.11), kind=kOutput, calls=%fused_computation.49 | convolution fusion | flops 821035776 | bytes 16990208 | tf_op jit(solution)/shard_map/while/body/eval_jaxpr/vmap()/sub | solution.py:37
  61.6 8.8 %fusion.7 = bf16[2,8,2,128,768]{3,4,2,1,0:T(8,128)(2,1)} fusion(f32[2,8,2,128,768]{3,4,2,1,0:T(8,128)} %get-tuple-element.45, f32[2,8,2,128]{3,2,1,0:T(2,128)S(1)} %get-tuple-element.44), kind=kLoop, calls=%fused_computation.15 | loop fusion | flops 6291456 | bytes 18890752 | tf_op jit(solution)/shard_map/while/body/eval_jaxpr/vmap()/convert_element_type | solution.py:39
  70.4 1.5 maximum_bitcast_fusion.1
  72.3 2.7 %gather_fusion.1 = bf16[12,128,8,128]{3,2,1,0:T(8,128)(2,1)} fusion(bf16[6,128,8,128]{3,2,1,0:T(8,128)(2,1)S(1)} %bitcast.143, s32[1024]{0:T(1024)S(1)} %pad_clamp_fusion), kind=kCustom, calls=%fused_computation.1 | custom fusion | bytes 6291504 | tf_op jit(solution)/shard_map/while/body/eval_jaxpr/gather | solution.py:99
  75.0 5.3 %copy.52 = bf16[2,768,8,128,1]{1,3,4,2,0:T(8,128)(2,1)} copy(bf16[2,768,8,128,1]{3,2,1,0,4:T(8,128)(2,1)} %bitcast.145) | data formatting | bytes 6291456 | tf_op jit(solution)/shard_map/while/body/eval_jaxpr/vmap()/reshape | solution.py:24
  80.3 7.6 %convolution_bitcast_fusion = f32[2,768,8,128]{3,1,2,0:T(8,128)} fusion(bf16[2,8,2,128,768]{3,4,2,1,0:T(8,128)(2,1)} %fusion.7, bf16[2,128,8,2,128]{1,4,3,2,0:T(8,128)(2,1)} %bitcast.20), kind=kOutput, calls=%fused_computation.16 | convolution fusion | flops 805306368 | bytes 13631488 | tf_op jit(solution)/shard_map/while/body/eval_jaxpr/vmap(kgqt,qkgd->tkd)/dot_general | solution.py:56
  87.9 2.7 %fusion.8 = f32[2,8,2,128]{3,2,1,0:T(2,128)S(1)} fusion(bf16[2,8,2,128,128]{3,4,2,1,0:T(8,128)(2,1)} %bitcast.1, bf16[2,768,8,128,1]{1,3,4,2,0:T(8,128)(2,1)S(1)} %copy-done.3, bf16[2,8,2,128,768]{3,4,2,1,0:T(8,128)(2,1)S(1)} %bitcast.138), kind=kOutput, calls=%fused_computation.19 | convolution fusion | flops 806875136 | bytes 10502144 | tf_op jit(solution)/shard_map/while/body/eval_jaxpr/vmap(kgqt,tkd->qkgd)/dot_general | solution.py:40
  90.6 8.6 %fusion.2 = bf16[2,8,2,128,768]{3,4,2,1,0:T(8,128)(2,1)S(1)} fusion(f32[2,8,2,128]{3,2,1,0:T(2,128)S(1)} %fusion.8, f32[2,8,2,128,768]{3,4,2,1,0:T(8,128)} %get-tuple-element.45, f32[2,8,2,128]{3,2,1,0:T(2,128)S(1)} %get-tuple-element.44, bf16[2,768,8,128,1]{1,3,4,2,0:T(8,128)(2,1)} %copy.52, bf16[2,128,8,2,128]{1,4,3,2,0:T(8,128)(2,1)} %bitcast.20), kind=kOutput, calls=%fused_computation.7 | convolution fusion | flops 821035008 | bytes 23101440 | tf_op jit(solution)/shard_map/while/body/eval_jaxpr/vmap(qkgd,tkd->kgqt)/dot_general | solution.py:44
  99.2 3.8 %convolution_bitcast_fusion.1 = f32[2,768,8,128]{3,1,2,0:T(8,128)S(1)} fusion(bf16[2,8,2,128,768]{3,4,2,1,0:T(8,128)(2,1)S(1)} %fusion.2, bf16[2,128,8,2,128]{1,4,3,2,0:T(8,128)(2,1)} %bitcast.11), kind=kOutput, calls=%fused_computation.17 | convolution fusion | flops 805306368 | bytes 13631488 | tf_op jit(solution)/shard_map/while/body/eval_jaxpr/vmap(kgqt,qkgd->tkd)/dot_general | solution.py:53
  103.1 6.3 %copy.41 = f32[2,768,8,128]{3,2,1,0:T(8,128)} copy(f32[2,768,8,128]{3,1,2,0:T(8,128)S(1)} %convolution_bitcast_fusion.1) | data formatting | bytes 12582912 | tf_op jit(solution)/shard_map/while/body/eval_jaxpr/vmap(kgqt,qkgd->tkd)/transpose | solution.py:53
  109.5 8.5 %scatter_fusion = f32[6,128,8,128]{3,2,1,0:T(8,128)S(1)} fusion(f32[6,128,8,128]{3,2,1,0:T(8,128)S(1)} %broadcast_in_dim.56.clone, s32[12]{0:T(128)S(1)} %fusion.13, f32[12,128,8,128]{3,2,1,0:T(8,128)} %bitcast.142), kind=kCustom, calls=%fused_computation.2 | custom fusion | flops 1572864 | bytes 18874416 | tf_op jit(solution)/shard_map/while/body/eval_jaxpr/scatter-add | solution.py:101
  118.1 1.5 fusion.17
  119.6 1.2 copy.94
  120.8 5.4 %collective-permute-start.4 = (f32[256,1024]{1,0:T(8,128)}, f32[256,1024]{1,0:T(8,128)}, u32[]{:S(2)}, u32[]{:S(2)}) collective-permute-start(f32[256,1024]{1,0:T(8,128)} %bitcast.134), channel_id=1, source_target_pairs={{2,0},{4,2},{6,4},{8,6},{10,8},{12,10},{14,12},{16,14},{18,16},{20... | collective-permute-start | bytes 3145736 | tf_op jit(solution)/shard_map/ppermute | solution.py:17
  126.2 9.0 %copy.44 = f32[2,768,8,128]{3,2,1,0:T(8,128)} copy(f32[2,768,8,128]{3,1,2,0:T(8,128)} %convolution_bitcast_fusion) | data formatting | bytes 12582912 | tf_op jit(solution)/shard_map/while/body/eval_jaxpr/vmap(kgqt,qkgd->tkd)/transpose | solution.py:56
  135.4 8.3 %scatter_fusion.1 = f32[6,128,8,128]{3,2,1,0:T(8,128)S(1)} fusion(f32[6,128,8,128]{3,2,1,0:T(8,128)S(1)} %broadcast_in_dim.56.clone.1, s32[12]{0:T(128)S(1)} %fusion.13, f32[12,128,8,128]{3,2,1,0:T(8,128)} %bitcast.141), kind=kCustom, calls=%fused_computation.3 | custom fusion | flops 1572864 | bytes 18874416 | tf_op jit(solution)/shard_map/while/body/eval_jaxpr/scatter-add | solution.py:104
  145.2 2.3 %collective-permute-start.6 = (f32[256,1024]{1,0:T(8,128)S(1)}, f32[256,1024]{1,0:T(8,128)S(1)}, u32[]{:S(2)}, u32[]{:S(2)}) collective-permute-start(f32[256,1024]{1,0:T(8,128)S(1)} %bitcast.165), channel_id=1, source_target_pairs={{2,0},{4,2},{6,4},{8,6},{10,8},{12,10},{14,12},{16,14},{18,16},{20... | collective-permute-start | bytes 3145736 | tf_op jit(solution)/shard_map/ppermute | solution.py:17
  147.5 2.7 %bitcast_add_fusion.3 = f32[256,1024]{1,0:T(8,128)} fusion(f32[256,1024]{1,0:T(8,128)} %collective-permute-done.4, f32[32,8,8,128]{3,2,1,0:T(8,128)S(1)} %bitcast.149), kind=kLoop, calls=%fused_computation.29 | loop fusion | flops 262144 | bytes 3145728 | tf_op jit(solution)/shard_map/add | solution.py:120
  150.2 2.8 %collective-permute-start.5 = (f32[256,1024]{1,0:T(8,128)}, f32[256,1024]{1,0:T(8,128)}, u32[]{:S(2)}, u32[]{:S(2)}) collective-permute-start(f32[256,1024]{1,0:T(8,128)} %bitcast_add_fusion.3), channel_id=1, source_target_pairs={{2,0},{4,2},{6,4},{8,6},{10,8},{12,10},{14,12},{16,14},{18,16},{20... | collective-permute-start | bytes 3145736 | tf_op jit(solution)/shard_map/ppermute | solution.py:17
  153.0 6.8 %collective-permute-done.6 = f32[256,1024]{1,0:T(8,128)S(1)} collective-permute-done((f32[256,1024]{1,0:T(8,128)S(1)}, f32[256,1024]{1,0:T(8,128)S(1)}, u32[]{:S(2)}, u32[]{:S(2)}) %collective-permute-start.6) | collective-permute-done | bytes 1048608 | tf_op jit(solution)/shard_map/ppermute | solution.py:17
  159.8 1.4 bitcast_add_fusion.1
  161.1 4.8 %collective-permute-start.7 = (f32[256,1024]{1,0:T(8,128)}, f32[256,1024]{1,0:T(8,128)}, u32[]{:S(2)}, u32[]{:S(2)}) collective-permute-start(f32[256,1024]{1,0:T(8,128)} %bitcast_add_fusion.1), channel_id=1, source_target_pairs={{2,0},{4,2},{6,4},{8,6},{10,8},{12,10},{14,12},{16,14},{18,16},{20... | collective-permute-start | bytes 3145736 | tf_op jit(solution)/shard_map/ppermute | solution.py:17
  166.0 2.2 %convolution_convert_fusion = bf16[2,8,128,2,128]{4,2,3,1,0:T(8,128)(2,1)} fusion(bf16[2,768,8,128,1]{1,3,4,2,0:T(8,128)(2,1)S(1)} %copy-done.2, bf16[2,8,2,128,768]{3,4,2,1,0:T(8,128)(2,1)S(1)} %bitcast.140), kind=kOutput, calls=%fused_computation.22 | convolution fusion | flops 805830656 | bytes 10485760 | tf_op jit(solution)/shard_map/while/body/eval_jaxpr/vmap(kgqt,tkd->qkgd)/dot_general | solution.py:50
  168.3 3.7 %all-to-all-start.4 = ((bf16[2,128,2048]{1,2,0:T(8,128)(2,1)}), bf16[2,128,2048]{1,2,0:T(8,128)(2,1)S(1)}, u32[]{:S(2)}, u32[]{:S(2)}) async-start(bf16[2,128,2048]{1,2,0:T(8,128)(2,1)} %bitcast.28), calls=%async_computation.4 | async-start | bytes 2097152 | tf_op jit(solution)/shard_map/all_to_all | solution.py:124
  172.0 2.2 %fusion.10 = bf16[256,1024]{1,0:T(8,128)(2,1)} fusion(f32[256,1024]{1,0:T(8,128)} %collective-permute-done.5, f32[32,8,8,128]{3,2,1,0:T(8,128)S(1)} %bitcast.151), kind=kLoop, calls=%fused_computation.28 | loop fusion | flops 524288 | bytes 2621440 | tf_op jit(solution)/shard_map/convert_element_type | solution.py:126
  174.2 12.0 %all-to-all-done.4 = bf16[2,128,2048]{1,2,0:T(8,128)(2,1)S(1)} async-done(((bf16[2,128,2048]{1,2,0:T(8,128)(2,1)}), bf16[2,128,2048]{1,2,0:T(8,128)(2,1)S(1)}, u32[]{:S(2)}, u32[]{:S(2)}) %all-to-all-start.4) | async-done | bytes 1048608 | tf_op jit(solution)/shard_map/all_to_all | solution.py:124
  186.2 3.5 %all-to-all-start.5 = ((bf16[2,128,1024]{2,1,0:T(8,128)(2,1)}), bf16[2,128,1024]{2,1,0:T(8,128)(2,1)S(1)}, u32[]{:S(2)}, u32[]{:S(2)}) async-start(bf16[2,128,1024]{2,1,0:T(8,128)(2,1)} %bitcast.155), calls=%async_computation.5 | async-start | bytes 1048576 | tf_op jit(solution)/shard_map/all_to_all | solution.py:125
  189.7 2.3 %fusion.9 = bf16[256,1024]{1,0:T(8,128)(2,1)} fusion(f32[256,1024]{1,0:T(8,128)} %collective-permute-done.7, f32[32,8,8,128]{3,2,1,0:T(8,128)S(1)} %bitcast.152), kind=kLoop, calls=%fused_computation.24 | loop fusion | flops 524288 | bytes 2621440 | tf_op jit(solution)/shard_map/convert_element_type | solution.py:129
  192.0 5.5 %all-to-all-done.5 = bf16[2,128,1024]{2,1,0:T(8,128)(2,1)S(1)} async-done(((bf16[2,128,1024]{2,1,0:T(8,128)(2,1)}), bf16[2,128,1024]{2,1,0:T(8,128)(2,1)S(1)}, u32[]{:S(2)}, u32[]{:S(2)}) %all-to-all-start.5) | async-done | bytes 524320 | tf_op jit(solution)/shard_map/all_to_all | solution.py:125
  197.5 3.5 %all-to-all-start.6 = ((bf16[2,128,1024]{2,1,0:T(8,128)(2,1)}), bf16[2,128,1024]{2,1,0:T(8,128)(2,1)S(1)}, u32[]{:S(2)}, u32[]{:S(2)}) async-start(bf16[2,128,1024]{2,1,0:T(8,128)(2,1)} %bitcast.44), calls=%async_computation.6 | async-start | bytes 1048576 | tf_op jit(solution)/shard_map/all_to_all | solution.py:128
  201.0 1.3 copy.74
  203.6 4.2 %all-to-all-done.6 = bf16[2,128,1024]{2,1,0:T(8,128)(2,1)S(1)} async-done(((bf16[2,128,1024]{2,1,0:T(8,128)(2,1)}), bf16[2,128,1024]{2,1,0:T(8,128)(2,1)S(1)}, u32[]{:S(2)}, u32[]{:S(2)}) %all-to-all-start.6) | async-done | bytes 524320 | tf_op jit(solution)/shard_map/all_to_all | solution.py:128
  (64 shorter events, 9.2 us)
Async XLA Ops:
  0.6 17.5 %copy-start.9 = (s32[2,6]{1,0:T(2,128)S(1)}, s32[2,6]{1,0:T(2,128)}, u32[]{:S(2)}) copy-start(s32[2,6]{1,0:T(2,128)} %param.10) | copy-start | bytes 148
  0.6 17.6 %copy-start.7 = (bf16[128,4096]{1,0:T(8,128)(2,1)S(1)}, bf16[128,4096]{1,0:T(8,128)(2,1)}, u32[]{:S(2)}) copy-start(bf16[128,4096]{1,0:T(8,128)(2,1)} %param.6) | copy-start | bytes 3145732
  2.8 11.7 %all-to-all-start = ((bf16[128,2,1024]{0,2,1:T(8,128)(2,1)}), bf16[128,2,1024]{0,2,1:T(8,128)(2,1)S(1)}, u32[]{:S(2)}, u32[]{:S(2)}) async-start(bf16[128,2,1024]{0,2,1:T(8,128)(2,1)} %bitcast.2), calls=%async_computation | async-start | bytes 1048576 | tf_op jit(solution)/shard_map/all_to_all | solution.py:70
  14.5 15.6 %copy-start.8 = (bf16[128,4096]{1,0:T(8,128)(2,1)S(1)}, bf16[128,4096]{1,0:T(8,128)(2,1)}, u32[]{:S(2)}) copy-start(bf16[128,4096]{1,0:T(8,128)(2,1)} %param.9) | copy-start | bytes 3145732
  14.5 11.0 %all-to-all-start.2 = ((bf16[128,2,1024]{0,2,1:T(8,128)(2,1)}), bf16[128,2,1024]{0,2,1:T(8,128)(2,1)S(1)}, u32[]{:S(2)}, u32[]{:S(2)}) async-start(bf16[128,2,1024]{0,2,1:T(8,128)(2,1)} %bitcast.13), calls=%async_computation.2 | async-start | bytes 1048576 | tf_op jit(solution)/shard_map/all_to_all | solution.py:71
  20.0 18.3 %collective-permute-start = (bf16[256,1024]{1,0:T(8,128)(2,1)S(1)}, bf16[256,1024]{1,0:T(8,128)(2,1)S(1)}, u32[]{:S(2)}, u32[]{:S(2)}) collective-permute-start(bf16[256,1024]{1,0:T(8,128)(2,1)S(1)} %bitcast.162), channel_id=1, source_target_pairs={{0,2},{2,4},{4,6},{6,8},{8,10},{10,12},{12,14},{14,16},{16,18},{18... | collective-permute-start | bytes 1572872 | tf_op jit(solution)/shard_map/ppermute | solution.py:17
  21.9 17.7 %collective-permute-start.1 = (bf16[256,1024]{1,0:T(8,128)(2,1)S(1)}, bf16[256,1024]{1,0:T(8,128)(2,1)S(1)}, u32[]{:S(2)}, u32[]{:S(2)}) collective-permute-start(bf16[256,1024]{1,0:T(8,128)(2,1)S(1)} %bitcast.163), channel_id=1, source_target_pairs={{0,4},{2,6},{4,8},{6,10},{8,12},{10,14},{12,16},{14,18},{16,20},{1... | collective-permute-start | bytes 1572872 | tf_op jit(solution)/shard_map/ppermute | solution.py:17
  25.5 21.1 %all-to-all-start.1 = ((bf16[128,2,2048]{0,2,1:T(8,128)(2,1)}), bf16[128,2,2048]{0,2,1:T(8,128)(2,1)}, u32[]{:S(2)}, u32[]{:S(2)}) async-start(bf16[128,2,2048]{0,2,1:T(8,128)(2,1)} %bitcast.9), calls=%async_computation.1 | async-start | bytes 2097152 | tf_op jit(solution)/shard_map/all_to_all | solution.py:68
  33.0 37.4 %collective-permute-start.2 = (bf16[256,1024]{1,0:T(8,128)(2,1)}, bf16[256,1024]{1,0:T(8,128)(2,1)}, u32[]{:S(2)}, u32[]{:S(2)}) collective-permute-start(bf16[256,1024]{1,0:T(8,128)(2,1)} %bitcast.15), channel_id=1, source_target_pairs={{0,2},{2,4},{4,6},{6,8},{8,10},{10,12},{12,14},{14,16},{16,18},{18... | collective-permute-start | bytes 1572872 | tf_op jit(solution)/shard_map/ppermute | solution.py:17
  34.9 35.5 %collective-permute-start.3 = (bf16[256,1024]{1,0:T(8,128)(2,1)}, bf16[256,1024]{1,0:T(8,128)(2,1)}, u32[]{:S(2)}, u32[]{:S(2)}) collective-permute-start(bf16[256,1024]{1,0:T(8,128)(2,1)} %bitcast.15), channel_id=1, source_target_pairs={{0,4},{2,6},{4,8},{6,10},{8,12},{10,14},{12,16},{14,18},{16,20},{1... | collective-permute-start | bytes 1572872 | tf_op jit(solution)/shard_map/ppermute | solution.py:17
  46.6 14.9 %copy-start.1 = (bf16[2,768,8,128,1]{1,3,4,2,0:T(8,128)(2,1)}, bf16[2,768,8,128,1]{1,3,4,2,0:T(8,128)(2,1)S(1)}, u32[]{:S(2)}) copy-start(bf16[2,768,8,128,1]{1,3,4,2,0:T(8,128)(2,1)S(1)} %copy.60) | copy-start | bytes 9437188
  46.6 33.7 %all-to-all-start.3 = ((bf16[128,2,2048]{0,2,1:T(8,128)(2,1)}), bf16[128,2,2048]{0,2,1:T(8,128)(2,1)}, u32[]{:S(2)}, u32[]{:S(2)}) async-start(bf16[128,2,2048]{0,2,1:T(8,128)(2,1)} %bitcast.147), calls=%async_computation.3 | async-start | bytes 2097152 | tf_op jit(solution)/shard_map/all_to_all | solution.py:69
  75.0 12.9 %slice-start = ((s8[6291456]{0:T(1024)(128)(4,1)}), s8[2097152]{0:T(1024)(128)(4,1)S(1)}, s32[]{:S(2)}) async-start(s8[6291456]{0:T(1024)(128)(4,1)} %bitcast.137), calls=%async_computation.7 | async-start | bytes 4194304
  80.3 7.6 %slice-start.1 = ((s8[6291456]{0:T(1024)(128)(4,1)}), s8[4194304]{0:T(1024)(128)(4,1)S(1)}, s32[]{:S(2)}) async-start(s8[6291456]{0:T(1024)(128)(4,1)} %bitcast.137), calls=%async_computation.8 | async-start | bytes 8388608
  80.3 7.6 %copy-start.3 = (bf16[2,768,8,128,1]{1,3,4,2,0:T(8,128)(2,1)S(1)}, bf16[2,768,8,128,1]{1,3,4,2,0:T(8,128)(2,1)}, u32[]{:S(2)}) copy-start(bf16[2,768,8,128,1]{1,3,4,2,0:T(8,128)(2,1)} %copy.52) | copy-start | bytes 9437188
  99.2 3.8 %copy-start = (bf16[2,8,2,128,768]{3,4,2,1,0:T(8,128)(2,1)}, bf16[2,8,2,128,768]{3,4,2,1,0:T(8,128)(2,1)S(1)}, u32[]{:S(2)}) copy-start(bf16[2,8,2,128,768]{3,4,2,1,0:T(8,128)(2,1)S(1)} %fusion.2) | copy-start | bytes 18874372
  120.8 26.7 %collective-permute-start.4 = (f32[256,1024]{1,0:T(8,128)}, f32[256,1024]{1,0:T(8,128)}, u32[]{:S(2)}, u32[]{:S(2)}) collective-permute-start(f32[256,1024]{1,0:T(8,128)} %bitcast.134), channel_id=1, source_target_pairs={{2,0},{4,2},{6,4},{8,6},{10,8},{12,10},{14,12},{16,14},{18,16},{20... | collective-permute-start | bytes 3145736 | tf_op jit(solution)/shard_map/ppermute | solution.py:17
  143.8 3.7 %copy-start.4 = (f32[2,128,8,128]{3,2,1,0:T(8,128)S(1)}, f32[2,128,8,128]{3,2,1,0:T(8,128)}, u32[]{:S(2)}) copy-start(f32[2,128,8,128]{3,2,1,0:T(8,128)} %get-tuple-element.40) | copy-start | bytes 3145732
  143.8 22.2 %slice-start.2 = ((s8[6291456]{0:T(1024)(128)(4,1)}), s8[4194304]{0:T(1024)(128)(4,1)S(1)}, s32[]{:S(2)}) async-start(s8[6291456]{0:T(1024)(128)(4,1)} %bitcast.139), calls=%async_computation.9 | async-start | bytes 8388608
  145.0 21.0 %slice-start.3 = ((s8[6291456]{0:T(1024)(128)(4,1)}), s8[2097152]{0:T(1024)(128)(4,1)S(1)}, s32[]{:S(2)}) async-start(s8[6291456]{0:T(1024)(128)(4,1)} %bitcast.139), calls=%async_computation.10 | async-start | bytes 4194304
  145.2 14.6 %collective-permute-start.6 = (f32[256,1024]{1,0:T(8,128)S(1)}, f32[256,1024]{1,0:T(8,128)S(1)}, u32[]{:S(2)}, u32[]{:S(2)}) collective-permute-start(f32[256,1024]{1,0:T(8,128)S(1)} %bitcast.165), channel_id=1, source_target_pairs={{2,0},{4,2},{6,4},{8,6},{10,8},{12,10},{14,12},{16,14},{18,16},{20... | collective-permute-start | bytes 3145736 | tf_op jit(solution)/shard_map/ppermute | solution.py:17
  147.5 18.5 %copy-start.2 = (bf16[2,768,8,128,1]{1,3,4,2,0:T(8,128)(2,1)S(1)}, bf16[2,768,8,128,1]{1,3,4,2,0:T(8,128)(2,1)}, u32[]{:S(2)}) copy-start(bf16[2,768,8,128,1]{1,3,4,2,0:T(8,128)(2,1)} %copy-done.1) | copy-start | bytes 9437188
  150.2 21.8 %collective-permute-start.5 = (f32[256,1024]{1,0:T(8,128)}, f32[256,1024]{1,0:T(8,128)}, u32[]{:S(2)}, u32[]{:S(2)}) collective-permute-start(f32[256,1024]{1,0:T(8,128)} %bitcast_add_fusion.3), channel_id=1, source_target_pairs={{2,0},{4,2},{6,4},{8,6},{10,8},{12,10},{14,12},{16,14},{18,16},{20... | collective-permute-start | bytes 3145736 | tf_op jit(solution)/shard_map/ppermute | solution.py:17
  161.1 10.9 %copy-start.5 = (f32[2,128,8,128]{3,2,1,0:T(8,128)S(1)}, f32[2,128,8,128]{3,2,1,0:T(8,128)}, u32[]{:S(2)}) copy-start(f32[2,128,8,128]{3,2,1,0:T(8,128)} %get-tuple-element.29) | copy-start | bytes 3145732
  161.1 28.6 %collective-permute-start.7 = (f32[256,1024]{1,0:T(8,128)}, f32[256,1024]{1,0:T(8,128)}, u32[]{:S(2)}, u32[]{:S(2)}) collective-permute-start(f32[256,1024]{1,0:T(8,128)} %bitcast_add_fusion.1), channel_id=1, source_target_pairs={{2,0},{4,2},{6,4},{8,6},{10,8},{12,10},{14,12},{16,14},{18,16},{20... | collective-permute-start | bytes 3145736 | tf_op jit(solution)/shard_map/ppermute | solution.py:17
  168.3 21.4 %copy-start.6 = (f32[2,128,8,128]{3,2,1,0:T(8,128)S(1)}, f32[2,128,8,128]{3,2,1,0:T(8,128)}, u32[]{:S(2)}) copy-start(f32[2,128,8,128]{3,2,1,0:T(8,128)} %get-tuple-element.26) | copy-start | bytes 3145732
  168.3 17.9 %all-to-all-start.4 = ((bf16[2,128,2048]{1,2,0:T(8,128)(2,1)}), bf16[2,128,2048]{1,2,0:T(8,128)(2,1)S(1)}, u32[]{:S(2)}, u32[]{:S(2)}) async-start(bf16[2,128,2048]{1,2,0:T(8,128)(2,1)} %bitcast.28), calls=%async_computation.4 | async-start | bytes 2097152 | tf_op jit(solution)/shard_map/all_to_all | solution.py:124
  186.2 11.3 %all-to-all-start.5 = ((bf16[2,128,1024]{2,1,0:T(8,128)(2,1)}), bf16[2,128,1024]{2,1,0:T(8,128)(2,1)S(1)}, u32[]{:S(2)}, u32[]{:S(2)}) async-start(bf16[2,128,1024]{2,1,0:T(8,128)(2,1)} %bitcast.155), calls=%async_computation.5 | async-start | bytes 1048576 | tf_op jit(solution)/shard_map/all_to_all | solution.py:125
  197.5 10.3 %all-to-all-start.6 = ((bf16[2,128,1024]{2,1,0:T(8,128)(2,1)}), bf16[2,128,1024]{2,1,0:T(8,128)(2,1)S(1)}, u32[]{:S(2)}, u32[]{:S(2)}) async-start(bf16[2,128,1024]{2,1,0:T(8,128)(2,1)} %bitcast.44), calls=%async_computation.6 | async-start | bytes 1048576 | tf_op jit(solution)/shard_map/all_to_all | solution.py:128
where the time goes:
time: 211 us; the launch traced here: 209 us
  starting transfers between devices  52.7 us (25%)
  local copies, waits for them, and re-layouts  47.4 us (22%)
  other arithmetic  37.9 us (18%)
  matrix products  35.4 us (17%)
  waiting for transfers between devices  34.6 us (16%)
    ppermute x8, starting transfers between devices, shifted_2(): return lax.ppermute(block, axis, route)  26 us
    all_to_all x1, waiting for transfers between devices, body(): lax.all_to_all(grad_query_heads, 'space', split_axis=0, concat_axis=1, ti...  12 us
    unnamed x41, local copies, waits for them, and re-layouts  11.3 us
    sub x1, matrix products, block_grads(): weights = jnp.where(visible, jnp.exp(masked - row_max), 0.0)  10.5 us
    transpose x1, local copies, waits for them, and re-layouts, block_grads(): jnp.einsum('kgqt,qkgd->tkd', probs_low, grad_rows, preferred_element_type...  9.05 us
    convert_element_type x1, other arithmetic, block_grads(): probs_low = probabilities.astype(jnp.bfloat16)  8.79 us
    dot_general x1, matrix products, block_grads(): jnp.einsum('qkgd,tkd->kgqt', grad_rows, value_flat, preferred_element_typ...  8.64 us
    scatter-add x1, other arithmetic, one_round(): summed_key_grad.at[flat_tiles]  8.55 us
  transfers between devices with their start and end apart: 15, of which 7 were waited for; matrix products, arithmetic and copies ran while one was open for 37% of the time, Pallas kernels for 0%

commit v1 on v0

--- a/solution.py
+++ b/solution.py
@@ -3,12 +3,17 @@
 import jax
 import jax.numpy as jnp
 from jax import lax
+from jax.experimental import pallas as pl
+from jax.experimental.pallas import tpu as pltpu
 from jax.sharding import PartitionSpec as P
 
 HEAD_SIZE = 128
 BLOCK_TOKENS = 128
 MAXT = 6
 REACH = 2
+CHUNKS = 2
+HIDDEN = -1e30
+FAR = 1 << 20
 
 
 def shifted_2(block, axis, distance):
@@ -63,7 +68,7 @@
     )
 
 
-def body(queries, keys, values, output_gradient, tiles, kinds):
+def general_body(queries, keys, values, output_gradient, tiles, kinds):
     query_heads, grad_heads, key_heads, value_heads = (
         lax.all_to_all(queries, "space", split_axis=1, concat_axis=0, tiled=True),
         lax.all_to_all(output_gradient, "space", split_axis=1, concat_axis=0, tiled=True),
@@ -131,6 +136,244 @@
     )
 
 
+def packed(arrays, part, chunk, chunks):
+    half = arrays[0].shape[1] // 2
+    width = half // chunks
+    first = part * half + chunk * width
+    return jnp.concatenate([lax.dynamic_slice_in_dim(a, first, width, 1) for a in arrays], axis=0)
+
+
+def dot(a, b, contract):
+    return lax.dot_general(a, b, ((contract[:1], contract[1:]), ((), ())), preferred_element_type=jnp.float32)
+
+
+def attend_kernel(
+    side_ref, limit_ref,
+    q_own, g_own, qg_other, k_own, v_own, kv_other, kv2_own, kv2_other, kv1,
+    dq_own, dq_other, d0, d1, d2_own, d2_other,
+    q_all, g_all, k_all, v_all, s_ref, dp_ref, p_ref, ds_ref,
+):
+    n, d = BLOCK_TOKENS, HEAD_SIZE
+    for r, (q, g) in enumerate(
+        ((q_own[...], g_own[...]), (qg_other[:n, :], qg_other[n:, :]))
+    ):
+        for j in range(2):
+            rows = pl.ds((2 * r + j) * n, n)
+            q_all[rows, :] = q[:, j * d : (j + 1) * d]
+            g_all[rows, :] = g[:, j * d : (j + 1) * d]
+    tiles = (
+        (k_own[...], v_own[...]),
+        (kv_other[:n, :], kv_other[n:, :]),
+        (kv1[:n, :], kv1[n : 2 * n, :]),
+        (kv1[2 * n : 3 * n, :], kv1[3 * n :, :]),
+        (kv2_own[:n, :], kv2_own[n:, :]),
+        (kv2_other[:n, :], kv2_other[n:, :]),
+    )
+    for p, (k, v) in enumerate(tiles):
+        k_all[p * n : (p + 1) * n, :] = k
+        v_all[p * n : (p + 1) * n, :] = v
+    lanes = 2 * n
+    column = lax.broadcasted_iota(jnp.int32, (n, lanes), 0)
+    row = lax.broadcasted_iota(jnp.int32, (n, lanes), 1)
+    ahead = column - jnp.where(row >= n, row - n, row)
+    scale = 1.0 / math.sqrt(d)
+    for r in range(2):
+        q = q_all[r * lanes : (r + 1) * lanes, :]
+        g = g_all[r * lanes : (r + 1) * lanes, :]
+        top = None
+        for p in range(6):
+            s = dot(k_all[p * n : (p + 1) * n, :], q, (1, 1))
+            s = jnp.where(ahead <= limit_ref[r * 6 + p], s, HIDDEN)
+            s_ref[p * n : (p + 1) * n, :] = s
+            high = jnp.max(s, axis=0, keepdims=True)
+            top = high if top is None else jnp.maximum(top, high)
+        total = jnp.zeros((1, lanes), jnp.float32)
+        for p in range(6):
+            e = jnp.exp((s_ref[p * n : (p + 1) * n, :] - top) * scale)
+            s_ref[p * n : (p + 1) * n, :] = e
+            total = total + jnp.sum(e, axis=0, keepdims=True)
+        share = 1.0 / total
+        delta = jnp.zeros((1, lanes), jnp.float32)
+        for p in range(6):
+            dp = dot(v_all[p * n : (p + 1) * n, :], g, (1, 1))
+            prob = s_ref[p * n : (p + 1) * n, :] * share
+            low = prob.astype(jnp.bfloat16)
+            delta = delta + jnp.sum(low.astype(jnp.float32) * dp, axis=0, keepdims=True)
+            s_ref[p * n : (p + 1) * n, :] = prob * scale
+            dp_ref[p * n : (p + 1) * n, :] = dp
+            p_ref[p * n : (p + 1) * n, r * lanes : (r + 1) * lanes] = low
+        for p in range(6):
+            ds = s_ref[p * n : (p + 1) * n, :] * (dp_ref[p * n : (p + 1) * n, :] - delta)
+            ds_ref[p * n : (p + 1) * n, r * lanes : (r + 1) * lanes] = ds.astype(jnp.bfloat16)
+    homes = ((d0, 0), (d0, 2), (d1, 0), (d1, 2), (d2_own, 0), (d2_other, 0))
+    for p, (out, place) in enumerate(homes):
+        dk = dot(ds_ref[p * n : (p + 1) * n, :], q_all[...], (1, 0))
+        dv = dot(p_ref[p * n : (p + 1) * n, :], g_all[...], (1, 0))
+        out[place * n : (place + 1) * n, :] = dk.astype(out.dtype)
+        out[(place + 1) * n : (place + 2) * n, :] = dv.astype(out.dtype)
+    dq = dot(k_all[...], ds_ref[...], (0, 0)).T.astype(jnp.bfloat16)
+    for j in range(2):
+        dq_own[:, j * d : (j + 1) * d] = dq[j * n : (j + 1) * n, :]
+        dq_other[:, j * d : (j + 1) * d] = dq[(2 + j) * n : (3 + j) * n, :]
+
+
+def attend(side, limits, chunk, heads, queries, grads, keys, values, qg_other, kv_other, kv2_own, kv2_other, kv1):
+    n, d = BLOCK_TOKENS, HEAD_SIZE
+    per_side = keys.shape[1] // (2 * d)
+
+    def mine(h, side_ref, limit_ref):
+        return 0, side_ref[0] * per_side + chunk * heads + h
+
+    def here(h, side_ref, limit_ref):
+        return 0, h
+
+    def out(rows, width, dtype):
+        return (
+            jax.ShapeDtypeStruct((rows, heads * width), dtype),
+            pl.BlockSpec((rows, width), here),
+        )
+
+    outs = [
+        out(n, 2 * d, jnp.bfloat16),
+        out(n, 2 * d, jnp.bfloat16),
+        out(4 * n, d, jnp.float32),
+        out(4 * n, d, jnp.bfloat16),
+        out(2 * n, d, jnp.bfloat16),
+        out(2 * n, d, jnp.bfloat16),
+    ]
+    flops = heads * 5 * 2 * 4 * n * 6 * n * d
+    return pl.pallas_call(
+        attend_kernel,
+        grid_spec=pltpu.PrefetchScalarGridSpec(
+            num_scalar_prefetch=2,
+            grid=(heads,),
+            in_specs=[
+                pl.BlockSpec((n, 2 * d), mine),
+                pl.BlockSpec((n, 2 * d), mine),
+                pl.BlockSpec((2 * n, 2 * d), here),
+                pl.BlockSpec((n, d), mine),
+                pl.BlockSpec((n, d), mine),
+                pl.BlockSpec((2 * n, d), here),
+                pl.BlockSpec((2 * n, d), here),
+                pl.BlockSpec((2 * n, d), here),
+                pl.BlockSpec((4 * n, d), here),
+            ],
+            out_specs=[spec for _, spec in outs],
+            scratch_shapes=[
+                pltpu.VMEM((4 * n, d), jnp.bfloat16),
+                pltpu.VMEM((4 * n, d), jnp.bfloat16),
+                pltpu.VMEM((6 * n, d), jnp.bfloat16),
+                pltpu.VMEM((6 * n, d), jnp.bfloat16),
+                pltpu.VMEM((6 * n, 2 * n), jnp.float32),
+                pltpu.VMEM((6 * n, 2 * n), jnp.float32),
+                pltpu.VMEM((6 * n, 4 * n), jnp.bfloat16),
+                pltpu.VMEM((6 * n, 4 * n), jnp.bfloat16),
+            ],
+        ),
+        out_shape=[shape for shape, _ in outs],
+        compiler_params=pltpu.CompilerParams(vmem_limit_bytes=32 * 1024 * 1024),
+        cost_estimate=pl.CostEstimate(
+            flops=flops, bytes_accessed=heads * 30 * n * d * 2, transcendentals=heads * 24 * n * n
+        ),
+    )(side, limits, queries, grads, qg_other, keys, values, kv_other, kv2_own, kv2_other, kv1)
+
+
+def swap(block):
+    return lax.ppermute(block, "space", [(0, 1), (1, 0)])
+
+
+def mate(block):
+    return lax.ppermute(block, "tm", [(i, i ^ 1) for i in range(lax.axis_size("tm"))])
+
+
+def moved(block, distance):
+    size = lax.axis_size("tm")
+    return lax.ppermute(
+        block, "tm", [(i, i + distance) for i in range(size) if 0 <= i + distance < size]
+    )
+
+
+def column_limits(side, tiles, kinds):
+    block = jnp.stack([side, 1 - side])
+    value = (jnp.arange(REACH + 1)[:, None] * 2 + block[None, :]).reshape(-1)
+    tiles, kinds = tiles[block], kinds[block]
+    limit = jnp.where(kinds == 0, FAR, jnp.where(kinds == 1, 0, -FAR))
+    named = tiles[:, None, :] == value[None, :, None]
+    return jnp.max(jnp.where(named, limit[:, None, :], -FAR), axis=2).reshape(-1).astype(jnp.int32)
+
+
+def pair_body(queries, keys, values, output_gradient, tiles, kinds):
+    n, d = BLOCK_TOKENS, HEAD_SIZE
+    side = lax.axis_index("space")
+    odd = lax.axis_index("tm") % 2 == 1
+    heads = keys.shape[1] // (2 * d) // CHUNKS
+    place = side.reshape(1).astype(jnp.int32)
+    limits = column_limits(side, tiles, kinds)
+
+    kv_away = [packed([keys, values], 1 - side, c, CHUNKS) for c in range(CHUNKS)]
+    kv_own = [packed([keys, values], side, c, CHUNKS) for c in range(CHUNKS)]
+    qg_away = [packed([queries, output_gradient], 1 - side, c, CHUNKS) for c in range(CHUNKS)]
+
+    kv_other = [swap(b) for b in kv_away]
+    qg_other = [swap(b) for b in qg_away]
+    kv2_own = [moved(b, 2) for b in kv_own]
+    kv2_other = [moved(b, 2) for b in kv_other]
+
+    dq, dkv = [], []
+    for c in range(CHUNKS):
+        kv1 = mate(
+            jnp.concatenate(
+                [
+                    jnp.where(odd, kv2_own[c], kv_own[c]),
+                    jnp.where(odd, kv2_other[c], kv_other[c]),
+                ],
+                axis=0,
+            )
+        )
+        dq_own, dq_away, d0, d1, d2_own, d2_other = attend(
+            place, limits, c, heads, queries, output_gradient, keys, values,
+            qg_other[c], kv_other[c], kv2_own[c], kv2_other[c], kv1,
+        )
+        dq_other = swap(dq_away)
+        met = mate(d1).astype(jnp.float32)
+        met_back = jnp.where(odd, met, 0.0)
+        met_here = jnp.where(odd, 0.0, met)
+        back_other = moved((d2_other + met_back[2 * n :]).astype(jnp.bfloat16), -2)
+        back_own = moved((d2_own + met_back[: 2 * n]).astype(jnp.bfloat16), -2)
+        sum_other = (d0[2 * n :] + met_here[2 * n :] + back_other).astype(jnp.bfloat16)
+        sum_own = (d0[: 2 * n] + met_here[: 2 * n] + back_own).astype(jnp.bfloat16)
+        dkv_other = swap(sum_other)
+        dq.append((dq_own, dq_other))
+        dkv.append((sum_own, dkv_other))
+
+    def placed(own, other):
+        own, other = jnp.concatenate(own, axis=1), jnp.concatenate(other, axis=1)
+        return jnp.where(
+            side == 0,
+            jnp.concatenate([own, other], axis=1),
+            jnp.concatenate([other, own], axis=1),
+        )
+
+    return (
+        placed([a for a, _ in dq], [b for _, b in dq]),
+        placed([a[:n] for a, _ in dkv], [b[:n] for _, b in dkv]),
+        placed([a[n:] for a, _ in dkv], [b[n:] for _, b in dkv]),
+    )
+
+
+def body(queries, keys, values, output_gradient, tiles, kinds):
+    pair = (
+        lax.axis_size("space") == 2
+        and lax.axis_size("tm") % 2 == 0
+        and tiles.shape[0] == 2
+        and queries.shape[0] == BLOCK_TOKENS
+        and queries.shape[1] == 2 * keys.shape[1]
+        and keys.shape[1] % (2 * HEAD_SIZE * CHUNKS) == 0
+    )
+    run = pair_body if pair else general_body
+    return run(queries, keys, values, output_gradient, tiles, kinds)
+
+
 def solution(mesh):
     in_specs = (
         P(("tm", "space"), None),

time: 211 us -> 119 us (0.56)
  the two profiles are of different devices: /device:TPU:24 before, /device:TPU:0 now
where the time goes in v1:
time: 119 us
  waiting for transfers between devices  42.5 us (36%)
  starting transfers between devices  30.4 us (26%)
  Pallas kernels  21.4 us (18%)
  other arithmetic  11.8 us (10%)
  local copies, waits for them, and re-layouts  11.7 us (10%)
    ppermute x8, waiting for transfers between devices, moved(): lax.ppermute(block, 'tm', [(i, i + distance) for i in range(size) if 0 <=...  22.3 us
    pallas_call x2, Pallas kernels, attend(): pl.pallas_call(attend_kernel, grid_spec=pltpu.PrefetchScalarGridSpec(num_...  21.4 us
    ppermute x8, waiting for transfers between devices, swap(): return lax.ppermute(block, 'space', [(0, 1), (1, 0)])  20.3 us
    ppermute x8, starting transfers between devices, moved(): lax.ppermute(block, 'tm', [(i, i + distance) for i in range(size) if 0 <=...  19 us
    ppermute x8, starting transfers between devices, swap(): return lax.ppermute(block, 'space', [(0, 1), (1, 0)])  10.9 us
    unnamed x60, local copies, waits for them, and re-layouts  8.74 us
    select_n x3, other arithmetic, placed(): jnp.where(side == 0, jnp.concatenate([own, other], axis=1), jnp.concatena...  4.4 us
    concatenate x6, other arithmetic, packed(): jnp.concatenate([lax.dynamic_slice_in_dim(a, first, width, 1) for a in ar...  3.83 us
  transfers between devices with their start and end apart: 20, of which 8 were waited for; matrix products, arithmetic and copies ran while one was open for 9% of the time, Pallas kernels for 18%

profile of v1, /device:TPU:0, one launch (start us, length us, event | category | flops | bytes accessed | tf_op | source)
XLA Modules:
  0.0 118.9 jit_solution(2994059136915368768)
XLA Ops:
  0.7 1.4 %constant_dynamic-slice_fusion.6 = (bf16[128,512]{1,0:T(8,128)(2,1)S(1)}, bf16[128,512]{1,0:T(8,128)(2,1)S(1)}, bf16[128,512]{1,0:T(8,128)(2,1)S(1)}, bf16[128,5...) fusion(bf16[128,2048]{1,0:T(8,128)(2,1)} %v_own.3, ...), kind=kLoop, calls=%fused_computation.50 | loop fusion | bytes 2097168 | tf_op jit(solution)/shard_map/dynamic_slice | solution.py:143
  2.1 0.7 pad_maximum_fusion.4
  2.9 2.9 %collective-permute-start.1 = (bf16[256,512]{1,0:T(8,128)(2,1)}, bf16[256,512]{1,0:T(8,128)(2,1)S(1)}, u32[]{:S(2)}, u32[]{:S(2)}) collective-permute-start(bf16[256,512]{1,0:T(8,128)(2,1)} %pad_maximum_fusion.4), channel_id=1, source_target_pairs={{0,1},{1,0},{2,3},{3,2},{4,5},{5,4},{6,7},{7,6},{8,9},{9,8},{10,11... | collective-permute-start | bytes 786440 | tf_op jit(solution)/shard_map/ppermute | solution.py:282
  5.8 0.7 pad_maximum_fusion.5
  6.5 3.4 %collective-permute-start.2 = (bf16[256,512]{1,0:T(8,128)(2,1)}, bf16[256,512]{1,0:T(8,128)(2,1)S(1)}, u32[]{:S(2)}, u32[]{:S(2)}) collective-permute-start(bf16[256,512]{1,0:T(8,128)(2,1)} %pad_maximum_fusion.5), channel_id=1, source_target_pairs={{0,4},{2,6},{4,8},{6,10},{8,12},{10,14},{12,16},{14,18},{16,20},{1... | collective-permute-start | bytes 786440 | tf_op jit(solution)/shard_map/ppermute | solution.py:291
  10.1 0.8 pad_maximum_fusion
  10.9 0.5 collective-permute-start
  11.4 0.7 pad_maximum_fusion.7
  12.1 3.4 %collective-permute-start.7 = (bf16[256,512]{1,0:T(8,128)(2,1)}, bf16[256,512]{1,0:T(8,128)(2,1)S(1)}, u32[]{:S(2)}, u32[]{:S(2)}) collective-permute-start(bf16[256,512]{1,0:T(8,128)(2,1)} %pad_maximum_fusion.7), channel_id=1, source_target_pairs={{0,4},{2,6},{4,8},{6,10},{8,12},{10,14},{12,16},{14,18},{16,20},{1... | collective-permute-start | bytes 786440 | tf_op jit(solution)/shard_map/ppermute | solution.py:291
  15.6 1.6 %collective-permute-start.6 = (bf16[256,512]{1,0:T(8,128)(2,1)S(1)}, bf16[256,512]{1,0:T(8,128)(2,1)S(1)}, u32[]{:S(2)}, u32[]{:S(2)}) collective-permute-start(bf16[256,512]{1,0:T(8,128)(2,1)S(1)} %pad_maximum_fusion.6), channel_id=1, source_target_pairs={{0,1},{1,0},{2,3},{3,2},{4,5},{5,4},{6,7},{7,6},{8,9},{9,8},{10,11... | collective-permute-start | bytes 786440 | tf_op jit(solution)/shard_map/ppermute | solution.py:282
  17.4 0.8 pad_maximum_fusion.2
  18.3 0.6 gather_fusion.1
  18.9 0.6 gather_fusion
  19.4 0.6 collective-permute-start.5
  20.1 3.4 %collective-permute-start.3 = (bf16[256,512]{1,0:T(8,128)(2,1)S(1)}, bf16[256,512]{1,0:T(8,128)(2,1)S(1)}, u32[]{:S(2)}, u32[]{:S(2)}) collective-permute-start(bf16[256,512]{1,0:T(8,128)(2,1)S(1)} %collective-permute-done.1.kv_other), channel_id=1, source_target_pairs={{0,4},{2,6},{4,8},{6,10},{8,12},{10,14},{12,16},{14,18},{16,20},{1... | collective-permute-start | bytes 786440 | tf_op jit(solution)/shard_map/ppermute | solution.py:291
  23.5 8.1 %collective-permute-done.6.kv_other = bf16[256,512]{1,0:T(8,128)(2,1)S(1)} collective-permute-done((bf16[256,512]{1,0:T(8,128)(2,1)S(1)}, bf16[256,512]{1,0:T(8,128)(2,1)S(1)}, u32[]{:S(2)}, u32[]{:S(2)}) %collective-permute-start.6) | collective-permute-done | bytes 262176 | tf_op jit(solution)/shard_map/ppermute | solution.py:282
  31.6 3.4 %collective-permute-start.8 = (bf16[256,512]{1,0:T(8,128)(2,1)S(1)}, bf16[256,512]{1,0:T(8,128)(2,1)S(1)}, u32[]{:S(2)}, u32[]{:S(2)}) collective-permute-start(bf16[256,512]{1,0:T(8,128)(2,1)S(1)} %collective-permute-done.6.kv_other), channel_id=1, source_target_pairs={{0,4},{2,6},{4,8},{6,10},{8,12},{10,14},{12,16},{14,18},{16,20},{1... | collective-permute-start | bytes 786440 | tf_op jit(solution)/shard_map/ppermute | solution.py:291
  35.3 0.8 pad_maximum_fusion.1
  36.1 2.8 %collective-permute-done.8.kv2_other = bf16[256,512]{1,0:T(8,128)(2,1)S(1)} collective-permute-done((bf16[256,512]{1,0:T(8,128)(2,1)S(1)}, bf16[256,512]{1,0:T(8,128)(2,1)S(1)}, u32[]{:S(2)}, u32[]{:S(2)}) %collective-permute-start.8) | collective-permute-done | bytes 262176 | tf_op jit(solution)/shard_map/ppermute | solution.py:291
  38.9 0.8 pad_maximum_fusion.3
  40.2 1.3 %copy-done.7 = bf16[128,4096]{1,0:T(8,128)(2,1)S(1)} copy-done((bf16[128,4096]{1,0:T(8,128)(2,1)S(1)}, bf16[128,4096]{1,0:T(8,128)(2,1)}, u32[]{:S(2)}) %copy-start.7) | copy-done | bytes 1048600
  41.5 0.9 copy-done.9
  42.5 0.9 copy-done.11
  43.4 0.9 copy-done.19
  44.4 10.7 %shard_map.85 = (bf16[128,1024]{1,0:T(8,128)(2,1)S(1)}, bf16[128,1024]{1,0:T(8,128)(2,1)}, f32[512,512]{1,0:T(8,128)S(1)}, bf16[512,512]{1,0:T(8,128)(2,1)}, bf1...) custom-call(s32[1]{0:T(128)} %bitcast.side_ref, s32[12]{0:T(128)S(1)} %reshape.125.limit_ref, ...), custom_call_target="tpu_custom_call" | custom-call | flops 2013265920 | bytes 3932160 | tf_op jit(solution)/shard_map/pallas_call | solution.py:245
  55.1 0.7 copy-done.20
  56.4 10.7 %shard_map.86 = (bf16[128,1024]{1,0:T(8,128)(2,1)S(1)}, bf16[128,1024]{1,0:T(8,128)(2,1)}, f32[512,512]{1,0:T(8,128)S(1)}, bf16[512,512]{1,0:T(8,128)(2,1)S(1)},...) custom-call(s32[1]{0:T(128)} %bitcast.side_ref, s32[12]{0:T(128)S(1)} %reshape.125.limit_ref, ...), custom_call_target="tpu_custom_call" | custom-call | flops 2013265920 | bytes 3932160 | tf_op jit(solution)/shard_map/pallas_call | solution.py:245
  67.1 0.7 copy-done.3
  67.8 0.7 copy-done.24
  68.5 0.7 copy-done.26
  69.2 0.8 copy-done.28
  70.0 1.5 %collective-permute-start.11 = (bf16[128,1024]{1,0:T(8,128)(2,1)}, bf16[128,1024]{1,0:T(8,128)(2,1)}, u32[]{:S(2)}, u32[]{:S(2)}) collective-permute-start(bf16[128,1024]{1,0:T(8,128)(2,1)} %get-tuple-element.18), channel_id=1, source_target_pairs={{0,1},{1,0},{2,3},{3,2},{4,5},{5,4},{6,7},{7,6},{8,9},{9,8},{10,11... | collective-permute-start | bytes 786440 | tf_op jit(solution)/shard_map/ppermute | solution.py:282
  72.1 6.8 %collective-permute-done.11 = bf16[128,1024]{1,0:T(8,128)(2,1)} collective-permute-done((bf16[128,1024]{1,0:T(8,128)(2,1)}, bf16[128,1024]{1,0:T(8,128)(2,1)}, u32[]{:S(2)}, u32[]{:S(2)}) %collective-permute-start.11) | collective-permute-done | bytes 262176 | tf_op jit(solution)/shard_map/ppermute | solution.py:282
  78.8 2.6 %maximum_select_fusion = bf16[128,4096]{1,0:T(8,128)(2,1)} fusion(bf16[128,1024]{1,0:T(8,128)(2,1)} %collective-permute-done.11, bf16[128,1024]{1,0:T(8,128)(2,1)} %collective-permute-done.10, bf16[128,1024]{1,0:T(8,128)(2,1)} %copy-done.3, bf16[128,1024]{1,0:T(8,128)(2,1)S(1)} %get-tuple-element.15, pred[]{:T(512)S(6)} %eq.37), kind=kLoop, calls=%fused_computation.6 | loop fusion | flops 8912896 | bytes 2097153 | tf_op jit(solution)/shard_map/jit(_where)/select_n | solution.py:351
  81.6 0.8 copy-done.21
  82.6 1.3 %collective-permute-start.13 = (bf16[256,512]{1,0:T(8,128)(2,1)S(1)}, bf16[256,512]{1,0:T(8,128)(2,1)S(1)}, u32[]{:S(2)}, u32[]{:S(2)}) collective-permute-start(bf16[256,512]{1,0:T(8,128)(2,1)S(1)} %get-tuple-element.31), channel_id=1, source_target_pairs={{4,0},{6,2},{8,4},{10,6},{12,8},{14,10},{16,12},{18,14},{20,16},{2... | collective-permute-start | bytes 786440 | tf_op jit(solution)/shard_map/ppermute | solution.py:291
  83.9 1.4 %collective-permute-start.16 = (bf16[256,512]{1,0:T(8,128)(2,1)S(1)}, bf16[256,512]{1,0:T(8,128)(2,1)S(1)}, u32[]{:S(2)}, u32[]{:S(2)}) collective-permute-start(bf16[256,512]{1,0:T(8,128)(2,1)S(1)} %get-tuple-element.32), channel_id=1, source_target_pairs={{4,0},{6,2},{8,4},{10,6},{12,8},{14,10},{16,12},{18,14},{20,16},{2... | collective-permute-start | bytes 786440 | tf_op jit(solution)/shard_map/ppermute | solution.py:291
  85.7 1.3 %collective-permute-start.15 = (bf16[256,512]{1,0:T(8,128)(2,1)S(1)}, bf16[256,512]{1,0:T(8,128)(2,1)S(1)}, u32[]{:S(2)}, u32[]{:S(2)}) collective-permute-start(bf16[256,512]{1,0:T(8,128)(2,1)S(1)} %get-tuple-element.33), channel_id=1, source_target_pairs={{4,0},{6,2},{8,4},{10,6},{12,8},{14,10},{16,12},{18,14},{20,16},{2... | collective-permute-start | bytes 786440 | tf_op jit(solution)/shard_map/ppermute | solution.py:291
  87.0 1.3 %collective-permute-start.18 = (bf16[256,512]{1,0:T(8,128)(2,1)S(1)}, bf16[256,512]{1,0:T(8,128)(2,1)S(1)}, u32[]{:S(2)}, u32[]{:S(2)}) collective-permute-start(bf16[256,512]{1,0:T(8,128)(2,1)S(1)} %get-tuple-element.34), channel_id=1, source_target_pairs={{4,0},{6,2},{8,4},{10,6},{12,8},{14,10},{16,12},{18,14},{20,16},{2... | collective-permute-start | bytes 786440 | tf_op jit(solution)/shard_map/ppermute | solution.py:291
  88.3 5.9 %collective-permute-done.13 = bf16[256,512]{1,0:T(8,128)(2,1)S(1)} collective-permute-done((bf16[256,512]{1,0:T(8,128)(2,1)S(1)}, bf16[256,512]{1,0:T(8,128)(2,1)S(1)}, u32[]{:S(2)}, u32[]{:S(2)}) %collective-permute-start.13) | collective-permute-done | bytes 262176 | tf_op jit(solution)/shard_map/ppermute | solution.py:291
  94.1 5.6 %collective-permute-done.16 = bf16[256,512]{1,0:T(8,128)(2,1)S(1)} collective-permute-done((bf16[256,512]{1,0:T(8,128)(2,1)S(1)}, bf16[256,512]{1,0:T(8,128)(2,1)S(1)}, u32[]{:S(2)}, u32[]{:S(2)}) %collective-permute-start.16) | collective-permute-done | bytes 262176 | tf_op jit(solution)/shard_map/ppermute | solution.py:291
  100.1 1.6 %collective-permute-start.17 = (bf16[256,512]{1,0:T(8,128)(2,1)S(1)}, bf16[256,512]{1,0:T(8,128)(2,1)S(1)}, u32[]{:S(2)}, u32[]{:S(2)}) collective-permute-start(bf16[256,512]{1,0:T(8,128)(2,1)S(1)} %get-tuple-element.28), channel_id=1, source_target_pairs={{0,1},{1,0},{2,3},{3,2},{4,5},{5,4},{6,7},{7,6},{8,9},{9,8},{10,11... | collective-permute-start | bytes 786440 | tf_op jit(solution)/shard_map/ppermute | solution.py:282
  101.7 3.7 %collective-permute-done.15 = bf16[256,512]{1,0:T(8,128)(2,1)S(1)} collective-permute-done((bf16[256,512]{1,0:T(8,128)(2,1)S(1)}, bf16[256,512]{1,0:T(8,128)(2,1)S(1)}, u32[]{:S(2)}, u32[]{:S(2)}) %collective-permute-start.15) | collective-permute-done | bytes 262176 | tf_op jit(solution)/shard_map/ppermute | solution.py:291
  105.4 4.3 %collective-permute-done.18 = bf16[256,512]{1,0:T(8,128)(2,1)S(1)} collective-permute-done((bf16[256,512]{1,0:T(8,128)(2,1)S(1)}, bf16[256,512]{1,0:T(8,128)(2,1)S(1)}, u32[]{:S(2)}, u32[]{:S(2)}) %collective-permute-start.18) | collective-permute-done | bytes 262176 | tf_op jit(solution)/shard_map/ppermute | solution.py:291
  110.0 1.6 %collective-permute-start.19 = (bf16[256,512]{1,0:T(8,128)(2,1)S(1)}, bf16[256,512]{1,0:T(8,128)(2,1)S(1)}, u32[]{:S(2)}, u32[]{:S(2)}) collective-permute-start(bf16[256,512]{1,0:T(8,128)(2,1)S(1)} %get-tuple-element.30), channel_id=1, source_target_pairs={{0,1},{1,0},{2,3},{3,2},{4,5},{5,4},{6,7},{7,6},{8,9},{9,8},{10,11... | collective-permute-start | bytes 786440 | tf_op jit(solution)/shard_map/ppermute | solution.py:282
  111.7 5.4 %collective-permute-done.19 = bf16[256,512]{1,0:T(8,128)(2,1)S(1)} collective-permute-done((bf16[256,512]{1,0:T(8,128)(2,1)S(1)}, bf16[256,512]{1,0:T(8,128)(2,1)S(1)}, u32[]{:S(2)}, u32[]{:S(2)}) %collective-permute-start.19) | collective-permute-done | bytes 262176 | tf_op jit(solution)/shard_map/ppermute | solution.py:282
  117.1 0.9 maximum_select_fusion.2
  118.0 0.9 maximum_select_fusion.1
  (93 shorter events, 3.6 us)
Async XLA Ops:
  0.6 17.7 %copy-start = (s32[2,6]{1,0:T(2,128)S(1)}, s32[2,6]{1,0:T(2,128)}, u32[]{:S(2)}) copy-start(s32[2,6]{1,0:T(2,128)} %param.11) | copy-start | bytes 148
  0.7 9.3 %copy-start.6 = (bf16[128,4096]{1,0:T(8,128)(2,1)S(1)}, bf16[128,4096]{1,0:T(8,128)(2,1)}, u32[]{:S(2)}) copy-start(bf16[128,4096]{1,0:T(8,128)(2,1)} %g_own.3) | copy-start | bytes 3145732
  2.1 7.8 %copy-start.4 = (bf16[128,4096]{1,0:T(8,128)(2,1)S(1)}, bf16[128,4096]{1,0:T(8,128)(2,1)}, u32[]{:S(2)}) copy-start(bf16[128,4096]{1,0:T(8,128)(2,1)} %q_own.3) | copy-start | bytes 3145732
  2.9 16.6 %collective-permute-start.1 = (bf16[256,512]{1,0:T(8,128)(2,1)}, bf16[256,512]{1,0:T(8,128)(2,1)S(1)}, u32[]{:S(2)}, u32[]{:S(2)}) collective-permute-start(bf16[256,512]{1,0:T(8,128)(2,1)} %pad_maximum_fusion.4), channel_id=1, source_target_pairs={{0,1},{1,0},{2,3},{3,2},{4,5},{5,4},{6,7},{7,6},{8,9},{9,8},{10,11... | collective-permute-start | bytes 786440 | tf_op jit(solution)/shard_map/ppermute | solution.py:282
  6.5 13.5 %collective-permute-start.2 = (bf16[256,512]{1,0:T(8,128)(2,1)}, bf16[256,512]{1,0:T(8,128)(2,1)S(1)}, u32[]{:S(2)}, u32[]{:S(2)}) collective-permute-start(bf16[256,512]{1,0:T(8,128)(2,1)} %pad_maximum_fusion.5), channel_id=1, source_target_pairs={{0,4},{2,6},{4,8},{6,10},{8,12},{10,14},{12,16},{14,18},{16,20},{1... | collective-permute-start | bytes 786440 | tf_op jit(solution)/shard_map/ppermute | solution.py:291
  10.9 29.3 %collective-permute-start = (bf16[256,1024]{1,0:T(8,128)(2,1)}, bf16[256,1024]{1,0:T(8,128)(2,1)}, u32[]{:S(2)}, u32[]{:S(2)}) collective-permute-start(bf16[256,1024]{1,0:T(8,128)(2,1)} %pad_maximum_fusion), channel_id=1, source_target_pairs={{0,1},{1,0},{2,3},{3,2},{4,5},{5,4},{6,7},{7,6},{8,9},{9,8},{10,11... | collective-permute-start | bytes 1572872 | tf_op jit(solution)/shard_map/ppermute | solution.py:282
  11.4 7.4 %copy-start.29 = (s32[2,6]{1,0:T(2,128)S(1)}, s32[2,6]{1,0:T(2,128)}, u32[]{:S(2)}) copy-start(s32[2,6]{1,0:T(2,128)} %param.10) | copy-start | bytes 148
  12.1 22.9 %collective-permute-start.7 = (bf16[256,512]{1,0:T(8,128)(2,1)}, bf16[256,512]{1,0:T(8,128)(2,1)S(1)}, u32[]{:S(2)}, u32[]{:S(2)}) collective-permute-start(bf16[256,512]{1,0:T(8,128)(2,1)} %pad_maximum_fusion.7), channel_id=1, source_target_pairs={{0,4},{2,6},{4,8},{6,10},{8,12},{10,14},{12,16},{14,18},{16,20},{1... | collective-permute-start | bytes 786440 | tf_op jit(solution)/shard_map/ppermute | solution.py:291
  15.6 16.0 %collective-permute-start.6 = (bf16[256,512]{1,0:T(8,128)(2,1)S(1)}, bf16[256,512]{1,0:T(8,128)(2,1)S(1)}, u32[]{:S(2)}, u32[]{:S(2)}) collective-permute-start(bf16[256,512]{1,0:T(8,128)(2,1)S(1)} %pad_maximum_fusion.6), channel_id=1, source_target_pairs={{0,1},{1,0},{2,3},{3,2},{4,5},{5,4},{6,7},{7,6},{8,9},{9,8},{10,11... | collective-permute-start | bytes 786440 | tf_op jit(solution)/shard_map/ppermute | solution.py:282
  19.4 15.8 %copy-start.8 = (bf16[256,512]{1,0:T(8,128)(2,1)}, bf16[256,512]{1,0:T(8,128)(2,1)S(1)}, u32[]{:S(2)}) copy-start(bf16[256,512]{1,0:T(8,128)(2,1)S(1)} %collective-permute-done.1.kv_other) | copy-start | bytes 786436
  19.4 36.9 %collective-permute-start.5 = (bf16[256,1024]{1,0:T(8,128)(2,1)}, bf16[256,1024]{1,0:T(8,128)(2,1)}, u32[]{:S(2)}, u32[]{:S(2)}) collective-permute-start(bf16[256,1024]{1,0:T(8,128)(2,1)} %pad_maximum_fusion.2), channel_id=1, source_target_pairs={{0,1},{1,0},{2,3},{3,2},{4,5},{5,4},{6,7},{7,6},{8,9},{9,8},{10,11... | collective-permute-start | bytes 1572872 | tf_op jit(solution)/shard_map/ppermute | solution.py:282
  20.0 15.2 %copy-start.10 = (bf16[256,512]{1,0:T(8,128)(2,1)}, bf16[256,512]{1,0:T(8,128)(2,1)S(1)}, u32[]{:S(2)}) copy-start(bf16[256,512]{1,0:T(8,128)(2,1)S(1)} %collective-permute-done.2.kv2_own) | copy-start | bytes 786436
  20.1 15.1 %collective-permute-start.3 = (bf16[256,512]{1,0:T(8,128)(2,1)S(1)}, bf16[256,512]{1,0:T(8,128)(2,1)S(1)}, u32[]{:S(2)}, u32[]{:S(2)}) collective-permute-start(bf16[256,512]{1,0:T(8,128)(2,1)S(1)} %collective-permute-done.1.kv_other), channel_id=1, source_target_pairs={{0,4},{2,6},{4,8},{6,10},{8,12},{10,14},{12,16},{14,18},{16,20},{1... | collective-permute-start | bytes 786440 | tf_op jit(solution)/shard_map/ppermute | solution.py:291
  31.6 7.3 %copy-start.14 = (bf16[256,512]{1,0:T(8,128)(2,1)}, bf16[256,512]{1,0:T(8,128)(2,1)S(1)}, u32[]{:S(2)}) copy-start(bf16[256,512]{1,0:T(8,128)(2,1)S(1)} %collective-permute-done.6.kv_other) | copy-start | bytes 786436
  31.6 7.3 %collective-permute-start.8 = (bf16[256,512]{1,0:T(8,128)(2,1)S(1)}, bf16[256,512]{1,0:T(8,128)(2,1)S(1)}, u32[]{:S(2)}, u32[]{:S(2)}) collective-permute-start(bf16[256,512]{1,0:T(8,128)(2,1)S(1)} %collective-permute-done.6.kv_other), channel_id=1, source_target_pairs={{0,4},{2,6},{4,8},{6,10},{8,12},{10,14},{12,16},{14,18},{16,20},{1... | collective-permute-start | bytes 786440 | tf_op jit(solution)/shard_map/ppermute | solution.py:291
  35.1 1.0 copy-start.12
  35.2 3.7 %copy-start.18 = (bf16[256,512]{1,0:T(8,128)(2,1)}, bf16[256,512]{1,0:T(8,128)(2,1)S(1)}, u32[]{:S(2)}) copy-start(bf16[256,512]{1,0:T(8,128)(2,1)S(1)} %collective-permute-done.3.kv2_other) | copy-start | bytes 786436
  36.1 4.1 %copy-start.1 = (bf16[128,2048]{1,0:T(8,128)(2,1)S(1)}, bf16[128,2048]{1,0:T(8,128)(2,1)}, u32[]{:S(2)}) copy-start(bf16[128,2048]{1,0:T(8,128)(2,1)} %k_own.3) | copy-start | bytes 1572868
  36.1 4.1 %copy-start.2 = (bf16[128,2048]{1,0:T(8,128)(2,1)S(1)}, bf16[128,2048]{1,0:T(8,128)(2,1)}, u32[]{:S(2)}) copy-start(bf16[128,2048]{1,0:T(8,128)(2,1)} %v_own.3) | copy-start | bytes 1572868
  36.1 4.1 %collective-permute-start.4 = (bf16[512,512]{1,0:T(8,128)(2,1)}, bf16[512,512]{1,0:T(8,128)(2,1)}, u32[]{:S(2)}, u32[]{:S(2)}) collective-permute-start(bf16[512,512]{1,0:T(8,128)(2,1)} %pad_maximum_fusion.1), channel_id=1, source_target_pairs={{0,2},{2,0},{4,6},{6,4},{8,10},{10,8},{12,14},{14,12},{16,18},{18,... | collective-permute-start | bytes 1572872 | tf_op jit(solution)/shard_map/ppermute | solution.py:286
  38.9 1.3 %copy-start.16 = (bf16[256,512]{1,0:T(8,128)(2,1)}, bf16[256,512]{1,0:T(8,128)(2,1)S(1)}, u32[]{:S(2)}) copy-start(bf16[256,512]{1,0:T(8,128)(2,1)S(1)} %collective-permute-done.8.kv2_other) | copy-start | bytes 786436
  39.7 16.6 %collective-permute-start.9 = (bf16[512,512]{1,0:T(8,128)(2,1)}, bf16[512,512]{1,0:T(8,128)(2,1)}, u32[]{:S(2)}, u32[]{:S(2)}) collective-permute-start(bf16[512,512]{1,0:T(8,128)(2,1)} %pad_maximum_fusion.3), channel_id=1, source_target_pairs={{0,2},{2,0},{4,6},{6,4},{8,10},{10,8},{12,14},{14,12},{16,18},{18,... | collective-permute-start | bytes 1572872 | tf_op jit(solution)/shard_map/ppermute | solution.py:286
  40.2 16.2 %copy-start.5 = (bf16[128,4096]{1,0:T(8,128)(2,1)S(1)}, bf16[128,4096]{1,0:T(8,128)(2,1)}, u32[]{:S(2)}) copy-start(bf16[128,4096]{1,0:T(8,128)(2,1)} %q_own.3) | copy-start | bytes 3145732
  40.2 1.3 %copy-start.7 = (bf16[128,4096]{1,0:T(8,128)(2,1)S(1)}, bf16[128,4096]{1,0:T(8,128)(2,1)}, u32[]{:S(2)}) copy-start(bf16[128,4096]{1,0:T(8,128)(2,1)} %g_own.3) | copy-start | bytes 3145732
  41.5 0.9 copy-start.9
  42.5 0.9 copy-start.11
  43.4 0.9 copy-start.19
  44.4 12.0 %copy-start.13 = (bf16[256,512]{1,0:T(8,128)(2,1)S(1)}, bf16[256,512]{1,0:T(8,128)(2,1)}, u32[]{:S(2)}) copy-start(bf16[256,512]{1,0:T(8,128)(2,1)} %copy-done.12) | copy-start | bytes 786436
  44.4 12.0 %copy-start.15 = (bf16[256,512]{1,0:T(8,128)(2,1)S(1)}, bf16[256,512]{1,0:T(8,128)(2,1)}, u32[]{:S(2)}) copy-start(bf16[256,512]{1,0:T(8,128)(2,1)} %copy-done.14) | copy-start | bytes 786436
  44.4 12.0 %copy-start.17 = (bf16[256,512]{1,0:T(8,128)(2,1)S(1)}, bf16[256,512]{1,0:T(8,128)(2,1)}, u32[]{:S(2)}) copy-start(bf16[256,512]{1,0:T(8,128)(2,1)} %copy-done.16) | copy-start | bytes 786436
  55.1 0.7 copy-start.20
  55.8 11.3 %copy-start.22 = (bf16[256,512]{1,0:T(8,128)(2,1)}, bf16[256,512]{1,0:T(8,128)(2,1)S(1)}, u32[]{:S(2)}) copy-start(bf16[256,512]{1,0:T(8,128)(2,1)S(1)} %get-tuple-element.25) | copy-start | bytes 786436
  55.8 16.2 %collective-permute-start.10 = (bf16[128,1024]{1,0:T(8,128)(2,1)}, bf16[128,1024]{1,0:T(8,128)(2,1)}, u32[]{:S(2)}, u32[]{:S(2)}) collective-permute-start(bf16[128,1024]{1,0:T(8,128)(2,1)} %get-tuple-element.17), channel_id=1, source_target_pairs={{0,1},{1,0},{2,3},{3,2},{4,5},{5,4},{6,7},{7,6},{8,9},{9,8},{10,11... | collective-permute-start | bytes 786440 | tf_op jit(solution)/shard_map/ppermute | solution.py:282
  68.5 0.7 copy-start.26
  69.2 0.8 copy-start.28
  70.0 8.8 %collective-permute-start.11 = (bf16[128,1024]{1,0:T(8,128)(2,1)}, bf16[128,1024]{1,0:T(8,128)(2,1)}, u32[]{:S(2)}, u32[]{:S(2)}) collective-permute-start(bf16[128,1024]{1,0:T(8,128)(2,1)} %get-tuple-element.18), channel_id=1, source_target_pairs={{0,1},{1,0},{2,3},{3,2},{4,5},{5,4},{6,7},{7,6},{8,9},{9,8},{10,11... | collective-permute-start | bytes 786440 | tf_op jit(solution)/shard_map/ppermute | solution.py:282
  71.6 9.8 %collective-permute-start.12 = (bf16[512,512]{1,0:T(8,128)(2,1)}, bf16[512,512]{1,0:T(8,128)(2,1)S(1)}, u32[]{:S(2)}, u32[]{:S(2)}) collective-permute-start(bf16[512,512]{1,0:T(8,128)(2,1)} %get-tuple-element.20), channel_id=1, source_target_pairs={{0,2},{2,0},{4,6},{6,4},{8,10},{10,8},{12,14},{14,12},{16,18},{18,... | collective-permute-start | bytes 1572872 | tf_op jit(solution)/shard_map/ppermute | solution.py:286
  71.6 13.8 %collective-permute-start.14 = (bf16[512,512]{1,0:T(8,128)(2,1)}, bf16[512,512]{1,0:T(8,128)(2,1)S(1)}, u32[]{:S(2)}, u32[]{:S(2)}) collective-permute-start(bf16[512,512]{1,0:T(8,128)(2,1)} %copy-done.28), channel_id=1, source_target_pairs={{0,2},{2,0},{4,6},{6,4},{8,10},{10,8},{12,14},{14,12},{16,18},{18,... | collective-permute-start | bytes 1572872 | tf_op jit(solution)/shard_map/ppermute | solution.py:286
  81.4 0.9 copy-start.21
  81.4 1.0 copy-start.23
  82.6 11.6 %collective-permute-start.13 = (bf16[256,512]{1,0:T(8,128)(2,1)S(1)}, bf16[256,512]{1,0:T(8,128)(2,1)S(1)}, u32[]{:S(2)}, u32[]{:S(2)}) collective-permute-start(bf16[256,512]{1,0:T(8,128)(2,1)S(1)} %get-tuple-element.31), channel_id=1, source_target_pairs={{4,0},{6,2},{8,4},{10,6},{12,8},{14,10},{16,12},{18,14},{20,16},{2... | collective-permute-start | bytes 786440 | tf_op jit(solution)/shard_map/ppermute | solution.py:291
  83.9 1.6 %copy-start.25 = (bf16[256,512]{1,0:T(8,128)(2,1)S(1)}, bf16[256,512]{1,0:T(8,128)(2,1)}, u32[]{:S(2)}) copy-start(bf16[256,512]{1,0:T(8,128)(2,1)} %copy-done.24) | copy-start | bytes 786436
  83.9 1.6 %copy-start.27 = (bf16[256,512]{1,0:T(8,128)(2,1)S(1)}, bf16[256,512]{1,0:T(8,128)(2,1)}, u32[]{:S(2)}) copy-start(bf16[256,512]{1,0:T(8,128)(2,1)} %copy-done.26) | copy-start | bytes 786436
  83.9 15.9 %collective-permute-start.16 = (bf16[256,512]{1,0:T(8,128)(2,1)S(1)}, bf16[256,512]{1,0:T(8,128)(2,1)S(1)}, u32[]{:S(2)}, u32[]{:S(2)}) collective-permute-start(bf16[256,512]{1,0:T(8,128)(2,1)S(1)} %get-tuple-element.32), channel_id=1, source_target_pairs={{4,0},{6,2},{8,4},{10,6},{12,8},{14,10},{16,12},{18,14},{20,16},{2... | collective-permute-start | bytes 786440 | tf_op jit(solution)/shard_map/ppermute | solution.py:291
  85.7 19.7 %collective-permute-start.15 = (bf16[256,512]{1,0:T(8,128)(2,1)S(1)}, bf16[256,512]{1,0:T(8,128)(2,1)S(1)}, u32[]{:S(2)}, u32[]{:S(2)}) collective-permute-start(bf16[256,512]{1,0:T(8,128)(2,1)S(1)} %get-tuple-element.33), channel_id=1, source_target_pairs={{4,0},{6,2},{8,4},{10,6},{12,8},{14,10},{16,12},{18,14},{20,16},{2... | collective-permute-start | bytes 786440 | tf_op jit(solution)/shard_map/ppermute | solution.py:291
  87.0 22.7 %collective-permute-start.18 = (bf16[256,512]{1,0:T(8,128)(2,1)S(1)}, bf16[256,512]{1,0:T(8,128)(2,1)S(1)}, u32[]{:S(2)}, u32[]{:S(2)}) collective-permute-start(bf16[256,512]{1,0:T(8,128)(2,1)S(1)} %get-tuple-element.34), channel_id=1, source_target_pairs={{4,0},{6,2},{8,4},{10,6},{12,8},{14,10},{16,12},{18,14},{20,16},{2... | collective-permute-start | bytes 786440 | tf_op jit(solution)/shard_map/ppermute | solution.py:291
  100.1 11.6 %collective-permute-start.17 = (bf16[256,512]{1,0:T(8,128)(2,1)S(1)}, bf16[256,512]{1,0:T(8,128)(2,1)S(1)}, u32[]{:S(2)}, u32[]{:S(2)}) collective-permute-start(bf16[256,512]{1,0:T(8,128)(2,1)S(1)} %get-tuple-element.28), channel_id=1, source_target_pairs={{0,1},{1,0},{2,3},{3,2},{4,5},{5,4},{6,7},{7,6},{8,9},{9,8},{10,11... | collective-permute-start | bytes 786440 | tf_op jit(solution)/shard_map/ppermute | solution.py:282
  110.0 7.1 %collective-permute-start.19 = (bf16[256,512]{1,0:T(8,128)(2,1)S(1)}, bf16[256,512]{1,0:T(8,128)(2,1)S(1)}, u32[]{:S(2)}, u32[]{:S(2)}) collective-permute-start(bf16[256,512]{1,0:T(8,128)(2,1)S(1)} %get-tuple-element.30), channel_id=1, source_target_pairs={{0,1},{1,0},{2,3},{3,2},{4,5},{5,4},{6,7},{7,6},{8,9},{9,8},{10,11... | collective-permute-start | bytes 786440 | tf_op jit(solution)/shard_map/ppermute | solution.py:282
  (2 other events, 1.4 us)

commit v2 on v0

--- a/solution.py
+++ b/solution.py
@@ -3,12 +3,18 @@
 import jax
 import jax.numpy as jnp
 from jax import lax
+from jax.experimental import pallas as pl
+from jax.experimental.pallas import tpu as pltpu
 from jax.sharding import PartitionSpec as P
 
 HEAD_SIZE = 128
 BLOCK_TOKENS = 128
 MAXT = 6
 REACH = 2
+STEP_HEADS = 1
+HIDDEN = -1e30
+FAR = 1 << 20
+VMEM_BYTES = 60 * 1024 * 1024
 
 
 def shifted_2(block, axis, distance):
@@ -63,7 +69,7 @@
     )
 
 
-def body(queries, keys, values, output_gradient, tiles, kinds):
+def general_body(queries, keys, values, output_gradient, tiles, kinds):
     query_heads, grad_heads, key_heads, value_heads = (
         lax.all_to_all(queries, "space", split_axis=1, concat_axis=0, tiled=True),
         lax.all_to_all(output_gradient, "space", split_axis=1, concat_axis=0, tiled=True),
@@ -131,6 +137,294 @@
     )
 
 
+def packed(arrays, half, first, width):
+    start = half * (arrays[0].shape[1] // 2) + first
+    return jnp.concatenate([lax.dynamic_slice_in_dim(a, start, width, 1) for a in arrays], axis=0)
+
+
+def dot(a, b, contract):
+    return lax.dot_general(a, b, ((contract[:1], contract[1:]), ((), ())), preferred_element_type=jnp.float32)
+
+
+def find_limits(side, code_ref, limit_ref):
+    for r in range(2):
+        block = side if r == 0 else 1 - side
+        codes = [code_ref[block * MAXT + m] for m in range(MAXT)]
+        for p in range(2 * (REACH + 1)):
+            value = p // 2 * 2 + (side if p % 2 == 0 else 1 - side)
+            limit = -FAR
+            for code in codes:
+                limit = jnp.where(code == 4 * value, FAR, jnp.where(code == 4 * value + 1, 0, limit))
+            limit_ref[r * 6 + p] = limit
+
+
+def attend_kernel(
+    side_ref, code_ref,
+    q_own, g_own, qg_other, k_own, v_own, kv_other, kv2_own, kv2_other, kv1,
+    dq_own, dq_other, d0, d1, d2_own, d2_other,
+    limit_ref, *scratch,
+):
+    n, d = BLOCK_TOKENS, HEAD_SIZE
+
+    @pl.when(pl.program_id(0) == 0)
+    def _():
+        find_limits(side_ref[0], code_ref, limit_ref)
+
+    lanes = 2 * n
+    column = lax.broadcasted_iota(jnp.int32, (n, lanes), 0)
+    row = lax.broadcasted_iota(jnp.int32, (n, lanes), 1)
+    ahead = column - jnp.where(row >= n, row - n, row)
+    scale = 1.0 / math.sqrt(d)
+    rate = scale * math.log2(math.e)
+    for h in range(STEP_HEADS):
+        q_all, g_all, k_all, v_all, s_ref, dp_ref, p_ref, ds_ref = scratch[8 * h : 8 * h + 8]
+        wide, slim = slice(2 * h * d, 2 * (h + 1) * d), slice(h * d, (h + 1) * d)
+        for r, (q, g) in enumerate(
+            ((q_own[:, wide], g_own[:, wide]), (qg_other[:n, wide], qg_other[n:, wide]))
+        ):
+            for j in range(2):
+                rows = slice((2 * r + j) * n, (2 * r + j + 1) * n)
+                q_all[rows, :] = q[:, j * d : (j + 1) * d]
+                g_all[rows, :] = g[:, j * d : (j + 1) * d]
+        tiles = (
+            (k_own[:, slim], v_own[:, slim]),
+            (kv_other[:n, slim], kv_other[n:, slim]),
+            (kv1[:n, slim], kv1[n : 2 * n, slim]),
+            (kv1[2 * n : 3 * n, slim], kv1[3 * n :, slim]),
+            (kv2_own[:n, slim], kv2_own[n:, slim]),
+            (kv2_other[:n, slim], kv2_other[n:, slim]),
+        )
+        for p, (k, v) in enumerate(tiles):
+            k_all[p * n : (p + 1) * n, :] = k
+            v_all[p * n : (p + 1) * n, :] = v
+        for r in range(2):
+            cols = slice(r * lanes, (r + 1) * lanes)
+            q, g = q_all[cols, :], g_all[cols, :]
+            top = None
+            for p in range(6):
+                rows = slice(p * n, (p + 1) * n)
+                s = dot(k_all[rows, :], q, (1, 1))
+                s = jnp.where(ahead <= limit_ref[r * 6 + p], s, HIDDEN)
+                s_ref[rows, :] = s
+                high = jnp.max(s, axis=0, keepdims=True)
+                top = high if top is None else jnp.maximum(top, high)
+            total = jnp.zeros((1, lanes), jnp.float32)
+            delta = jnp.zeros((1, lanes), jnp.float32)
+            for p in range(6):
+                rows = slice(p * n, (p + 1) * n)
+                e = jnp.exp2((s_ref[rows, :] - top) * rate)
+                dp = dot(v_all[rows, :], g, (1, 1))
+                s_ref[rows, :] = e
+                dp_ref[rows, :] = dp
+                total = total + jnp.sum(e, axis=0, keepdims=True)
+                delta = delta + jnp.sum(e * dp, axis=0, keepdims=True)
+            share = 1.0 / total
+            delta = delta * share
+            for p in range(6):
+                rows = slice(p * n, (p + 1) * n)
+                prob = s_ref[rows, :] * share
+                ds = prob * (dp_ref[rows, :] - delta)
+                p_ref[rows, cols] = prob.astype(jnp.bfloat16)
+                ds_ref[rows, cols] = ds.astype(jnp.bfloat16)
+        dk = dot(ds_ref[...], q_all[...], (1, 0)) * scale
+        dv = dot(p_ref[...], g_all[...], (1, 0))
+        homes = ((d0, 0), (d0, 2), (d1, 0), (d1, 2), (d2_own, 0), (d2_other, 0))
+        for p, (out, place) in enumerate(homes):
+            rows = slice(p * n, (p + 1) * n)
+            out[place * n : (place + 1) * n, slim] = dk[rows].astype(out.dtype)
+            out[(place + 1) * n : (place + 2) * n, slim] = dv[rows].astype(out.dtype)
+        dq = (dot(k_all[...], ds_ref[...], (0, 0)) * scale).T.astype(jnp.bfloat16)
+        for j in range(2):
+            here = slice((2 * h + j) * d, (2 * h + j + 1) * d)
+            dq_own[:, here] = dq[j * n : (j + 1) * n, :]
+            dq_other[:, here] = dq[(2 + j) * n : (3 + j) * n, :]
+
+
+def attend(side, limits, first, heads, queries, grads, keys, values, qg_other, kv_other, kv2_own, kv2_other, kv1):
+    n, d = BLOCK_TOKENS, HEAD_SIZE
+    steps = heads // STEP_HEADS
+    per_side = keys.shape[1] // (2 * d * STEP_HEADS)
+    slim, wide = STEP_HEADS * d, 2 * STEP_HEADS * d
+
+    def mine(h, side_ref, code_ref):
+        return 0, side_ref[0] * per_side + first // STEP_HEADS + h
+
+    def here(h, side_ref, code_ref):
+        return 0, h
+
+    def out(rows, width, dtype):
+        return (
+            jax.ShapeDtypeStruct((rows, steps * width), dtype),
+            pl.BlockSpec((rows, width), here),
+        )
+
+    outs = [
+        out(n, wide, jnp.bfloat16),
+        out(n, wide, jnp.bfloat16),
+        out(4 * n, slim, jnp.float32),
+        out(4 * n, slim, jnp.bfloat16),
+        out(2 * n, slim, jnp.bfloat16),
+        out(2 * n, slim, jnp.bfloat16),
+    ]
+    work = [
+        pltpu.VMEM((4 * n, d), jnp.bfloat16),
+        pltpu.VMEM((4 * n, d), jnp.bfloat16),
+        pltpu.VMEM((6 * n, d), jnp.bfloat16),
+        pltpu.VMEM((6 * n, d), jnp.bfloat16),
+        pltpu.VMEM((6 * n, 2 * n), jnp.float32),
+        pltpu.VMEM((6 * n, 2 * n), jnp.float32),
+        pltpu.VMEM((6 * n, 4 * n), jnp.bfloat16),
+        pltpu.VMEM((6 * n, 4 * n), jnp.bfloat16),
+    ]
+    return pl.pallas_call(
+        attend_kernel,
+        grid_spec=pltpu.PrefetchScalarGridSpec(
+            num_scalar_prefetch=2,
+            grid=(steps,),
+            in_specs=[
+                pl.BlockSpec((n, wide), mine),
+                pl.BlockSpec((n, wide), mine),
+                pl.BlockSpec((2 * n, wide), here),
+                pl.BlockSpec((n, slim), mine),
+                pl.BlockSpec((n, slim), mine),
+                pl.BlockSpec((2 * n, slim), here),
+                pl.BlockSpec((2 * n, slim), here),
+                pl.BlockSpec((2 * n, slim), here),
+                pl.BlockSpec((4 * n, slim), here),
+            ],
+            out_specs=[spec for _, spec in outs],
+            scratch_shapes=[pltpu.SMEM((12,), jnp.int32)] + work * STEP_HEADS,
+        ),
+        out_shape=[shape for shape, _ in outs],
+        compiler_params=pltpu.CompilerParams(vmem_limit_bytes=VMEM_BYTES),
+    )(side, limits, queries, grads, qg_other, keys, values, kv_other, kv2_own, kv2_other, kv1)
+
+
+def swap(block):
+    return lax.ppermute(block, "space", [(0, 1), (1, 0)])
+
+
+def mate(block):
+    return lax.ppermute(block, "tm", [(i, i ^ 1) for i in range(lax.axis_size("tm"))])
+
+
+def moved(block, distance):
+    size = lax.axis_size("tm")
+    return lax.ppermute(
+        block, "tm", [(i, i + distance) for i in range(size) if 0 <= i + distance < size]
+    )
+
+
+def after(arrays, *earlier):
+    arrays = list(arrays)
+    return lax.optimization_barrier((*arrays, *earlier))[: len(arrays)]
+
+
+def pair_body(queries, keys, values, output_gradient, tiles, kinds):
+    n, d = BLOCK_TOKENS, HEAD_SIZE
+    side = lax.axis_index("space")
+    odd = lax.axis_index("tm") % 2 == 1
+    half = keys.shape[1] // (2 * d)
+    sizes = [half // 2, half - half // 2]
+    firsts = [0, half // 2]
+    place = side.reshape(1).astype(jnp.int32)
+    codes = 4 * tiles + kinds
+    limits = jnp.concatenate([codes[0], codes[1]])
+
+    def kv_part(part, c, *earlier):
+        return packed(after([keys, values], *earlier), part, firsts[c] * d, sizes[c] * d)
+
+    def qg_part(part, c, *earlier):
+        arrays = after([queries, output_gradient], *earlier)
+        return packed(arrays, part, 2 * firsts[c] * d, 2 * sizes[c] * d)
+
+    kv_away = [kv_part(1 - side, 0)]
+    kv_away.append(kv_part(1 - side, 1, kv_away[0]))
+    kv_own = [kv_part(side, 0, kv_away[1])]
+    qg_away = [qg_part(1 - side, 0, kv_own[0])]
+    qg_away.append(qg_part(1 - side, 1, qg_away[0]))
+    kv_own.append(kv_part(side, 1, qg_away[1]))
+
+    kv_other = [swap(b) for b in kv_away]
+    qg_other = [swap(b) for b in qg_away]
+    kv2_own = [moved(b, 2) for b in kv_own]
+    kv2_other = [moved(b, 2) for b in kv_other]
+
+    def attended(c, *earlier):
+        kv1 = mate(
+            jnp.concatenate(
+                [
+                    jnp.where(odd, kv2_own[c], kv_own[c]),
+                    jnp.where(odd, kv2_other[c], kv_other[c]),
+                ],
+                axis=0,
+            )
+        )
+        return attend(
+            place, after([limits], *earlier)[0] if earlier else limits, firsts[c], sizes[c],
+            queries, output_gradient, keys, values,
+            qg_other[c], kv_other[c], kv2_own[c], kv2_other[c], kv1,
+        )
+
+    def met(d1):
+        both = mate(d1).astype(jnp.float32)
+        return jnp.where(odd, both, 0.0), jnp.where(odd, 0.0, both)
+
+    def low(total):
+        return total.astype(jnp.bfloat16)
+
+    dq_own0, dq_away0, e0, d1, d2_own, d2_other = attended(0)
+    dq_other0 = swap(dq_away0)
+    met_back, met_here0 = met(d1)
+    ship0 = low(jnp.concatenate([d2_own, d2_other], axis=0) + met_back)
+    back0 = moved(ship0, -2)
+    dq_own1, dq_away1, d0, d1, d2_own, d2_other = attended(1, ship0)
+    d1, dq_other0 = after([d1, dq_other0])
+    dq_other1 = swap(dq_away1)
+    met_back, met_here = met(d1)
+    ship_other = low(d2_other + met_back[2 * n :])
+    ship_own = low(d2_own + met_back[: 2 * n])
+    back_other = moved(ship_other, -2)
+    back_own = moved(ship_own, -2)
+    sum0 = low(e0 + met_here0 + back0)
+    own0 = sum0[: 2 * n]
+    other0 = swap(sum0[2 * n :])
+    sum_other = low(d0[2 * n :] + met_here[2 * n :] + back_other)
+    other1 = swap(sum_other)
+    own1 = low(d0[: 2 * n] + met_here[: 2 * n] + back_own)
+
+    def placed(own, other):
+        own, other = jnp.concatenate(own, axis=1), jnp.concatenate(other, axis=1)
+        return jnp.where(
+            side == 0,
+            jnp.concatenate([own, other], axis=1),
+            jnp.concatenate([other, own], axis=1),
+        )
+
+    dq_own0, dq_own1, dq_other0, dq_other1 = after(
+        [dq_own0, dq_own1, dq_other0, dq_other1], ship_other, ship_own
+    )
+    grad_queries = placed([dq_own0, dq_own1], [dq_other0, dq_other1])
+    return (
+        grad_queries,
+        placed([own0[:n], own1[:n]], [other0[:n], other1[:n]]),
+        placed([own0[n:], own1[n:]], [other0[n:], other1[n:]]),
+    )
+
+
+def body(queries, keys, values, output_gradient, tiles, kinds):
+    pair = (
+        lax.axis_size("space") == 2
+        and lax.axis_size("tm") % 2 == 0
+        and tiles.shape[0] == 2
+        and queries.shape[0] == BLOCK_TOKENS
+        and queries.shape[1] == 2 * keys.shape[1]
+        and keys.shape[1] % (4 * HEAD_SIZE) == 0
+    )
+    run = pair_body if pair else general_body
+    return run(queries, keys, values, output_gradient, tiles, kinds)
+
+
 def solution(mesh):
     in_specs = (
         P(("tm", "space"), None),

time: 211 us -> 86.5 us (0.41)
  the two profiles are of different devices: /device:TPU:24 before, /device:TPU:0 now
where the time goes in v2:
time: 86.5 us; the launch traced here: 86.1 us
  starting transfers between devices  29.3 us (34%)
  waiting for transfers between devices  24.4 us (28%)
  Pallas kernels  18.8 us (22%)
  other arithmetic  10.2 us (12%)
  local copies, waits for them, and re-layouts  2.21 us (3%)
  between operations  1.16 us (1%)
    ppermute x7, starting transfers between devices, moved(): lax.ppermute(block, 'tm', [(i, i + distance) for i in range(size) if 0 <=...  19 us
    pallas_call x2, Pallas kernels, attend(): pl.pallas_call(attend_kernel, grid_spec=pltpu.PrefetchScalarGridSpec(num_...  18.8 us
    ppermute x7, waiting for transfers between devices, moved(): lax.ppermute(block, 'tm', [(i, i + distance) for i in range(size) if 0 <=...  17.2 us
    ppermute x8, starting transfers between devices, swap(): return lax.ppermute(block, 'space', [(0, 1), (1, 0)])  9.86 us
    ppermute x8, waiting for transfers between devices, swap(): return lax.ppermute(block, 'space', [(0, 1), (1, 0)])  6.65 us
    select_n x3, other arithmetic, placed(): jnp.where(side == 0, jnp.concatenate([own, other], axis=1), jnp.concatena...  3.05 us
    concatenate x6, other arithmetic, packed(): jnp.concatenate([lax.dynamic_slice_in_dim(a, start, width, 1) for a in ar...  3.05 us
    select_n x2, other arithmetic, attended(): jnp.where(odd, kv2_other[c], kv_other[c])  2.22 us
  transfers between devices with their start and end apart: 19, of which 7 were waited for; matrix products, arithmetic and copies ran while one was open for 9% of the time, Pallas kernels for 22%

profile of v2, /device:TPU:0, one launch (start us, length us, event | category | flops | bytes accessed | tf_op | source)
XLA Modules:
  0.0 86.1 jit_solution(11800489426794018543)
XLA Ops:
  0.7 1.1 %constant_dynamic-slice_fusion.10 = (bf16[128,512]{1,0:T(8,128)(2,1)S(1)}, bf16[128,512]{1,0:T(8,128)(2,1)S(1)}) fusion(bf16[128,2048]{1,0:T(8,128)(2,1)} %v_own.3, s32[]{:T(128)S(6)} %select_n.94, bf16[128,2048]{1,0:T(8,128)(2,1)} %k_own.3), kind=kLoop, calls=%fused_computation.44 | loop fusion | bytes 524292 | tf_op jit(solution)/shard_map/dynamic_slice | solution.py:142
  1.7 0.7 pad_maximum_fusion.4
  2.5 2.9 %collective-permute-start.1 = (bf16[256,512]{1,0:T(8,128)(2,1)}, bf16[256,512]{1,0:T(8,128)(2,1)}, u32[]{:S(2)}, u32[]{:S(2)}) collective-permute-start(bf16[256,512]{1,0:T(8,128)(2,1)} %pad_maximum_fusion.4), channel_id=1, source_target_pairs={{0,1},{1,0},{2,3},{3,2},{4,5},{5,4},{6,7},{7,6},{8,9},{9,8},{10,11... | collective-permute-start | bytes 786440 | tf_op jit(solution)/shard_map/ppermute | solution.py:304
  5.5 0.0 copy-start.1
  5.5 0.7 pad_maximum_fusion.5
  6.2 0.0 collective-permute-start.7
  6.2 0.7 pad_maximum_fusion.6
  7.0 4.6 %collective-permute-start.2 = (bf16[256,512]{1,0:T(8,128)(2,1)}, bf16[256,512]{1,0:T(8,128)(2,1)}, u32[]{:S(2)}, u32[]{:S(2)}) collective-permute-start(bf16[256,512]{1,0:T(8,128)(2,1)} %pad_maximum_fusion.6), channel_id=1, source_target_pairs={{0,4},{2,6},{4,8},{6,10},{8,12},{10,14},{12,16},{14,18},{16,20},{1... | collective-permute-start | bytes 786440 | tf_op jit(solution)/shard_map/ppermute | solution.py:313
  11.7 0.8 pad_maximum_fusion
  12.5 1.5 %collective-permute-start = (bf16[256,1024]{1,0:T(8,128)(2,1)}, bf16[256,1024]{1,0:T(8,128)(2,1)}, u32[]{:S(2)}, u32[]{:S(2)}) collective-permute-start(bf16[256,1024]{1,0:T(8,128)(2,1)} %pad_maximum_fusion), channel_id=1, source_target_pairs={{0,1},{1,0},{2,3},{3,2},{4,5},{5,4},{6,7},{7,6},{8,9},{9,8},{10,11... | collective-permute-start | bytes 1572872 | tf_op jit(solution)/shard_map/ppermute | solution.py:304
  14.1 0.6 collective-permute-start.6
  14.8 2.8 %collective-permute-start.3 = (bf16[256,512]{1,0:T(8,128)(2,1)}, bf16[256,512]{1,0:T(8,128)(2,1)S(1)}, u32[]{:S(2)}, u32[]{:S(2)}) collective-permute-start(bf16[256,512]{1,0:T(8,128)(2,1)} %collective-permute-done.1.kv_other), channel_id=1, source_target_pairs={{0,4},{2,6},{4,8},{6,10},{8,12},{10,14},{12,16},{14,18},{16,20},{1... | collective-permute-start | bytes 786440 | tf_op jit(solution)/shard_map/ppermute | solution.py:313
  17.6 3.4 %collective-permute-start.8 = (bf16[256,512]{1,0:T(8,128)(2,1)S(1)}, bf16[256,512]{1,0:T(8,128)(2,1)S(1)}, u32[]{:S(2)}, u32[]{:S(2)}) collective-permute-start(bf16[256,512]{1,0:T(8,128)(2,1)S(1)} %pad_maximum_fusion.7), channel_id=1, source_target_pairs={{0,4},{2,6},{4,8},{6,10},{8,12},{10,14},{12,16},{14,18},{16,20},{1... | collective-permute-start | bytes 786440 | tf_op jit(solution)/shard_map/ppermute | solution.py:313
  21.0 0.1 broadcast_select_fusion.3
  21.1 3.5 %collective-permute-done.3.kv2_other = bf16[256,512]{1,0:T(8,128)(2,1)S(1)} collective-permute-done((bf16[256,512]{1,0:T(8,128)(2,1)}, bf16[256,512]{1,0:T(8,128)(2,1)S(1)}, u32[]{:S(2)}, u32[]{:S(2)}) %collective-permute-start.3) | collective-permute-done | bytes 262176 | tf_op jit(solution)/shard_map/ppermute | solution.py:313
  24.6 1.1 %broadcast_select_fusion.2 = bf16[256,512]{1,0:T(8,128)(2,1)S(1)} fusion(bf16[256,512]{1,0:T(8,128)(2,1)S(1)} %collective-permute-done.3.kv2_other, bf16[256,512]{1,0:T(8,128)(2,1)} %collective-permute-done.1.kv_other, pred[]{:T(512)S(6)} %eq.11), kind=kLoop, calls=%fused_computation.32 | loop fusion | flops 131072 | bytes 786433 | tf_op jit(solution)/shard_map/jit(_where)/select_n | solution.py:358
  25.7 0.1 collective-permute-start.4
  25.8 4.3 %collective-permute-start.9 = (bf16[256,512]{1,0:T(8,128)(2,1)}, bf16[256,512]{1,0:T(8,128)(2,1)S(1)}, u32[]{:S(2)}, u32[]{:S(2)}) collective-permute-start(bf16[256,512]{1,0:T(8,128)(2,1)} %collective-permute-done.7.kv_other), channel_id=1, source_target_pairs={{0,4},{2,6},{4,8},{6,10},{8,12},{10,14},{12,16},{14,18},{16,20},{1... | collective-permute-start | bytes 786440 | tf_op jit(solution)/shard_map/ppermute | solution.py:313
  30.1 0.6 pad_add_fusion.code_ref
  30.8 0.8 copy-done.9
  31.6 9.4 %shard_map.85 = (bf16[128,1024]{1,0:T(8,128)(2,1)}, bf16[128,1024]{1,0:T(8,128)(2,1)}, f32[512,512]{1,0:T(8,128)}, bf16[512,512]{1,0:T(8,128)(2,1)}, bf16[256,512]{1,0:T(8,128)(2,1)}, /*index=5*/bf16[256,512]{1,0:T(8,128)(2,1)}) custom-call(s32[1]{0:T(128)} %bitcast.side_ref, s32[12]{0:T(128)} %pad_add_fusion.code_ref, bf16[128,4096]{1,0:T(8,128)(2,1)} %q_own.3, ...), custom_call_target="tpu_custom_call" | custom-call | tf_op jit(solution)/shard_map/pallas_call | solution.py:279
  41.0 0.3 collective-permute-start.5
  41.3 0.1 broadcast_select_fusion.1
  41.4 1.1 %broadcast_select_fusion = bf16[256,512]{1,0:T(8,128)(2,1)S(1)} fusion(bf16[256,512]{1,0:T(8,128)(2,1)S(1)} %collective-permute-done.9.kv2_other, bf16[256,512]{1,0:T(8,128)(2,1)} %collective-permute-done.7.kv_other, pred[]{:T(512)S(6)} %eq.11), kind=kLoop, calls=%fused_computation.30 | loop fusion | flops 131072 | bytes 786433 | tf_op jit(solution)/shard_map/jit(_where)/select_n | solution.py:358
  42.6 0.1 collective-permute-start.10
  42.7 0.5 collective-permute-done.5
  43.2 0.2 fusion.1
  43.4 1.3 %collective-permute-start.14 = (bf16[512,512]{1,0:T(8,128)(2,1)S(1)}, bf16[512,512]{1,0:T(8,128)(2,1)S(1)}, u32[]{:S(2)}, u32[]{:S(2)}) collective-permute-start(bf16[512,512]{1,0:T(8,128)(2,1)S(1)} %fusion.1), channel_id=1, source_target_pairs={{4,0},{6,2},{8,4},{10,6},{12,8},{14,10},{16,12},{18,14},{20,16},{2... | collective-permute-start | bytes 1572872 | tf_op jit(solution)/shard_map/ppermute | solution.py:313
  44.7 1.6 %collective-permute-start.11 = (bf16[128,1024]{1,0:T(8,128)(2,1)}, bf16[128,1024]{1,0:T(8,128)(2,1)S(1)}, u32[]{:S(2)}, u32[]{:S(2)}) collective-permute-start(bf16[128,1024]{1,0:T(8,128)(2,1)} %get-tuple-element.53), channel_id=1, source_target_pairs={{0,1},{1,0},{2,3},{3,2},{4,5},{5,4},{6,7},{7,6},{8,9},{9,8},{10,11... | collective-permute-start | bytes 786440 | tf_op jit(solution)/shard_map/ppermute | solution.py:304
  46.2 9.4 %shard_map.86 = (bf16[128,1024]{1,0:T(8,128)(2,1)}, bf16[128,1024]{1,0:T(8,128)(2,1)}, f32[512,512]{1,0:T(8,128)}, bf16[512,512]{1,0:T(8,128)(2,1)}, bf16[256,512]{1,0:T(8,128)(2,1)}, /*index=5*/bf16[256,512]{1,0:T(8,128)(2,1)}) custom-call(s32[1]{0:T(128)} %bitcast.side_ref, s32[12]{0:T(128)} %pad_add_fusion.code_ref, bf16[128,4096]{1,0:T(8,128)(2,1)} %q_own.3, ...), custom_call_target="tpu_custom_call" | custom-call | tf_op jit(solution)/shard_map/pallas_call | solution.py:279
  55.7 0.1 collective-permute-start.13
  55.8 0.6 collective-permute-start.12
  56.4 2.9 %collective-permute-done.14 = bf16[512,512]{1,0:T(8,128)(2,1)S(1)} collective-permute-done((bf16[512,512]{1,0:T(8,128)(2,1)S(1)}, bf16[512,512]{1,0:T(8,128)(2,1)S(1)}, u32[]{:S(2)}, u32[]{:S(2)}) %collective-permute-start.14) | collective-permute-done | bytes 524320 | tf_op jit(solution)/shard_map/ppermute | solution.py:313
  59.3 0.2 fusion.4
  59.6 1.5 %collective-permute-start.16 = (bf16[256,512]{1,0:T(8,128)(2,1)S(1)}, bf16[256,512]{1,0:T(8,128)(2,1)S(1)}, u32[]{:S(2)}, u32[]{:S(2)}) collective-permute-start(bf16[256,512]{1,0:T(8,128)(2,1)S(1)} %slice.76), channel_id=1, source_target_pairs={{0,1},{1,0},{2,3},{3,2},{4,5},{5,4},{6,7},{7,6},{8,9},{9,8},{10,11... | collective-permute-start | bytes 786440 | tf_op jit(solution)/shard_map/ppermute | solution.py:304
  61.1 0.1 convert_select_fusion
  61.3 0.2 fusion.9
  61.5 1.3 %collective-permute-start.15 = (bf16[256,512]{1,0:T(8,128)(2,1)S(1)}, bf16[256,512]{1,0:T(8,128)(2,1)S(1)}, u32[]{:S(2)}, u32[]{:S(2)}) collective-permute-start(bf16[256,512]{1,0:T(8,128)(2,1)S(1)} %get-tuple-element.67), channel_id=1, source_target_pairs={{4,0},{6,2},{8,4},{10,6},{12,8},{14,10},{16,12},{18,14},{20,16},{2... | collective-permute-start | bytes 786440 | tf_op jit(solution)/shard_map/ppermute | solution.py:313
  62.8 1.3 %collective-permute-start.17 = (bf16[256,512]{1,0:T(8,128)(2,1)S(1)}, bf16[256,512]{1,0:T(8,128)(2,1)S(1)}, u32[]{:S(2)}, u32[]{:S(2)}) collective-permute-start(bf16[256,512]{1,0:T(8,128)(2,1)S(1)} %get-tuple-element.68), channel_id=1, source_target_pairs={{4,0},{6,2},{8,4},{10,6},{12,8},{14,10},{16,12},{18,14},{20,16},{2... | collective-permute-start | bytes 786440 | tf_op jit(solution)/shard_map/ppermute | solution.py:313
  64.1 1.1 %collective-permute-done.12 = bf16[128,1024]{1,0:T(8,128)(2,1)S(1)} collective-permute-done((bf16[128,1024]{1,0:T(8,128)(2,1)}, bf16[128,1024]{1,0:T(8,128)(2,1)S(1)}, u32[]{:S(2)}, u32[]{:S(2)}) %collective-permute-start.12) | collective-permute-done | bytes 262176 | tf_op jit(solution)/shard_map/ppermute | solution.py:304
  65.2 1.2 %maximum_select_fusion = bf16[128,4096]{1,0:T(8,128)(2,1)} fusion(bf16[128,1024]{1,0:T(8,128)(2,1)S(1)} %collective-permute-done.12, bf16[128,1024]{1,0:T(8,128)(2,1)S(1)} %collective-permute-done.11, bf16[128,1024]{1,0:T(8,128)(2,1)S(1)} %copy-done.11, bf16[128,1024]{1,0:T(8,128)(2,1)S(1)} %copy-done.10, pred[]{:T(512)S(6)} %eq.10), kind=kLoop, calls=%fused_computation.9 | loop fusion | flops 8912896 | bytes 2097153 | tf_op jit(solution)/shard_map/jit(_where)/select_n | solution.py:398
  66.4 6.8 %collective-permute-done.15 = bf16[256,512]{1,0:T(8,128)(2,1)S(1)} collective-permute-done((bf16[256,512]{1,0:T(8,128)(2,1)S(1)}, bf16[256,512]{1,0:T(8,128)(2,1)S(1)}, u32[]{:S(2)}, u32[]{:S(2)}) %collective-permute-start.15) | collective-permute-done | bytes 262176 | tf_op jit(solution)/shard_map/ppermute | solution.py:313
  73.2 4.0 %collective-permute-done.17 = bf16[256,512]{1,0:T(8,128)(2,1)S(1)} collective-permute-done((bf16[256,512]{1,0:T(8,128)(2,1)S(1)}, bf16[256,512]{1,0:T(8,128)(2,1)S(1)}, u32[]{:S(2)}, u32[]{:S(2)}) %collective-permute-start.17) | collective-permute-done | bytes 262176 | tf_op jit(solution)/shard_map/ppermute | solution.py:313
  77.2 0.3 fusion.8
  77.5 1.1 %collective-permute-start.18 = (bf16[256,512]{1,0:T(8,128)(2,1)S(1)}, bf16[256,512]{1,0:T(8,128)(2,1)S(1)}, u32[]{:S(2)}, u32[]{:S(2)}) collective-permute-start(bf16[256,512]{1,0:T(8,128)(2,1)S(1)} %get-tuple-element.66), channel_id=1, source_target_pairs={{0,1},{1,0},{2,3},{3,2},{4,5},{5,4},{6,7},{7,6},{8,9},{9,8},{10,11... | collective-permute-start | bytes 786440 | tf_op jit(solution)/shard_map/ppermute | solution.py:304
  78.7 5.6 %collective-permute-done.18 = bf16[256,512]{1,0:T(8,128)(2,1)S(1)} collective-permute-done((bf16[256,512]{1,0:T(8,128)(2,1)S(1)}, bf16[256,512]{1,0:T(8,128)(2,1)S(1)}, u32[]{:S(2)}, u32[]{:S(2)}) %collective-permute-start.18) | collective-permute-done | bytes 262176 | tf_op jit(solution)/shard_map/ppermute | solution.py:304
  84.3 0.9 %maximum_select_fusion.2 = bf16[128,2048]{1,0:T(8,128)(2,1)} fusion(bf16[128,512]{1,0:T(8,128)(2,1)S(1)} %get-tuple-element.77, bf16[128,512]{1,0:T(8,128)(2,1)S(1)} %get-tuple-element.75, bf16[128,512]{1,0:T(8,128)(2,1)S(1)} %get-tuple-element.73, bf16[128,512]{1,0:T(8,128)(2,1)S(1)} %get-tuple-element.69, pred[]{:T(512)S(6)} %eq.10), kind=kLoop, calls=%fused_computation.25 | loop fusion | flops 4456448 | bytes 1048577 | tf_op jit(solution)/shard_map/jit(_where)/select_n | solution.py:398
  85.2 0.9 %maximum_select_fusion.1 = bf16[128,2048]{1,0:T(8,128)(2,1)} fusion(bf16[128,512]{1,0:T(8,128)(2,1)S(1)} %get-tuple-element.78, bf16[128,512]{1,0:T(8,128)(2,1)S(1)} %get-tuple-element.76, bf16[128,512]{1,0:T(8,128)(2,1)S(1)} %get-tuple-element.74, bf16[128,512]{1,0:T(8,128)(2,1)S(1)} %get-tuple-element.70, pred[]{:T(512)S(6)} %eq.10), kind=kLoop, calls=%fused_computation.24 | loop fusion | flops 4456448 | bytes 1048577 | tf_op jit(solution)/shard_map/jit(_where)/select_n | solution.py:398
  (67 shorter events, 0.5 us)
Async XLA Ops:
  0.6 4.8 %copy-start.2 = (bf16[128,2048]{1,0:T(8,128)(2,1)S(1)}, bf16[128,2048]{1,0:T(8,128)(2,1)}, u32[]{:S(2)}) copy-start(bf16[128,2048]{1,0:T(8,128)(2,1)} %k_own.3) | copy-start | bytes 1572868
  0.6 4.8 %copy-start.3 = (bf16[128,2048]{1,0:T(8,128)(2,1)S(1)}, bf16[128,2048]{1,0:T(8,128)(2,1)}, u32[]{:S(2)}) copy-start(bf16[128,2048]{1,0:T(8,128)(2,1)} %v_own.3) | copy-start | bytes 1572868
  2.5 12.3 %collective-permute-start.1 = (bf16[256,512]{1,0:T(8,128)(2,1)}, bf16[256,512]{1,0:T(8,128)(2,1)}, u32[]{:S(2)}, u32[]{:S(2)}) collective-permute-start(bf16[256,512]{1,0:T(8,128)(2,1)} %pad_maximum_fusion.4), channel_id=1, source_target_pairs={{0,1},{1,0},{2,3},{3,2},{4,5},{5,4},{6,7},{7,6},{8,9},{9,8},{10,11... | collective-permute-start | bytes 786440 | tf_op jit(solution)/shard_map/ppermute | solution.py:304
  5.4 6.2 %copy-start = (bf16[128,4096]{1,0:T(8,128)(2,1)S(1)}, bf16[128,4096]{1,0:T(8,128)(2,1)}, u32[]{:S(2)}) copy-start(bf16[128,4096]{1,0:T(8,128)(2,1)} %q_own.3) | copy-start | bytes 3145732
  5.5 6.2 %copy-start.1 = (bf16[128,4096]{1,0:T(8,128)(2,1)S(1)}, bf16[128,4096]{1,0:T(8,128)(2,1)}, u32[]{:S(2)}) copy-start(bf16[128,4096]{1,0:T(8,128)(2,1)} %g_own.3) | copy-start | bytes 3145732
  6.2 19.6 %collective-permute-start.7 = (bf16[256,512]{1,0:T(8,128)(2,1)}, bf16[256,512]{1,0:T(8,128)(2,1)}, u32[]{:S(2)}, u32[]{:S(2)}) collective-permute-start(bf16[256,512]{1,0:T(8,128)(2,1)} %pad_maximum_fusion.5), channel_id=1, source_target_pairs={{0,1},{1,0},{2,3},{3,2},{4,5},{5,4},{6,7},{7,6},{8,9},{9,8},{10,11... | collective-permute-start | bytes 786440 | tf_op jit(solution)/shard_map/ppermute | solution.py:304
  7.0 10.6 %collective-permute-start.2 = (bf16[256,512]{1,0:T(8,128)(2,1)}, bf16[256,512]{1,0:T(8,128)(2,1)}, u32[]{:S(2)}, u32[]{:S(2)}) collective-permute-start(bf16[256,512]{1,0:T(8,128)(2,1)} %pad_maximum_fusion.6), channel_id=1, source_target_pairs={{0,4},{2,6},{4,8},{6,10},{8,12},{10,14},{12,16},{14,18},{16,20},{1... | collective-permute-start | bytes 786440 | tf_op jit(solution)/shard_map/ppermute | solution.py:313
  12.5 18.3 %collective-permute-start = (bf16[256,1024]{1,0:T(8,128)(2,1)}, bf16[256,1024]{1,0:T(8,128)(2,1)}, u32[]{:S(2)}, u32[]{:S(2)}) collective-permute-start(bf16[256,1024]{1,0:T(8,128)(2,1)} %pad_maximum_fusion), channel_id=1, source_target_pairs={{0,1},{1,0},{2,3},{3,2},{4,5},{5,4},{6,7},{7,6},{8,9},{9,8},{10,11... | collective-permute-start | bytes 1572872 | tf_op jit(solution)/shard_map/ppermute | solution.py:304
  14.1 32.1 %collective-permute-start.6 = (bf16[256,1024]{1,0:T(8,128)(2,1)S(1)}, bf16[256,1024]{1,0:T(8,128)(2,1)}, u32[]{:S(2)}, u32[]{:S(2)}) collective-permute-start(bf16[256,1024]{1,0:T(8,128)(2,1)S(1)} %pad_maximum_fusion.2), channel_id=1, source_target_pairs={{0,1},{1,0},{2,3},{3,2},{4,5},{5,4},{6,7},{7,6},{8,9},{9,8},{10,11... | collective-permute-start | bytes 1572872 | tf_op jit(solution)/shard_map/ppermute | solution.py:304
  14.8 9.8 %collective-permute-start.3 = (bf16[256,512]{1,0:T(8,128)(2,1)}, bf16[256,512]{1,0:T(8,128)(2,1)S(1)}, u32[]{:S(2)}, u32[]{:S(2)}) collective-permute-start(bf16[256,512]{1,0:T(8,128)(2,1)} %collective-permute-done.1.kv_other), channel_id=1, source_target_pairs={{0,4},{2,6},{4,8},{6,10},{8,12},{10,14},{12,16},{14,18},{16,20},{1... | collective-permute-start | bytes 786440 | tf_op jit(solution)/shard_map/ppermute | solution.py:313
  17.6 23.7 %collective-permute-start.8 = (bf16[256,512]{1,0:T(8,128)(2,1)S(1)}, bf16[256,512]{1,0:T(8,128)(2,1)S(1)}, u32[]{:S(2)}, u32[]{:S(2)}) collective-permute-start(bf16[256,512]{1,0:T(8,128)(2,1)S(1)} %pad_maximum_fusion.7), channel_id=1, source_target_pairs={{0,4},{2,6},{4,8},{6,10},{8,12},{10,14},{12,16},{14,18},{16,20},{1... | collective-permute-start | bytes 786440 | tf_op jit(solution)/shard_map/ppermute | solution.py:313
  21.1 4.7 %copy-start.16 = (s32[2,6]{1,0:T(2,128)S(1)}, s32[2,6]{1,0:T(2,128)}, u32[]{:S(2)}) copy-start(s32[2,6]{1,0:T(2,128)} %param.11) | copy-start | bytes 148
  21.1 4.7 %copy-start.17 = (s32[2,6]{1,0:T(2,128)S(1)}, s32[2,6]{1,0:T(2,128)}, u32[]{:S(2)}) copy-start(s32[2,6]{1,0:T(2,128)} %param.10) | copy-start | bytes 148
  24.6 6.2 %copy-start.7 = (bf16[256,512]{1,0:T(8,128)(2,1)}, bf16[256,512]{1,0:T(8,128)(2,1)S(1)}, u32[]{:S(2)}) copy-start(bf16[256,512]{1,0:T(8,128)(2,1)S(1)} %collective-permute-done.3.kv2_other) | copy-start | bytes 786436
  25.7 5.1 %collective-permute-start.4 = (bf16[512,512]{1,0:T(8,128)(2,1)S(1)}, bf16[512,512]{1,0:T(8,128)(2,1)S(1)}, u32[]{:S(2)}, u32[]{:S(2)}) collective-permute-start(bf16[512,512]{1,0:T(8,128)(2,1)S(1)} %pad_maximum_fusion.1), channel_id=1, source_target_pairs={{0,2},{2,0},{4,6},{6,4},{8,10},{10,8},{12,14},{14,12},{16,18},{18,... | collective-permute-start | bytes 1572872 | tf_op jit(solution)/shard_map/ppermute | solution.py:308
  25.8 15.5 %collective-permute-start.9 = (bf16[256,512]{1,0:T(8,128)(2,1)}, bf16[256,512]{1,0:T(8,128)(2,1)S(1)}, u32[]{:S(2)}, u32[]{:S(2)}) collective-permute-start(bf16[256,512]{1,0:T(8,128)(2,1)} %collective-permute-done.7.kv_other), channel_id=1, source_target_pairs={{0,4},{2,6},{4,8},{6,10},{8,12},{10,14},{12,16},{14,18},{16,20},{1... | collective-permute-start | bytes 786440 | tf_op jit(solution)/shard_map/ppermute | solution.py:313
  30.8 0.8 copy-start.9
  41.0 2.2 %collective-permute-start.5 = (bf16[512,512]{1,0:T(8,128)(2,1)}, bf16[512,512]{1,0:T(8,128)(2,1)S(1)}, u32[]{:S(2)}, u32[]{:S(2)}) collective-permute-start(bf16[512,512]{1,0:T(8,128)(2,1)} %get-tuple-element.45), channel_id=1, source_target_pairs={{0,2},{2,0},{4,6},{6,4},{8,10},{10,8},{12,14},{14,12},{16,18},{18,... | collective-permute-start | bytes 1572872 | tf_op jit(solution)/shard_map/ppermute | solution.py:308
  41.3 1.3 %copy-start.6 = (bf16[256,512]{1,0:T(8,128)(2,1)}, bf16[256,512]{1,0:T(8,128)(2,1)S(1)}, u32[]{:S(2)}) copy-start(bf16[256,512]{1,0:T(8,128)(2,1)S(1)} %collective-permute-done.8.kv2_own) | copy-start | bytes 786436
  41.4 1.8 %copy-start.12 = (bf16[256,512]{1,0:T(8,128)(2,1)S(1)}, bf16[256,512]{1,0:T(8,128)(2,1)}, u32[]{:S(2)}) copy-start(bf16[256,512]{1,0:T(8,128)(2,1)} %get-tuple-element.43) | copy-start | bytes 786436
  41.4 1.8 %copy-start.13 = (bf16[256,512]{1,0:T(8,128)(2,1)S(1)}, bf16[256,512]{1,0:T(8,128)(2,1)}, u32[]{:S(2)}) copy-start(bf16[256,512]{1,0:T(8,128)(2,1)} %get-tuple-element.44) | copy-start | bytes 786436
  41.4 2.0 %copy-start.8 = (bf16[256,512]{1,0:T(8,128)(2,1)}, bf16[256,512]{1,0:T(8,128)(2,1)S(1)}, u32[]{:S(2)}) copy-start(bf16[256,512]{1,0:T(8,128)(2,1)S(1)} %collective-permute-done.9.kv2_other) | copy-start | bytes 786436
  42.6 3.6 %collective-permute-start.10 = (bf16[512,512]{1,0:T(8,128)(2,1)S(1)}, bf16[512,512]{1,0:T(8,128)(2,1)}, u32[]{:S(2)}, u32[]{:S(2)}) collective-permute-start(bf16[512,512]{1,0:T(8,128)(2,1)S(1)} %pad_maximum_fusion.3), channel_id=1, source_target_pairs={{0,2},{2,0},{4,6},{6,4},{8,10},{10,8},{12,14},{14,12},{16,18},{18,... | collective-permute-start | bytes 1572872 | tf_op jit(solution)/shard_map/ppermute | solution.py:308
  43.4 15.9 %collective-permute-start.14 = (bf16[512,512]{1,0:T(8,128)(2,1)S(1)}, bf16[512,512]{1,0:T(8,128)(2,1)S(1)}, u32[]{:S(2)}, u32[]{:S(2)}) collective-permute-start(bf16[512,512]{1,0:T(8,128)(2,1)S(1)} %fusion.1), channel_id=1, source_target_pairs={{4,0},{6,2},{8,4},{10,6},{12,8},{14,10},{16,12},{18,14},{20,16},{2... | collective-permute-start | bytes 1572872 | tf_op jit(solution)/shard_map/ppermute | solution.py:313
  44.7 14.6 %copy-start.5 = (f32[512,512]{1,0:T(8,128)S(1)}, f32[512,512]{1,0:T(8,128)}, u32[]{:S(2)}) copy-start(f32[512,512]{1,0:T(8,128)} %get-tuple-element.63) | copy-start | bytes 3145732
  44.7 11.0 %collective-permute-start.11 = (bf16[128,1024]{1,0:T(8,128)(2,1)}, bf16[128,1024]{1,0:T(8,128)(2,1)S(1)}, u32[]{:S(2)}, u32[]{:S(2)}) collective-permute-start(bf16[128,1024]{1,0:T(8,128)(2,1)} %get-tuple-element.53), channel_id=1, source_target_pairs={{0,1},{1,0},{2,3},{3,2},{4,5},{5,4},{6,7},{7,6},{8,9},{9,8},{10,11... | collective-permute-start | bytes 786440 | tf_op jit(solution)/shard_map/ppermute | solution.py:304
  55.7 5.5 %collective-permute-start.13 = (bf16[512,512]{1,0:T(8,128)(2,1)}, bf16[512,512]{1,0:T(8,128)(2,1)S(1)}, u32[]{:S(2)}, u32[]{:S(2)}) collective-permute-start(bf16[512,512]{1,0:T(8,128)(2,1)} %get-tuple-element.57), channel_id=1, source_target_pairs={{0,2},{2,0},{4,6},{6,4},{8,10},{10,8},{12,14},{14,12},{16,18},{18,... | collective-permute-start | bytes 1572872 | tf_op jit(solution)/shard_map/ppermute | solution.py:308
  55.8 9.4 %collective-permute-start.12 = (bf16[128,1024]{1,0:T(8,128)(2,1)}, bf16[128,1024]{1,0:T(8,128)(2,1)S(1)}, u32[]{:S(2)}, u32[]{:S(2)}) collective-permute-start(bf16[128,1024]{1,0:T(8,128)(2,1)} %get-tuple-element.55), channel_id=1, source_target_pairs={{0,1},{1,0},{2,3},{3,2},{4,5},{5,4},{6,7},{7,6},{8,9},{9,8},{10,11... | collective-permute-start | bytes 786440 | tf_op jit(solution)/shard_map/ppermute | solution.py:304
  59.6 1.7 %copy-start.14 = (bf16[256,512]{1,0:T(8,128)(2,1)S(1)}, bf16[256,512]{1,0:T(8,128)(2,1)}, u32[]{:S(2)}) copy-start(bf16[256,512]{1,0:T(8,128)(2,1)} %get-tuple-element.58) | copy-start | bytes 786436
  59.6 1.7 %copy-start.15 = (bf16[256,512]{1,0:T(8,128)(2,1)S(1)}, bf16[256,512]{1,0:T(8,128)(2,1)}, u32[]{:S(2)}) copy-start(bf16[256,512]{1,0:T(8,128)(2,1)} %get-tuple-element.56) | copy-start | bytes 786436
  59.6 19.0 %collective-permute-start.16 = (bf16[256,512]{1,0:T(8,128)(2,1)S(1)}, bf16[256,512]{1,0:T(8,128)(2,1)S(1)}, u32[]{:S(2)}, u32[]{:S(2)}) collective-permute-start(bf16[256,512]{1,0:T(8,128)(2,1)S(1)} %slice.76), channel_id=1, source_target_pairs={{0,1},{1,0},{2,3},{3,2},{4,5},{5,4},{6,7},{7,6},{8,9},{9,8},{10,11... | collective-permute-start | bytes 786440 | tf_op jit(solution)/shard_map/ppermute | solution.py:304
  61.3 3.8 %copy-start.10 = (bf16[128,1024]{1,0:T(8,128)(2,1)S(1)}, bf16[128,1024]{1,0:T(8,128)(2,1)}, u32[]{:S(2)}) copy-start(bf16[128,1024]{1,0:T(8,128)(2,1)} %get-tuple-element.59) | copy-start | bytes 786436
  61.3 3.8 %copy-start.11 = (bf16[128,1024]{1,0:T(8,128)(2,1)S(1)}, bf16[128,1024]{1,0:T(8,128)(2,1)}, u32[]{:S(2)}) copy-start(bf16[128,1024]{1,0:T(8,128)(2,1)} %get-tuple-element.60) | copy-start | bytes 786436
  61.5 11.7 %collective-permute-start.15 = (bf16[256,512]{1,0:T(8,128)(2,1)S(1)}, bf16[256,512]{1,0:T(8,128)(2,1)S(1)}, u32[]{:S(2)}, u32[]{:S(2)}) collective-permute-start(bf16[256,512]{1,0:T(8,128)(2,1)S(1)} %get-tuple-element.67), channel_id=1, source_target_pairs={{4,0},{6,2},{8,4},{10,6},{12,8},{14,10},{16,12},{18,14},{20,16},{2... | collective-permute-start | bytes 786440 | tf_op jit(solution)/shard_map/ppermute | solution.py:313
  62.8 14.4 %collective-permute-start.17 = (bf16[256,512]{1,0:T(8,128)(2,1)S(1)}, bf16[256,512]{1,0:T(8,128)(2,1)S(1)}, u32[]{:S(2)}, u32[]{:S(2)}) collective-permute-start(bf16[256,512]{1,0:T(8,128)(2,1)S(1)} %get-tuple-element.68), channel_id=1, source_target_pairs={{4,0},{6,2},{8,4},{10,6},{12,8},{14,10},{16,12},{18,14},{20,16},{2... | collective-permute-start | bytes 786440 | tf_op jit(solution)/shard_map/ppermute | solution.py:313
  65.2 12.1 %copy-start.4 = (f32[512,512]{1,0:T(8,128)S(1)}, f32[512,512]{1,0:T(8,128)}, u32[]{:S(2)}) copy-start(f32[512,512]{1,0:T(8,128)} %get-tuple-element.64) | copy-start | bytes 3145732
  77.5 6.7 %collective-permute-start.18 = (bf16[256,512]{1,0:T(8,128)(2,1)S(1)}, bf16[256,512]{1,0:T(8,128)(2,1)S(1)}, u32[]{:S(2)}, u32[]{:S(2)}) collective-permute-start(bf16[256,512]{1,0:T(8,128)(2,1)S(1)} %get-tuple-element.66), channel_id=1, source_target_pairs={{0,1},{1,0},{2,3},{3,2},{4,5},{5,4},{6,7},{7,6},{8,9},{9,8},{10,11... | collective-permute-start | bytes 786440 | tf_op jit(solution)/shard_map/ppermute | solution.py:304

commit v3 on v2

--- a/solution.py
+++ b/solution.py
@@ -14,7 +14,7 @@
 STEP_HEADS = 1
 HIDDEN = -1e30
 FAR = 1 << 20
-VMEM_BYTES = 60 * 1024 * 1024
+VMEM_BYTES = 57344 * 1024
 
 
 def shifted_2(block, axis, distance):
@@ -161,7 +161,7 @@
 def attend_kernel(
     side_ref, code_ref,
     q_own, g_own, qg_other, k_own, v_own, kv_other, kv2_own, kv2_other, kv1,
-    dq_own, dq_other, d0, d1, d2_own, d2_other,
+    dq_own, dq_other, d0_own, d0_other, d1_own, d1_other, d2_own, d2_other,
     limit_ref, *scratch,
 ):
     n, d = BLOCK_TOKENS, HEAD_SIZE
@@ -206,20 +206,21 @@
                 s = dot(k_all[rows, :], q, (1, 1))
                 s = jnp.where(ahead <= limit_ref[r * 6 + p], s, HIDDEN)
                 s_ref[rows, :] = s
-                high = jnp.max(s, axis=0, keepdims=True)
+                high = jnp.max(s.reshape(n // 8, 8, lanes), axis=0)
                 top = high if top is None else jnp.maximum(top, high)
-            total = jnp.zeros((1, lanes), jnp.float32)
-            delta = jnp.zeros((1, lanes), jnp.float32)
+            top = jnp.max(top, axis=0, keepdims=True)
+            total = jnp.zeros((8, lanes), jnp.float32)
+            delta = jnp.zeros((8, lanes), jnp.float32)
             for p in range(6):
                 rows = slice(p * n, (p + 1) * n)
                 e = jnp.exp2((s_ref[rows, :] - top) * rate)
                 dp = dot(v_all[rows, :], g, (1, 1))
                 s_ref[rows, :] = e
                 dp_ref[rows, :] = dp
-                total = total + jnp.sum(e, axis=0, keepdims=True)
-                delta = delta + jnp.sum(e * dp, axis=0, keepdims=True)
-            share = 1.0 / total
-            delta = delta * share
+                total = total + jnp.sum(e.reshape(n // 8, 8, lanes), axis=0)
+                delta = delta + jnp.sum((e * dp).reshape(n // 8, 8, lanes), axis=0)
+            share = 1.0 / jnp.sum(total, axis=0, keepdims=True)
+            delta = jnp.sum(delta, axis=0, keepdims=True) * share
             for p in range(6):
                 rows = slice(p * n, (p + 1) * n)
                 prob = s_ref[rows, :] * share
@@ -228,11 +229,10 @@
                 ds_ref[rows, cols] = ds.astype(jnp.bfloat16)
         dk = dot(ds_ref[...], q_all[...], (1, 0)) * scale
         dv = dot(p_ref[...], g_all[...], (1, 0))
-        homes = ((d0, 0), (d0, 2), (d1, 0), (d1, 2), (d2_own, 0), (d2_other, 0))
-        for p, (out, place) in enumerate(homes):
+        for p, out in enumerate((d0_own, d0_other, d1_own, d1_other, d2_own, d2_other)):
             rows = slice(p * n, (p + 1) * n)
-            out[place * n : (place + 1) * n, slim] = dk[rows].astype(out.dtype)
-            out[(place + 1) * n : (place + 2) * n, slim] = dv[rows].astype(out.dtype)
+            out[:n, slim] = dk[rows].astype(out.dtype)
+            out[n:, slim] = dv[rows].astype(out.dtype)
         dq = (dot(k_all[...], ds_ref[...], (0, 0)) * scale).T.astype(jnp.bfloat16)
         for j in range(2):
             here = slice((2 * h + j) * d, (2 * h + j + 1) * d)
@@ -261,8 +261,10 @@
     outs = [
         out(n, wide, jnp.bfloat16),
         out(n, wide, jnp.bfloat16),
-        out(4 * n, slim, jnp.float32),
-        out(4 * n, slim, jnp.bfloat16),
+        out(2 * n, slim, jnp.float32),
+        out(2 * n, slim, jnp.float32),
+        out(2 * n, slim, jnp.bfloat16),
+        out(2 * n, slim, jnp.bfloat16),
         out(2 * n, slim, jnp.bfloat16),
         out(2 * n, slim, jnp.bfloat16),
     ]
@@ -347,8 +349,10 @@
 
     kv_other = [swap(b) for b in kv_away]
     qg_other = [swap(b) for b in qg_away]
-    kv2_own = [moved(b, 2) for b in kv_own]
-    kv2_other = [moved(b, 2) for b in kv_other]
+    kv2_own, kv2_other = [moved(kv_own[0], 2)], [moved(kv_other[0], 2)]
+    late = moved(jnp.concatenate([kv_own[1], kv_other[1]], axis=0), 2)
+    kv2_own.append(late[: 2 * n])
+    kv2_other.append(late[2 * n :])
 
     def attended(c, *earlier):
         kv1 = mate(
@@ -366,32 +370,36 @@
             qg_other[c], kv_other[c], kv2_own[c], kv2_other[c], kv1,
         )
 
-    def met(d1):
-        both = mate(d1).astype(jnp.float32)
-        return jnp.where(odd, both, 0.0), jnp.where(odd, 0.0, both)
-
     def low(total):
         return total.astype(jnp.bfloat16)
 
-    dq_own0, dq_away0, e0, d1, d2_own, d2_other = attended(0)
+    def back_sum(own, met):
+        return low(own + jnp.where(odd, met.astype(jnp.float32), 0.0))
+
+    def here_sum(own, met, back):
+        return low(own + jnp.where(odd, 0.0, met.astype(jnp.float32)) + back)
+
+    dq_own0, dq_away0, e0_own, e0_other, e1_own, e1_other, e2_own, e2_other = attended(0)
+    e1_own, e1_other = after([e1_own, e1_other], qg_other[1])
     dq_other0 = swap(dq_away0)
-    met_back, met_here0 = met(d1)
-    ship0 = low(jnp.concatenate([d2_own, d2_other], axis=0) + met_back)
-    back0 = moved(ship0, -2)
-    dq_own1, dq_away1, d0, d1, d2_own, d2_other = attended(1, ship0)
-    d1, dq_other0 = after([d1, dq_other0])
+    e1_own, e1_other = mate(e1_own), mate(e1_other)
+    ship0 = [jnp.concatenate([back_sum(e2_own, e1_own), back_sum(e2_other, e1_other)], axis=0)]
+    back0 = moved(ship0[0], -2)
+    back_own0, back_other0 = back0[: 2 * n], back0[2 * n :]
+
+    dq_own1, dq_away1, d0_own, d0_other, d1_own, d1_other, d2_own, d2_other = attended(1, *ship0)
+    d1_own, d1_other, back_other0 = after([d1_own, d1_other, back_other0])
     dq_other1 = swap(dq_away1)
-    met_back, met_here = met(d1)
-    ship_other = low(d2_other + met_back[2 * n :])
-    ship_own = low(d2_own + met_back[: 2 * n])
+    d1_other = mate(d1_other)
+    d1_own = mate(d1_own)
+    ship_other = back_sum(d2_other, d1_other)
     back_other = moved(ship_other, -2)
+    ship_own = back_sum(d2_own, d1_own)
     back_own = moved(ship_own, -2)
-    sum0 = low(e0 + met_here0 + back0)
-    own0 = sum0[: 2 * n]
-    other0 = swap(sum0[2 * n :])
-    sum_other = low(d0[2 * n :] + met_here[2 * n :] + back_other)
-    other1 = swap(sum_other)
-    own1 = low(d0[: 2 * n] + met_here[: 2 * n] + back_own)
+    other0 = swap(here_sum(e0_other, e1_other, back_other0))
+    other1 = swap(here_sum(d0_other, d1_other, back_other))
+    own0 = here_sum(e0_own, e1_own, back_own0)
+    own1 = here_sum(d0_own, d1_own, back_own)
 
     def placed(own, other):
         own, other = jnp.concatenate(own, axis=1), jnp.concatenate(other, axis=1)

time: 86.5 us -> 82.4 us (0.953)
  starting transfers between devices: 29.3 us -> 25.8 us
  waiting for transfers between devices: 24.4 us -> 22.1 us
  local copies, waits for them, and re-layouts: 2.21 us -> 3.91 us
    ppermute x7 -> x6, waiting for transfers between devices: 17.2 us -> 12.6 us  [moved(): lax.ppermute(block, 'tm', [(i, i + distance) for i in range(size) if 0 <=...]
    ppermute x7 -> x6, starting transfers between devices: 19 us -> 14.7 us  [moved(): lax.ppermute(block, 'tm', [(i, i + distance) for i in range(size) if 0 <=...]
    ppermute x8, waiting for transfers between devices: 6.65 us -> 8.76 us  [swap(): return lax.ppermute(block, 'space', [(0, 1), (1, 0)])]
    unnamed x36 -> x48, local copies, waits for them, and re-layouts: 0.87 us -> 2.56 us
    select_n x2 -> x1, other arithmetic: 2.22 us -> 1.07 us  [attended(): jnp.where(odd, kv2_other[c], kv_other[c])]
    select_n x2, other arithmetic: 0.14 us -> 1.09 us  [attended(): jnp.where(odd, kv2_own[c], kv_own[c])]
    concatenate x6 -> x5, other arithmetic: 3.05 us -> 3.83 us  [packed(): jnp.concatenate([lax.dynamic_slice_in_dim(a, start, width, 1) for a in ar...]
  transfers between devices with their start and end apart: 19 -> 20, of which waited for: 7 -> 11; matrix products, arithmetic and copies ran while one was open for 9% -> 10% of each run, Pallas kernels for 22% -> 23%
where the time goes in v3:
time: 82.4 us; the launch traced here: 82 us
  starting transfers between devices  25.8 us (31%)
  waiting for transfers between devices  22.1 us (27%)
  Pallas kernels  18.5 us (22%)
  other arithmetic  10.6 us (13%)
  local copies, waits for them, and re-layouts  3.91 us (5%)
  between operations  1.15 us (1%)
    pallas_call x2, Pallas kernels, attend(): pl.pallas_call(attend_kernel, grid_spec=pltpu.PrefetchScalarGridSpec(num_...  18.5 us
    ppermute x6, starting transfers between devices, moved(): lax.ppermute(block, 'tm', [(i, i + distance) for i in range(size) if 0 <=...  14.7 us
    ppermute x6, waiting for transfers between devices, moved(): lax.ppermute(block, 'tm', [(i, i + distance) for i in range(size) if 0 <=...  12.6 us
    ppermute x8, starting transfers between devices, swap(): return lax.ppermute(block, 'space', [(0, 1), (1, 0)])  9.77 us
    ppermute x8, waiting for transfers between devices, swap(): return lax.ppermute(block, 'space', [(0, 1), (1, 0)])  8.76 us
    concatenate x5, other arithmetic, packed(): jnp.concatenate([lax.dynamic_slice_in_dim(a, start, width, 1) for a in ar...  3.83 us
    select_n x3, other arithmetic, placed(): jnp.where(side == 0, jnp.concatenate([own, other], axis=1), jnp.concatena...  3.07 us
    unnamed x48, local copies, waits for them, and re-layouts  2.56 us
  transfers between devices with their start and end apart: 20, of which 11 were waited for; matrix products, arithmetic and copies ran while one was open for 10% of the time, Pallas kernels for 23%

profile of v3, /device:TPU:0, one launch (start us, length us, event | category | flops | bytes accessed | tf_op | source)
XLA Modules:
  0.0 82.0 jit_solution(4182816842513447214)
XLA Ops:
  0.7 1.1 %constant_dynamic-slice_fusion.10 = (bf16[128,512]{1,0:T(8,128)(2,1)S(1)}, bf16[128,512]{1,0:T(8,128)(2,1)S(1)}) fusion(bf16[128,2048]{1,0:T(8,128)(2,1)} %v_own.3, s32[]{:T(128)S(6)} %select_n.108, bf16[128,2048]{1,0:T(8,128)(2,1)} %k_own.3), kind=kLoop, calls=%fused_computation.54 | loop fusion | bytes 524292 | tf_op jit(solution)/shard_map/dynamic_slice | solution.py:142
  1.7 0.7 pad_maximum_fusion.6
  2.5 2.9 %collective-permute-start.1 = (bf16[256,512]{1,0:T(8,128)(2,1)}, bf16[256,512]{1,0:T(8,128)(2,1)}, u32[]{:S(2)}, u32[]{:S(2)}) collective-permute-start(bf16[256,512]{1,0:T(8,128)(2,1)} %pad_maximum_fusion.6), channel_id=1, source_target_pairs={{0,1},{1,0},{2,3},{3,2},{4,5},{5,4},{6,7},{7,6},{8,9},{9,8},{10,11... | collective-permute-start | bytes 786440 | tf_op jit(solution)/shard_map/ppermute | solution.py:306
  5.5 0.7 pad_maximum_fusion.7
  6.3 0.6 copy-done.5
  6.9 0.7 pad_maximum_fusion.8
  7.6 4.6 %collective-permute-start.2 = (bf16[256,512]{1,0:T(8,128)(2,1)}, bf16[256,512]{1,0:T(8,128)(2,1)}, u32[]{:S(2)}, u32[]{:S(2)}) collective-permute-start(bf16[256,512]{1,0:T(8,128)(2,1)} %pad_maximum_fusion.8), channel_id=1, source_target_pairs={{0,4},{2,6},{4,8},{6,10},{8,12},{10,14},{12,16},{14,18},{16,20},{1... | collective-permute-start | bytes 786440 | tf_op jit(solution)/shard_map/ppermute | solution.py:315
  12.4 0.8 %pad_maximum_fusion = bf16[256,1024]{1,0:T(8,128)(2,1)} fusion(bf16[128,1024]{1,0:T(8,128)(2,1)S(1)} %constant_dynamic-slice_fusion.4, bf16[128,1024]{1,0:T(8,128)(2,1)S(1)} %constant_dynamic-slice_fusion.5), kind=kLoop, calls=%fused_computation.29 | loop fusion | flops 1048576 | bytes 1048576 | tf_op jit(solution)/shard_map/concatenate | solution.py:142
  13.2 1.5 %collective-permute-start = (bf16[256,1024]{1,0:T(8,128)(2,1)}, bf16[256,1024]{1,0:T(8,128)(2,1)}, u32[]{:S(2)}, u32[]{:S(2)}) collective-permute-start(bf16[256,1024]{1,0:T(8,128)(2,1)} %pad_maximum_fusion), channel_id=1, source_target_pairs={{0,1},{1,0},{2,3},{3,2},{4,5},{5,4},{6,7},{7,6},{8,9},{9,8},{10,11... | collective-permute-start | bytes 1572872 | tf_op jit(solution)/shard_map/ppermute | solution.py:306
  14.7 0.8 %pad_maximum_fusion.2 = bf16[256,1024]{1,0:T(8,128)(2,1)} fusion(bf16[128,1024]{1,0:T(8,128)(2,1)S(1)} %constant_dynamic-slice_fusion.2, bf16[128,1024]{1,0:T(8,128)(2,1)S(1)} %constant_dynamic-slice_fusion.3), kind=kLoop, calls=%fused_computation.31 | loop fusion | flops 1048576 | bytes 1048576 | tf_op jit(solution)/shard_map/concatenate | solution.py:142
  15.6 0.5 collective-permute-start.5
  16.2 2.8 %collective-permute-start.3 = (bf16[256,512]{1,0:T(8,128)(2,1)}, bf16[256,512]{1,0:T(8,128)(2,1)S(1)}, u32[]{:S(2)}, u32[]{:S(2)}) collective-permute-start(bf16[256,512]{1,0:T(8,128)(2,1)} %collective-permute-done.1.kv_other), channel_id=1, source_target_pairs={{0,4},{2,6},{4,8},{6,10},{8,12},{10,14},{12,16},{14,18},{16,20},{1... | collective-permute-start | bytes 786440 | tf_op jit(solution)/shard_map/ppermute | solution.py:315
  19.0 3.4 %collective-permute-start.9 = (bf16[512,512]{1,0:T(8,128)(2,1)S(1)}, bf16[512,512]{1,0:T(8,128)(2,1)S(1)}, u32[]{:S(2)}, u32[]{:S(2)}) collective-permute-start(bf16[512,512]{1,0:T(8,128)(2,1)S(1)} %pad_maximum_fusion.4), channel_id=1, source_target_pairs={{0,4},{2,6},{4,8},{6,10},{8,12},{10,14},{12,16},{14,18},{16,20},{1... | collective-permute-start | bytes 1572872 | tf_op jit(solution)/shard_map/ppermute | solution.py:315
  22.6 3.4 %collective-permute-done.3.kv2_other = bf16[256,512]{1,0:T(8,128)(2,1)S(1)} collective-permute-done((bf16[256,512]{1,0:T(8,128)(2,1)}, bf16[256,512]{1,0:T(8,128)(2,1)S(1)}, u32[]{:S(2)}, u32[]{:S(2)}) %collective-permute-start.3) | collective-permute-done | bytes 262176 | tf_op jit(solution)/shard_map/ppermute | solution.py:315
  26.0 1.1 %broadcast_select_fusion.1 = bf16[256,512]{1,0:T(8,128)(2,1)S(1)} fusion(bf16[256,512]{1,0:T(8,128)(2,1)S(1)} %collective-permute-done.3.kv2_other, bf16[256,512]{1,0:T(8,128)(2,1)} %collective-permute-done.1.kv_other, pred[]{:T(512)S(6)} %eq.11), kind=kLoop, calls=%fused_computation.42 | loop fusion | flops 131072 | bytes 786433 | tf_op jit(solution)/shard_map/jit(_where)/select_n | solution.py:362
  27.2 0.6 pad_add_fusion.code_ref
  27.9 1.9 %collective-permute-done.qg_other = bf16[256,1024]{1,0:T(8,128)(2,1)} collective-permute-done((bf16[256,1024]{1,0:T(8,128)(2,1)}, bf16[256,1024]{1,0:T(8,128)(2,1)}, u32[]{:S(2)}, u32[]{:S(2)}) %collective-permute-start) | collective-permute-done | bytes 524320 | tf_op jit(solution)/shard_map/ppermute | solution.py:306
  29.7 0.8 copy-done.13
  30.5 9.2 %shard_map.85 = (bf16[128,1024]{1,0:T(8,128)(2,1)}, bf16[128,1024]{1,0:T(8,128)(2,1)}, f32[256,512]{1,0:T(8,128)}, f32[256,512]{1,0:T(8,128)}, bf16[256,512]{1,0...) custom-call(s32[1]{0:T(128)} %bitcast.side_ref, ...), custom_call_target="tpu_custom_call" | custom-call | tf_op jit(solution)/shard_map/pallas_call | solution.py:281
  39.7 0.5 collective-permute-done.5.qg_other
  40.1 1.0 %maximum_select_fusion.3 = (bf16[256,512]{1,0:T(8,128)(2,1)S(1)}, bf16[256,512]{1,0:T(8,128)(2,1)}, bf16[256,512]{1,0:T(8,128)(2,1)}, bf16[256,512]{1,0:T(8,128)(2,1)S(1)}) fusion(bf16[128,512]{1,0:T(8,128)(2,1)S(1)} %constant_dynamic-slice_fusion, bf16[128,512]{1,0:T(8,128)(2,1)S(1)} %constant_dynamic-slice_fusion.1, pred[]{:T(512)S(6)} %eq.11, ...), kind=kLoop, calls=%fused_computation.40 | loop fusion | flops 786432 | bytes 2097153 | tf_op jit(solution)/shard_map/jit(_where)/select_n | solution.py:361
  41.2 0.5 collective-permute-start.7
  41.7 0.1 collective-permute-start.10
  41.9 0.2 copy-done.19
  42.2 0.6 collective-permute-done.7
  43.0 1.3 %collective-permute-start.13 = (bf16[512,512]{1,0:T(8,128)(2,1)S(1)}, bf16[512,512]{1,0:T(8,128)(2,1)S(1)}, u32[]{:S(2)}, u32[]{:S(2)}) collective-permute-start(bf16[512,512]{1,0:T(8,128)(2,1)S(1)} %pad_maximum_fusion.3), channel_id=1, source_target_pairs={{4,0},{6,2},{8,4},{10,6},{12,8},{14,10},{16,12},{18,14},{20,16},{2... | collective-permute-start | bytes 1572872 | tf_op jit(solution)/shard_map/ppermute | solution.py:315
  44.3 1.8 %collective-permute-start.11 = (bf16[128,1024]{1,0:T(8,128)(2,1)S(1)}, bf16[128,1024]{1,0:T(8,128)(2,1)S(1)}, u32[]{:S(2)}, u32[]{:S(2)}) collective-permute-start(bf16[128,1024]{1,0:T(8,128)(2,1)S(1)} %copy-done.22), channel_id=1, source_target_pairs={{0,1},{1,0},{2,3},{3,2},{4,5},{5,4},{6,7},{7,6},{8,9},{9,8},{10,11... | collective-permute-start | bytes 786440 | tf_op jit(solution)/shard_map/ppermute | solution.py:306
  46.1 0.8 copy-done.12
  46.9 9.3 %shard_map.86 = (bf16[128,1024]{1,0:T(8,128)(2,1)}, bf16[128,1024]{1,0:T(8,128)(2,1)}, f32[256,512]{1,0:T(8,128)}, f32[256,512]{1,0:T(8,128)}, bf16[256,512]{1,0...) custom-call(s32[1]{0:T(128)} %bitcast.side_ref, ...), custom_call_target="tpu_custom_call" | custom-call | tf_op jit(solution)/shard_map/pallas_call | solution.py:281
  56.2 0.3 collective-permute-start.12
  56.6 2.5 %collective-permute-done.13 = bf16[512,512]{1,0:T(8,128)(2,1)S(1)} collective-permute-done((bf16[512,512]{1,0:T(8,128)(2,1)S(1)}, bf16[512,512]{1,0:T(8,128)(2,1)S(1)}, u32[]{:S(2)}, u32[]{:S(2)}) %collective-permute-start.13) | collective-permute-done | bytes 524320 | tf_op jit(solution)/shard_map/ppermute | solution.py:315
  59.2 0.5 collective-permute-start.15
  59.7 0.1 fusion.4
  59.9 0.1 fusion.9
  60.0 1.8 %collective-permute-start.17 = (bf16[256,512]{1,0:T(8,128)(2,1)S(1)}, bf16[256,512]{1,0:T(8,128)(2,1)S(1)}, u32[]{:S(2)}, u32[]{:S(2)}) collective-permute-start(bf16[256,512]{1,0:T(8,128)(2,1)S(1)} %fusion.9), channel_id=1, source_target_pairs={{0,1},{1,0},{2,3},{3,2},{4,5},{5,4},{6,7},{7,6},{8,9},{9,8},{10,11... | collective-permute-start | bytes 786440 | tf_op jit(solution)/shard_map/ppermute | solution.py:306
  61.9 1.3 %collective-permute-start.18 = (bf16[256,512]{1,0:T(8,128)(2,1)S(1)}, bf16[256,512]{1,0:T(8,128)(2,1)S(1)}, u32[]{:S(2)}, u32[]{:S(2)}) collective-permute-start(bf16[256,512]{1,0:T(8,128)(2,1)S(1)} %fusion.11), channel_id=1, source_target_pairs={{4,0},{6,2},{8,4},{10,6},{12,8},{14,10},{16,12},{18,14},{20,16},{2... | collective-permute-start | bytes 786440 | tf_op jit(solution)/shard_map/ppermute | solution.py:315
  63.3 1.3 %collective-permute-start.16 = (bf16[256,512]{1,0:T(8,128)(2,1)S(1)}, bf16[256,512]{1,0:T(8,128)(2,1)S(1)}, u32[]{:S(2)}, u32[]{:S(2)}) collective-permute-start(bf16[256,512]{1,0:T(8,128)(2,1)S(1)} %fusion.16), channel_id=1, source_target_pairs={{4,0},{6,2},{8,4},{10,6},{12,8},{14,10},{16,12},{18,14},{20,16},{2... | collective-permute-start | bytes 786440 | tf_op jit(solution)/shard_map/ppermute | solution.py:315
  64.6 1.1 %collective-permute-done.12 = bf16[128,1024]{1,0:T(8,128)(2,1)S(1)} collective-permute-done((bf16[128,1024]{1,0:T(8,128)(2,1)}, bf16[128,1024]{1,0:T(8,128)(2,1)S(1)}, u32[]{:S(2)}, u32[]{:S(2)}) %collective-permute-start.12) | collective-permute-done | bytes 262176 | tf_op jit(solution)/shard_map/ppermute | solution.py:306
  65.7 1.2 %maximum_select_fusion = bf16[128,4096]{1,0:T(8,128)(2,1)} fusion(bf16[128,1024]{1,0:T(8,128)(2,1)S(1)} %collective-permute-done.12, bf16[128,1024]{1,0:T(8,128)(2,1)S(1)} %collective-permute-done.11, bf16[128,1024]{1,0:T(8,128)(2,1)S(1)} %copy-done.15, bf16[128,1024]{1,0:T(8,128)(2,1)S(1)} %copy-done.14, pred[]{:T(512)S(6)} %eq.10), kind=kLoop, calls=%fused_computation | loop fusion | flops 8912896 | bytes 2097153 | tf_op jit(solution)/shard_map/jit(_where)/select_n | solution.py:406
  66.9 3.5 %collective-permute-done.17 = bf16[256,512]{1,0:T(8,128)(2,1)S(1)} collective-permute-done((bf16[256,512]{1,0:T(8,128)(2,1)S(1)}, bf16[256,512]{1,0:T(8,128)(2,1)S(1)}, u32[]{:S(2)}, u32[]{:S(2)}) %collective-permute-start.17) | collective-permute-done | bytes 262176 | tf_op jit(solution)/shard_map/ppermute | solution.py:306
  70.5 2.9 %collective-permute-done.18 = bf16[256,512]{1,0:T(8,128)(2,1)S(1)} collective-permute-done((bf16[256,512]{1,0:T(8,128)(2,1)S(1)}, bf16[256,512]{1,0:T(8,128)(2,1)S(1)}, u32[]{:S(2)}, u32[]{:S(2)}) %collective-permute-start.18) | collective-permute-done | bytes 262176 | tf_op jit(solution)/shard_map/ppermute | solution.py:315
  73.4 0.1 fusion.14
  73.5 0.9 %collective-permute-start.19 = (bf16[256,512]{1,0:T(8,128)(2,1)S(1)}, bf16[256,512]{1,0:T(8,128)(2,1)S(1)}, u32[]{:S(2)}, u32[]{:S(2)}) collective-permute-start(bf16[256,512]{1,0:T(8,128)(2,1)S(1)} %fusion.14), channel_id=1, source_target_pairs={{0,1},{1,0},{2,3},{3,2},{4,5},{5,4},{6,7},{7,6},{8,9},{9,8},{10,11... | collective-permute-start | bytes 786440 | tf_op jit(solution)/shard_map/ppermute | solution.py:306
  74.3 3.8 %collective-permute-done.16 = bf16[256,512]{1,0:T(8,128)(2,1)S(1)} collective-permute-done((bf16[256,512]{1,0:T(8,128)(2,1)S(1)}, bf16[256,512]{1,0:T(8,128)(2,1)S(1)}, u32[]{:S(2)}, u32[]{:S(2)}) %collective-permute-start.16) | collective-permute-done | bytes 262176 | tf_op jit(solution)/shard_map/ppermute | solution.py:315
  78.1 0.1 fusion.19
  78.2 1.9 %collective-permute-done.19 = bf16[256,512]{1,0:T(8,128)(2,1)S(1)} collective-permute-done((bf16[256,512]{1,0:T(8,128)(2,1)S(1)}, bf16[256,512]{1,0:T(8,128)(2,1)S(1)}, u32[]{:S(2)}, u32[]{:S(2)}) %collective-permute-start.19) | collective-permute-done | bytes 262176 | tf_op jit(solution)/shard_map/ppermute | solution.py:306
  80.1 0.9 %maximum_select_fusion.2 = bf16[128,2048]{1,0:T(8,128)(2,1)} fusion(bf16[128,512]{1,0:T(8,128)(2,1)S(1)} %get-tuple-element.89, bf16[128,512]{1,0:T(8,128)(2,1)S(1)} %get-tuple-element.87, bf16[128,512]{1,0:T(8,128)(2,1)S(1)} %get-tuple-element.85, bf16[128,512]{1,0:T(8,128)(2,1)S(1)} %get-tuple-element.83, pred[]{:T(512)S(6)} %eq.10), kind=kLoop, calls=%fused_computation.36 | loop fusion | flops 4456448 | bytes 1048577 | tf_op jit(solution)/shard_map/jit(_where)/select_n | solution.py:406
  81.1 0.9 %maximum_select_fusion.1 = bf16[128,2048]{1,0:T(8,128)(2,1)} fusion(bf16[128,512]{1,0:T(8,128)(2,1)S(1)} %get-tuple-element.90, bf16[128,512]{1,0:T(8,128)(2,1)S(1)} %get-tuple-element.88, bf16[128,512]{1,0:T(8,128)(2,1)S(1)} %get-tuple-element.86, bf16[128,512]{1,0:T(8,128)(2,1)S(1)} %get-tuple-element.84, pred[]{:T(512)S(6)} %eq.10), kind=kLoop, calls=%fused_computation.35 | loop fusion | flops 4456448 | bytes 1048577 | tf_op jit(solution)/shard_map/jit(_where)/select_n | solution.py:406
  (84 shorter events, 1.2 us)
Async XLA Ops:
  0.6 4.8 %copy-start.3 = (bf16[128,2048]{1,0:T(8,128)(2,1)S(1)}, bf16[128,2048]{1,0:T(8,128)(2,1)}, u32[]{:S(2)}) copy-start(bf16[128,2048]{1,0:T(8,128)(2,1)} %v_own.3) | copy-start | bytes 1572868
  0.6 4.8 %copy-start.2 = (bf16[128,2048]{1,0:T(8,128)(2,1)S(1)}, bf16[128,2048]{1,0:T(8,128)(2,1)}, u32[]{:S(2)}) copy-start(bf16[128,2048]{1,0:T(8,128)(2,1)} %k_own.3) | copy-start | bytes 1572868
  2.5 13.7 %collective-permute-start.1 = (bf16[256,512]{1,0:T(8,128)(2,1)}, bf16[256,512]{1,0:T(8,128)(2,1)}, u32[]{:S(2)}, u32[]{:S(2)}) collective-permute-start(bf16[256,512]{1,0:T(8,128)(2,1)} %pad_maximum_fusion.6), channel_id=1, source_target_pairs={{0,1},{1,0},{2,3},{3,2},{4,5},{5,4},{6,7},{7,6},{8,9},{9,8},{10,11... | collective-permute-start | bytes 786440 | tf_op jit(solution)/shard_map/ppermute | solution.py:306
  5.4 6.9 %copy-start = (bf16[128,4096]{1,0:T(8,128)(2,1)S(1)}, bf16[128,4096]{1,0:T(8,128)(2,1)}, u32[]{:S(2)}) copy-start(bf16[128,4096]{1,0:T(8,128)(2,1)} %q_own.3) | copy-start | bytes 3145732
  5.5 6.8 %copy-start.1 = (bf16[128,4096]{1,0:T(8,128)(2,1)S(1)}, bf16[128,4096]{1,0:T(8,128)(2,1)}, u32[]{:S(2)}) copy-start(bf16[128,4096]{1,0:T(8,128)(2,1)} %g_own.3) | copy-start | bytes 3145732
  6.2 12.7 %collective-permute-start.8 = (bf16[256,512]{1,0:T(8,128)(2,1)}, bf16[256,512]{1,0:T(8,128)(2,1)S(1)}, u32[]{:S(2)}, u32[]{:S(2)}) collective-permute-start(bf16[256,512]{1,0:T(8,128)(2,1)} %pad_maximum_fusion.7), channel_id=1, source_target_pairs={{0,1},{1,0},{2,3},{3,2},{4,5},{5,4},{6,7},{7,6},{8,9},{9,8},{10,11... | collective-permute-start | bytes 786440 | tf_op jit(solution)/shard_map/ppermute | solution.py:306
  6.3 0.7 copy-start.5
  7.6 14.8 %collective-permute-start.2 = (bf16[256,512]{1,0:T(8,128)(2,1)}, bf16[256,512]{1,0:T(8,128)(2,1)}, u32[]{:S(2)}, u32[]{:S(2)}) collective-permute-start(bf16[256,512]{1,0:T(8,128)(2,1)} %pad_maximum_fusion.8), channel_id=1, source_target_pairs={{0,4},{2,6},{4,8},{6,10},{8,12},{10,14},{12,16},{14,18},{16,20},{1... | collective-permute-start | bytes 786440 | tf_op jit(solution)/shard_map/ppermute | solution.py:315
  13.2 16.5 %collective-permute-start = (bf16[256,1024]{1,0:T(8,128)(2,1)}, bf16[256,1024]{1,0:T(8,128)(2,1)}, u32[]{:S(2)}, u32[]{:S(2)}) collective-permute-start(bf16[256,1024]{1,0:T(8,128)(2,1)} %pad_maximum_fusion), channel_id=1, source_target_pairs={{0,1},{1,0},{2,3},{3,2},{4,5},{5,4},{6,7},{7,6},{8,9},{9,8},{10,11... | collective-permute-start | bytes 1572872 | tf_op jit(solution)/shard_map/ppermute | solution.py:306
  15.6 6.9 %copy-start.6 = (bf16[128,512]{1,0:T(8,128)(2,1)S(1)}, bf16[128,512]{1,0:T(8,128)(2,1)}, u32[]{:S(2)}) copy-start(bf16[128,512]{1,0:T(8,128)(2,1)} %copy-done.5) | copy-start | bytes 393220
  15.6 24.6 %collective-permute-start.5 = (bf16[256,1024]{1,0:T(8,128)(2,1)}, bf16[256,1024]{1,0:T(8,128)(2,1)}, u32[]{:S(2)}, u32[]{:S(2)}) collective-permute-start(bf16[256,1024]{1,0:T(8,128)(2,1)} %pad_maximum_fusion.2), channel_id=1, source_target_pairs={{0,1},{1,0},{2,3},{3,2},{4,5},{5,4},{6,7},{7,6},{8,9},{9,8},{10,11... | collective-permute-start | bytes 1572872 | tf_op jit(solution)/shard_map/ppermute | solution.py:306
  16.2 9.8 %collective-permute-start.3 = (bf16[256,512]{1,0:T(8,128)(2,1)}, bf16[256,512]{1,0:T(8,128)(2,1)S(1)}, u32[]{:S(2)}, u32[]{:S(2)}) collective-permute-start(bf16[256,512]{1,0:T(8,128)(2,1)} %collective-permute-done.1.kv_other), channel_id=1, source_target_pairs={{0,4},{2,6},{4,8},{6,10},{8,12},{10,14},{12,16},{14,18},{16,20},{1... | collective-permute-start | bytes 786440 | tf_op jit(solution)/shard_map/ppermute | solution.py:315
  18.9 21.2 %copy-start.4 = (bf16[256,512]{1,0:T(8,128)(2,1)}, bf16[256,512]{1,0:T(8,128)(2,1)S(1)}, u32[]{:S(2)}) copy-start(bf16[256,512]{1,0:T(8,128)(2,1)S(1)} %collective-permute-done.8.kv_other) | copy-start | bytes 786436
  19.0 21.1 %collective-permute-start.9 = (bf16[512,512]{1,0:T(8,128)(2,1)S(1)}, bf16[512,512]{1,0:T(8,128)(2,1)S(1)}, u32[]{:S(2)}, u32[]{:S(2)}) collective-permute-start(bf16[512,512]{1,0:T(8,128)(2,1)S(1)} %pad_maximum_fusion.4), channel_id=1, source_target_pairs={{0,4},{2,6},{4,8},{6,10},{8,12},{10,14},{12,16},{14,18},{16,20},{1... | collective-permute-start | bytes 1572872 | tf_op jit(solution)/shard_map/ppermute | solution.py:315
  22.6 4.6 %copy-start.20 = (s32[2,6]{1,0:T(2,128)S(1)}, s32[2,6]{1,0:T(2,128)}, u32[]{:S(2)}) copy-start(s32[2,6]{1,0:T(2,128)} %param.11) | copy-start | bytes 148
  22.6 4.6 %copy-start.21 = (s32[2,6]{1,0:T(2,128)S(1)}, s32[2,6]{1,0:T(2,128)}, u32[]{:S(2)}) copy-start(s32[2,6]{1,0:T(2,128)} %param.10) | copy-start | bytes 148
  26.0 3.7 %copy-start.7 = (bf16[256,512]{1,0:T(8,128)(2,1)}, bf16[256,512]{1,0:T(8,128)(2,1)S(1)}, u32[]{:S(2)}) copy-start(bf16[256,512]{1,0:T(8,128)(2,1)S(1)} %collective-permute-done.3.kv2_other) | copy-start | bytes 786436
  27.1 2.6 %collective-permute-start.4 = (bf16[512,512]{1,0:T(8,128)(2,1)S(1)}, bf16[512,512]{1,0:T(8,128)(2,1)S(1)}, u32[]{:S(2)}, u32[]{:S(2)}) collective-permute-start(bf16[512,512]{1,0:T(8,128)(2,1)S(1)} %pad_maximum_fusion.1), channel_id=1, source_target_pairs={{0,2},{2,0},{4,6},{6,4},{8,10},{10,8},{12,14},{14,12},{16,18},{18,... | collective-permute-start | bytes 1572872 | tf_op jit(solution)/shard_map/ppermute | solution.py:310
  29.7 0.8 copy-start.13
  40.1 1.0 %copy-start.23 = (bf16[256,512]{1,0:T(8,128)(2,1)S(1)}, bf16[256,512]{1,0:T(8,128)(2,1)}, u32[]{:S(2)}) copy-start(bf16[256,512]{1,0:T(8,128)(2,1)} %get-tuple-element.57) | copy-start | bytes 786436
  40.1 1.7 %collective-permute-start.6 = (bf16[256,512]{1,0:T(8,128)(2,1)}, bf16[256,512]{1,0:T(8,128)(2,1)S(1)}, u32[]{:S(2)}, u32[]{:S(2)}) collective-permute-start(bf16[256,512]{1,0:T(8,128)(2,1)} %get-tuple-element.55), channel_id=1, source_target_pairs={{0,2},{2,0},{4,6},{6,4},{8,10},{10,8},{12,14},{14,12},{16,18},{18,... | collective-permute-start | bytes 786440 | tf_op jit(solution)/shard_map/ppermute | solution.py:310
  41.2 1.0 %copy-start.19 = (bf16[256,512]{1,0:T(8,128)(2,1)S(1)}, bf16[256,512]{1,0:T(8,128)(2,1)}, u32[]{:S(2)}) copy-start(bf16[256,512]{1,0:T(8,128)(2,1)} %get-tuple-element.50) | copy-start | bytes 786436
  41.2 1.7 %copy-start.17 = (bf16[256,512]{1,0:T(8,128)(2,1)S(1)}, bf16[256,512]{1,0:T(8,128)(2,1)}, u32[]{:S(2)}) copy-start(bf16[256,512]{1,0:T(8,128)(2,1)} %get-tuple-element.56) | copy-start | bytes 786436
  41.2 1.7 %collective-permute-start.7 = (bf16[256,512]{1,0:T(8,128)(2,1)S(1)}, bf16[256,512]{1,0:T(8,128)(2,1)S(1)}, u32[]{:S(2)}, u32[]{:S(2)}) collective-permute-start(bf16[256,512]{1,0:T(8,128)(2,1)S(1)} %copy-done.23), channel_id=1, source_target_pairs={{0,2},{2,0},{4,6},{6,4},{8,10},{10,8},{12,14},{14,12},{16,18},{18,... | collective-permute-start | bytes 786440 | tf_op jit(solution)/shard_map/ppermute | solution.py:310
  41.7 4.4 %collective-permute-start.10 = (bf16[512,512]{1,0:T(8,128)(2,1)S(1)}, bf16[512,512]{1,0:T(8,128)(2,1)S(1)}, u32[]{:S(2)}, u32[]{:S(2)}) collective-permute-start(bf16[512,512]{1,0:T(8,128)(2,1)S(1)} %pad_maximum_fusion.5), channel_id=1, source_target_pairs={{0,2},{2,0},{4,6},{6,4},{8,10},{10,8},{12,14},{14,12},{16,18},{18,... | collective-permute-start | bytes 1572872 | tf_op jit(solution)/shard_map/ppermute | solution.py:310
  42.2 2.1 %copy-start.22 = (bf16[128,1024]{1,0:T(8,128)(2,1)S(1)}, bf16[128,1024]{1,0:T(8,128)(2,1)}, u32[]{:S(2)}) copy-start(bf16[128,1024]{1,0:T(8,128)(2,1)} %get-tuple-element.62) | copy-start | bytes 786436
  43.0 16.1 %collective-permute-start.13 = (bf16[512,512]{1,0:T(8,128)(2,1)S(1)}, bf16[512,512]{1,0:T(8,128)(2,1)S(1)}, u32[]{:S(2)}, u32[]{:S(2)}) collective-permute-start(bf16[512,512]{1,0:T(8,128)(2,1)S(1)} %pad_maximum_fusion.3), channel_id=1, source_target_pairs={{4,0},{6,2},{8,4},{10,6},{12,8},{14,10},{16,12},{18,14},{20,16},{2... | collective-permute-start | bytes 1572872 | tf_op jit(solution)/shard_map/ppermute | solution.py:315
  44.3 20.3 %collective-permute-start.11 = (bf16[128,1024]{1,0:T(8,128)(2,1)S(1)}, bf16[128,1024]{1,0:T(8,128)(2,1)S(1)}, u32[]{:S(2)}, u32[]{:S(2)}) collective-permute-start(bf16[128,1024]{1,0:T(8,128)(2,1)S(1)} %copy-done.22), channel_id=1, source_target_pairs={{0,1},{1,0},{2,3},{3,2},{4,5},{5,4},{6,7},{7,6},{8,9},{9,8},{10,11... | collective-permute-start | bytes 786440 | tf_op jit(solution)/shard_map/ppermute | solution.py:306
  46.1 0.8 copy-start.12
  46.9 12.8 %copy-start.9 = (f32[256,512]{1,0:T(8,128)S(1)}, f32[256,512]{1,0:T(8,128)}, u32[]{:S(2)}) copy-start(f32[256,512]{1,0:T(8,128)} %get-tuple-element.74) | copy-start | bytes 1572868
  56.2 3.6 %copy-start.8 = (f32[256,512]{1,0:T(8,128)S(1)}, f32[256,512]{1,0:T(8,128)}, u32[]{:S(2)}) copy-start(f32[256,512]{1,0:T(8,128)} %get-tuple-element.76) | copy-start | bytes 1572868
  56.2 9.4 %collective-permute-start.12 = (bf16[128,1024]{1,0:T(8,128)(2,1)}, bf16[128,1024]{1,0:T(8,128)(2,1)S(1)}, u32[]{:S(2)}, u32[]{:S(2)}) collective-permute-start(bf16[128,1024]{1,0:T(8,128)(2,1)} %get-tuple-element.63), channel_id=1, source_target_pairs={{0,1},{1,0},{2,3},{3,2},{4,5},{5,4},{6,7},{7,6},{8,9},{9,8},{10,11... | collective-permute-start | bytes 786440 | tf_op jit(solution)/shard_map/ppermute | solution.py:306
  59.1 2.7 %collective-permute-start.14 = (bf16[256,512]{1,0:T(8,128)(2,1)}, bf16[256,512]{1,0:T(8,128)(2,1)S(1)}, u32[]{:S(2)}, u32[]{:S(2)}) collective-permute-start(bf16[256,512]{1,0:T(8,128)(2,1)} %get-tuple-element.67), channel_id=1, source_target_pairs={{0,2},{2,0},{4,6},{6,4},{8,10},{10,8},{12,14},{14,12},{16,18},{18,... | collective-permute-start | bytes 786440 | tf_op jit(solution)/shard_map/ppermute | solution.py:310
  59.2 4.0 %collective-permute-start.15 = (bf16[256,512]{1,0:T(8,128)(2,1)}, bf16[256,512]{1,0:T(8,128)(2,1)S(1)}, u32[]{:S(2)}, u32[]{:S(2)}) collective-permute-start(bf16[256,512]{1,0:T(8,128)(2,1)} %get-tuple-element.69), channel_id=1, source_target_pairs={{0,2},{2,0},{4,6},{6,4},{8,10},{10,8},{12,14},{14,12},{16,18},{18,... | collective-permute-start | bytes 786440 | tf_op jit(solution)/shard_map/ppermute | solution.py:310
  59.8 2.0 %copy-start.18 = (bf16[256,512]{1,0:T(8,128)(2,1)S(1)}, bf16[256,512]{1,0:T(8,128)(2,1)}, u32[]{:S(2)}) copy-start(bf16[256,512]{1,0:T(8,128)(2,1)} %get-tuple-element.64) | copy-start | bytes 786436
  59.8 3.4 %copy-start.16 = (bf16[256,512]{1,0:T(8,128)(2,1)S(1)}, bf16[256,512]{1,0:T(8,128)(2,1)}, u32[]{:S(2)}) copy-start(bf16[256,512]{1,0:T(8,128)(2,1)} %get-tuple-element.68) | copy-start | bytes 786436
  60.0 5.7 %copy-start.14 = (bf16[128,1024]{1,0:T(8,128)(2,1)S(1)}, bf16[128,1024]{1,0:T(8,128)(2,1)}, u32[]{:S(2)}) copy-start(bf16[128,1024]{1,0:T(8,128)(2,1)} %get-tuple-element.70) | copy-start | bytes 786436
  60.0 5.7 %copy-start.15 = (bf16[128,1024]{1,0:T(8,128)(2,1)S(1)}, bf16[128,1024]{1,0:T(8,128)(2,1)}, u32[]{:S(2)}) copy-start(bf16[128,1024]{1,0:T(8,128)(2,1)} %get-tuple-element.71) | copy-start | bytes 786436
  60.0 10.4 %collective-permute-start.17 = (bf16[256,512]{1,0:T(8,128)(2,1)S(1)}, bf16[256,512]{1,0:T(8,128)(2,1)S(1)}, u32[]{:S(2)}, u32[]{:S(2)}) collective-permute-start(bf16[256,512]{1,0:T(8,128)(2,1)S(1)} %fusion.9), channel_id=1, source_target_pairs={{0,1},{1,0},{2,3},{3,2},{4,5},{5,4},{6,7},{7,6},{8,9},{9,8},{10,11... | collective-permute-start | bytes 786440 | tf_op jit(solution)/shard_map/ppermute | solution.py:306
  61.9 11.5 %collective-permute-start.18 = (bf16[256,512]{1,0:T(8,128)(2,1)S(1)}, bf16[256,512]{1,0:T(8,128)(2,1)S(1)}, u32[]{:S(2)}, u32[]{:S(2)}) collective-permute-start(bf16[256,512]{1,0:T(8,128)(2,1)S(1)} %fusion.11), channel_id=1, source_target_pairs={{4,0},{6,2},{8,4},{10,6},{12,8},{14,10},{16,12},{18,14},{20,16},{2... | collective-permute-start | bytes 786440 | tf_op jit(solution)/shard_map/ppermute | solution.py:315
  63.3 14.8 %collective-permute-start.16 = (bf16[256,512]{1,0:T(8,128)(2,1)S(1)}, bf16[256,512]{1,0:T(8,128)(2,1)S(1)}, u32[]{:S(2)}, u32[]{:S(2)}) collective-permute-start(bf16[256,512]{1,0:T(8,128)(2,1)S(1)} %fusion.16), channel_id=1, source_target_pairs={{4,0},{6,2},{8,4},{10,6},{12,8},{14,10},{16,12},{18,14},{20,16},{2... | collective-permute-start | bytes 786440 | tf_op jit(solution)/shard_map/ppermute | solution.py:315
  65.7 7.7 %copy-start.11 = (f32[256,512]{1,0:T(8,128)S(1)}, f32[256,512]{1,0:T(8,128)}, u32[]{:S(2)}) copy-start(f32[256,512]{1,0:T(8,128)} %get-tuple-element.78) | copy-start | bytes 1572868
  66.9 11.2 %copy-start.10 = (f32[256,512]{1,0:T(8,128)S(1)}, f32[256,512]{1,0:T(8,128)}, u32[]{:S(2)}) copy-start(f32[256,512]{1,0:T(8,128)} %get-tuple-element.75) | copy-start | bytes 1572868
  73.5 6.6 %collective-permute-start.19 = (bf16[256,512]{1,0:T(8,128)(2,1)S(1)}, bf16[256,512]{1,0:T(8,128)(2,1)S(1)}, u32[]{:S(2)}, u32[]{:S(2)}) collective-permute-start(bf16[256,512]{1,0:T(8,128)(2,1)S(1)} %fusion.14), channel_id=1, source_target_pairs={{0,1},{1,0},{2,3},{3,2},{4,5},{5,4},{6,7},{7,6},{8,9},{9,8},{10,11... | collective-permute-start | bytes 786440 | tf_op jit(solution)/shard_map/ppermute | solution.py:306

commit v4 on v3

--- a/solution.py
+++ b/solution.py
@@ -355,6 +355,8 @@
     kv2_other.append(late[2 * n :])
 
     def attended(c, *earlier):
+        if earlier:
+            kv2_own[c], kv2_other[c] = after([kv2_own[c], kv2_other[c]], e1_own, e1_other)
         kv1 = mate(
             jnp.concatenate(
                 [
@@ -388,14 +390,15 @@
     back_own0, back_other0 = back0[: 2 * n], back0[2 * n :]
 
     dq_own1, dq_away1, d0_own, d0_other, d1_own, d1_other, d2_own, d2_other = attended(1, *ship0)
-    d1_own, d1_other, back_other0 = after([d1_own, d1_other, back_other0])
     dq_other1 = swap(dq_away1)
     d1_other = mate(d1_other)
     d1_own = mate(d1_own)
+    d1_other, back_other0 = after([d1_other, back_other0])
     ship_other = back_sum(d2_other, d1_other)
     back_other = moved(ship_other, -2)
     ship_own = back_sum(d2_own, d1_own)
     back_own = moved(ship_own, -2)
+    (back_other0,) = after([back_other0], ship_other)
     other0 = swap(here_sum(e0_other, e1_other, back_other0))
     other1 = swap(here_sum(d0_other, d1_other, back_other))
     own0 = here_sum(e0_own, e1_own, back_own0)
@@ -413,10 +416,15 @@
         [dq_own0, dq_own1, dq_other0, dq_other1], ship_other, ship_own
     )
     grad_queries = placed([dq_own0, dq_own1], [dq_other0, dq_other1])
+    blank = jnp.zeros_like(own1[:n])
+    grad_keys = placed([own0[:n], own1[:n]], [other0[:n], blank])
+    grad_values = placed([own0[n:], own1[n:]], [other0[n:], blank])
+    grad_keys, grad_values, other1 = after([grad_keys, grad_values, other1])
+    last = ((1 - side) * half + firsts[1]) * d
     return (
         grad_queries,
-        placed([own0[:n], own1[:n]], [other0[:n], other1[:n]]),
-        placed([own0[n:], own1[n:]], [other0[n:], other1[n:]]),
+        lax.dynamic_update_slice_in_dim(grad_keys, other1[:n], last, 1),
+        lax.dynamic_update_slice_in_dim(grad_values, other1[n:], last, 1),
     )
 
 

time: 82.4 us -> 80.1 us (0.972)
  other arithmetic: 10.6 us -> 7.37 us
  waiting for transfers between devices: 22.1 us -> 19.6 us
  local copies, waits for them, and re-layouts: 3.91 us -> 6.08 us
  starting transfers between devices: 25.8 us -> 27.1 us
    ppermute x8, waiting for transfers between devices: 8.76 us -> 6.37 us  [swap(): return lax.ppermute(block, 'space', [(0, 1), (1, 0)])]
    unnamed x48 -> x54, local copies, waits for them, and re-layouts: 2.56 us -> 4.67 us
    select_n x3 -> x2, other arithmetic: 3.07 us -> 1.49 us  [placed(): jnp.where(side == 0, jnp.concatenate([own, other], axis=1), jnp.concatena...]
    ppermute x6, waiting for transfers between devices: 12.6 us -> 11.6 us  [moved(): lax.ppermute(block, 'tm', [(i, i + distance) for i in range(size) if 0 <=...]
    select_n x2, other arithmetic: 1.09 us -> 0.14 us  [attended(): jnp.where(odd, kv2_own[c], kv_own[c])]
    ppermute x6, waiting for transfers between devices: 0.72 us -> 1.56 us  [mate(): lax.ppermute(block, 'tm', [(i, i ^ 1) for i in range(lax.axis_size('tm'))])]
  transfers between devices with their start and end apart: 20 -> 20, of which waited for: 11 -> 11; matrix products, arithmetic and copies ran while one was open for 10% -> 9% of each run, Pallas kernels for 23% -> 23%
where the time goes in v4:
time: 80.1 us; the launch traced here: 79.7 us
  starting transfers between devices  27.1 us (34%)
  waiting for transfers between devices  19.6 us (24%)
  Pallas kernels  18.3 us (23%)
  other arithmetic  7.37 us (9%)
  local copies, waits for them, and re-layouts  6.08 us (8%)
  between operations  1.24 us (2%)
    pallas_call x2, Pallas kernels, attend(): pl.pallas_call(attend_kernel, grid_spec=pltpu.PrefetchScalarGridSpec(num_...  18.3 us
    ppermute x6, starting transfers between devices, moved(): lax.ppermute(block, 'tm', [(i, i + distance) for i in range(size) if 0 <=...  15.3 us
    ppermute x6, waiting for transfers between devices, moved(): lax.ppermute(block, 'tm', [(i, i + distance) for i in range(size) if 0 <=...  11.6 us
    ppermute x8, starting transfers between devices, swap(): return lax.ppermute(block, 'space', [(0, 1), (1, 0)])  10.5 us
    ppermute x8, waiting for transfers between devices, swap(): return lax.ppermute(block, 'space', [(0, 1), (1, 0)])  6.37 us
    unnamed x54, local copies, waits for them, and re-layouts  4.67 us
    concatenate x5, other arithmetic, packed(): jnp.concatenate([lax.dynamic_slice_in_dim(a, start, width, 1) for a in ar...  3.03 us
  transfers between devices with their start and end apart: 20, of which 11 were waited for; matrix products, arithmetic and copies ran while one was open for 9% of the time, Pallas kernels for 23%

profile of v4, /device:TPU:0, one launch (start us, length us, event | category | flops | bytes accessed | tf_op | source)
XLA Modules:
  0.0 79.7 jit_solution(12519464810829643394)
XLA Ops:
  0.7 1.1 %constant_dynamic-slice_fusion.10 = (bf16[128,512]{1,0:T(8,128)(2,1)S(1)}, bf16[128,512]{1,0:T(8,128)(2,1)S(1)}) fusion(bf16[128,2048]{1,0:T(8,128)(2,1)} %v_own.3, s32[]{:T(128)S(6)} %select_n.112, bf16[128,2048]{1,0:T(8,128)(2,1)} %k_own.3), kind=kLoop, calls=%fused_computation.64 | loop fusion | bytes 524292 | tf_op jit(solution)/shard_map/dynamic_slice | solution.py:142
  1.7 0.7 pad_maximum_fusion.10
  2.5 2.9 %collective-permute-start.1 = (bf16[256,512]{1,0:T(8,128)(2,1)}, bf16[256,512]{1,0:T(8,128)(2,1)}, u32[]{:S(2)}, u32[]{:S(2)}) collective-permute-start(bf16[256,512]{1,0:T(8,128)(2,1)} %pad_maximum_fusion.10), channel_id=1, source_target_pairs={{0,1},{1,0},{2,3},{3,2},{4,5},{5,4},{6,7},{7,6},{8,9},{9,8},{10,11... | collective-permute-start | bytes 786440 | tf_op jit(solution)/shard_map/ppermute | solution.py:306
  5.5 0.7 pad_maximum_fusion.11
  6.2 0.7 copy-done.7
  6.9 0.7 pad_maximum_fusion.12
  7.6 4.7 %collective-permute-start.2 = (bf16[256,512]{1,0:T(8,128)(2,1)}, bf16[256,512]{1,0:T(8,128)(2,1)}, u32[]{:S(2)}, u32[]{:S(2)}) collective-permute-start(bf16[256,512]{1,0:T(8,128)(2,1)} %pad_maximum_fusion.12), channel_id=1, source_target_pairs={{0,4},{2,6},{4,8},{6,10},{8,12},{10,14},{12,16},{14,18},{16,20},{1... | collective-permute-start | bytes 786440 | tf_op jit(solution)/shard_map/ppermute | solution.py:315
  12.3 0.8 %pad_maximum_fusion.4 = bf16[256,1024]{1,0:T(8,128)(2,1)} fusion(bf16[128,1024]{1,0:T(8,128)(2,1)S(1)} %constant_dynamic-slice_fusion.4, bf16[128,1024]{1,0:T(8,128)(2,1)S(1)} %constant_dynamic-slice_fusion.5), kind=kLoop, calls=%fused_computation.39 | loop fusion | flops 1048576 | bytes 1048576 | tf_op jit(solution)/shard_map/concatenate | solution.py:142
  13.2 1.5 %collective-permute-start = (bf16[256,1024]{1,0:T(8,128)(2,1)}, bf16[256,1024]{1,0:T(8,128)(2,1)}, u32[]{:S(2)}, u32[]{:S(2)}) collective-permute-start(bf16[256,1024]{1,0:T(8,128)(2,1)} %pad_maximum_fusion.4), channel_id=1, source_target_pairs={{0,1},{1,0},{2,3},{3,2},{4,5},{5,4},{6,7},{7,6},{8,9},{9,8},{10,11... | collective-permute-start | bytes 1572872 | tf_op jit(solution)/shard_map/ppermute | solution.py:306
  14.8 0.6 collective-permute-start.5
  15.5 2.8 %collective-permute-start.3 = (bf16[256,512]{1,0:T(8,128)(2,1)}, bf16[256,512]{1,0:T(8,128)(2,1)S(1)}, u32[]{:S(2)}, u32[]{:S(2)}) collective-permute-start(bf16[256,512]{1,0:T(8,128)(2,1)} %collective-permute-done.1.kv_other), channel_id=1, source_target_pairs={{0,4},{2,6},{4,8},{6,10},{8,12},{10,14},{12,16},{14,18},{16,20},{1... | collective-permute-start | bytes 786440 | tf_op jit(solution)/shard_map/ppermute | solution.py:315
  18.2 0.1 collective-permute-done.8.kv_other
  18.4 4.0 %collective-permute-start.9 = (bf16[512,512]{1,0:T(8,128)(2,1)S(1)}, bf16[512,512]{1,0:T(8,128)(2,1)S(1)}, u32[]{:S(2)}, u32[]{:S(2)}) collective-permute-start(bf16[512,512]{1,0:T(8,128)(2,1)S(1)} %pad_maximum_fusion.8), channel_id=1, source_target_pairs={{0,4},{2,6},{4,8},{6,10},{8,12},{10,14},{12,16},{14,18},{16,20},{1... | collective-permute-start | bytes 1572872 | tf_op jit(solution)/shard_map/ppermute | solution.py:315
  22.6 2.2 %collective-permute-done.3.kv2_other = bf16[256,512]{1,0:T(8,128)(2,1)S(1)} collective-permute-done((bf16[256,512]{1,0:T(8,128)(2,1)}, bf16[256,512]{1,0:T(8,128)(2,1)S(1)}, u32[]{:S(2)}, u32[]{:S(2)}) %collective-permute-start.3) | collective-permute-done | bytes 262176 | tf_op jit(solution)/shard_map/ppermute | solution.py:315
  24.8 1.1 %broadcast_select_fusion.1 = bf16[256,512]{1,0:T(8,128)(2,1)S(1)} fusion(bf16[256,512]{1,0:T(8,128)(2,1)S(1)} %collective-permute-done.3.kv2_other, bf16[256,512]{1,0:T(8,128)(2,1)} %collective-permute-done.1.kv_other, pred[]{:T(512)S(6)} %eq.11), kind=kLoop, calls=%fused_computation.50 | loop fusion | flops 131072 | bytes 786433 | tf_op jit(solution)/shard_map/jit(_where)/select_n | solution.py:364
  26.0 0.6 pad_add_fusion.code_ref
  26.7 3.0 %collective-permute-done.qg_other = bf16[256,1024]{1,0:T(8,128)(2,1)} collective-permute-done((bf16[256,1024]{1,0:T(8,128)(2,1)}, bf16[256,1024]{1,0:T(8,128)(2,1)}, u32[]{:S(2)}, u32[]{:S(2)}) %collective-permute-start) | collective-permute-done | bytes 524320 | tf_op jit(solution)/shard_map/ppermute | solution.py:306
  29.7 0.8 copy-done.17
  30.5 9.2 %shard_map.85 = (bf16[128,1024]{1,0:T(8,128)(2,1)}, bf16[128,1024]{1,0:T(8,128)(2,1)}, f32[256,512]{1,0:T(8,128)}, f32[256,512]{1,0:T(8,128)}, bf16[256,512]{1,0...) custom-call(s32[1]{0:T(128)} %bitcast.side_ref, ...), custom_call_target="tpu_custom_call" | custom-call | tf_op jit(solution)/shard_map/pallas_call | solution.py:281
  39.7 0.4 collective-permute-done.5.qg_other
  40.1 0.5 collective-permute-start.7
  40.7 1.2 %collective-permute-done.6 = bf16[256,512]{1,0:T(8,128)(2,1)S(1)} collective-permute-done((bf16[256,512]{1,0:T(8,128)(2,1)}, bf16[256,512]{1,0:T(8,128)(2,1)S(1)}, u32[]{:S(2)}, u32[]{:S(2)}) %collective-permute-start.6) | collective-permute-done | bytes 262176 | tf_op jit(solution)/shard_map/ppermute | solution.py:310
  41.9 0.4 collective-permute-done.7
  42.4 0.2 collective-permute-start.10
  42.6 0.6 copy-done.22
  43.5 1.3 %collective-permute-start.14 = (bf16[512,512]{1,0:T(8,128)(2,1)S(1)}, bf16[512,512]{1,0:T(8,128)(2,1)S(1)}, u32[]{:S(2)}, u32[]{:S(2)}) collective-permute-start(bf16[512,512]{1,0:T(8,128)(2,1)S(1)} %pad_maximum_fusion.7), channel_id=1, source_target_pairs={{4,0},{6,2},{8,4},{10,6},{12,8},{14,10},{16,12},{18,14},{20,16},{2... | collective-permute-start | bytes 1572872 | tf_op jit(solution)/shard_map/ppermute | solution.py:315
  44.8 1.8 %collective-permute-start.11 = (bf16[128,1024]{1,0:T(8,128)(2,1)S(1)}, bf16[128,1024]{1,0:T(8,128)(2,1)S(1)}, u32[]{:S(2)}, u32[]{:S(2)}) collective-permute-start(bf16[128,1024]{1,0:T(8,128)(2,1)S(1)} %copy-done.26), channel_id=1, source_target_pairs={{0,1},{1,0},{2,3},{3,2},{4,5},{5,4},{6,7},{7,6},{8,9},{9,8},{10,11... | collective-permute-start | bytes 786440 | tf_op jit(solution)/shard_map/ppermute | solution.py:306
  46.6 0.8 copy-done.16
  47.4 9.2 %shard_map.86 = (bf16[128,1024]{1,0:T(8,128)(2,1)}, bf16[128,1024]{1,0:T(8,128)(2,1)}, f32[256,512]{1,0:T(8,128)}, f32[256,512]{1,0:T(8,128)}, bf16[256,512]{1,0...) custom-call(s32[1]{0:T(128)} %bitcast.side_ref, ...), custom_call_target="tpu_custom_call" | custom-call | tf_op jit(solution)/shard_map/pallas_call | solution.py:281
  56.6 0.3 collective-permute-start.12
  57.0 0.5 collective-permute-start.15
  57.5 1.9 %collective-permute-done.14 = bf16[512,512]{1,0:T(8,128)(2,1)S(1)} collective-permute-done((bf16[512,512]{1,0:T(8,128)(2,1)S(1)}, bf16[512,512]{1,0:T(8,128)(2,1)S(1)}, u32[]{:S(2)}, u32[]{:S(2)}) %collective-permute-start.14) | collective-permute-done | bytes 524320 | tf_op jit(solution)/shard_map/ppermute | solution.py:315
  59.6 0.8 copy-done.23
  60.4 1.3 %collective-permute-start.18 = (bf16[256,512]{1,0:T(8,128)(2,1)S(1)}, bf16[256,512]{1,0:T(8,128)(2,1)S(1)}, u32[]{:S(2)}, u32[]{:S(2)}) collective-permute-start(bf16[256,512]{1,0:T(8,128)(2,1)S(1)} %fusion.11), channel_id=1, source_target_pairs={{4,0},{6,2},{8,4},{10,6},{12,8},{14,10},{16,12},{18,14},{20,16},{2... | collective-permute-start | bytes 786440 | tf_op jit(solution)/shard_map/ppermute | solution.py:315
  61.8 0.1 fusion.9
  61.9 1.8 %collective-permute-start.17 = (bf16[256,512]{1,0:T(8,128)(2,1)S(1)}, bf16[256,512]{1,0:T(8,128)(2,1)S(1)}, u32[]{:S(2)}, u32[]{:S(2)}) collective-permute-start(bf16[256,512]{1,0:T(8,128)(2,1)S(1)} %fusion.9), channel_id=1, source_target_pairs={{0,1},{1,0},{2,3},{3,2},{4,5},{5,4},{6,7},{7,6},{8,9},{9,8},{10,11... | collective-permute-start | bytes 786440 | tf_op jit(solution)/shard_map/ppermute | solution.py:306
  63.8 1.3 %collective-permute-start.16 = (bf16[256,512]{1,0:T(8,128)(2,1)S(1)}, bf16[256,512]{1,0:T(8,128)(2,1)S(1)}, u32[]{:S(2)}, u32[]{:S(2)}) collective-permute-start(bf16[256,512]{1,0:T(8,128)(2,1)S(1)} %fusion.16), channel_id=1, source_target_pairs={{4,0},{6,2},{8,4},{10,6},{12,8},{14,10},{16,12},{18,14},{20,16},{2... | collective-permute-start | bytes 786440 | tf_op jit(solution)/shard_map/ppermute | solution.py:315
  65.1 0.9 %collective-permute-done.12 = bf16[128,1024]{1,0:T(8,128)(2,1)S(1)} collective-permute-done((bf16[128,1024]{1,0:T(8,128)(2,1)}, bf16[128,1024]{1,0:T(8,128)(2,1)S(1)}, u32[]{:S(2)}, u32[]{:S(2)}) %collective-permute-start.12) | collective-permute-done | bytes 262176 | tf_op jit(solution)/shard_map/ppermute | solution.py:306
  66.0 1.2 %maximum_select_fusion = bf16[128,4096]{1,0:T(8,128)(2,1)} fusion(bf16[128,1024]{1,0:T(8,128)(2,1)S(1)} %collective-permute-done.12, bf16[128,1024]{1,0:T(8,128)(2,1)S(1)} %collective-permute-done.11, bf16[128,1024]{1,0:T(8,128)(2,1)S(1)} %copy-done.19, bf16[128,1024]{1,0:T(8,128)(2,1)S(1)} %copy-done.18, pred[]{:T(512)S(6)} %eq.10), kind=kLoop, calls=%fused_computation | loop fusion | flops 8912896 | bytes 2097153 | tf_op jit(solution)/shard_map/jit(_where)/select_n | solution.py:409
  67.2 5.0 %collective-permute-done.18 = bf16[256,512]{1,0:T(8,128)(2,1)S(1)} collective-permute-done((bf16[256,512]{1,0:T(8,128)(2,1)S(1)}, bf16[256,512]{1,0:T(8,128)(2,1)S(1)}, u32[]{:S(2)}, u32[]{:S(2)}) %collective-permute-start.18) | collective-permute-done | bytes 262176 | tf_op jit(solution)/shard_map/ppermute | solution.py:315
  72.2 0.1 fusion.14
  72.3 1.6 %collective-permute-start.19 = (bf16[256,512]{1,0:T(8,128)(2,1)S(1)}, bf16[256,512]{1,0:T(8,128)(2,1)S(1)}, u32[]{:S(2)}, u32[]{:S(2)}) collective-permute-start(bf16[256,512]{1,0:T(8,128)(2,1)S(1)} %fusion.14), channel_id=1, source_target_pairs={{0,1},{1,0},{2,3},{3,2},{4,5},{5,4},{6,7},{7,6},{8,9},{9,8},{10,11... | collective-permute-start | bytes 786440 | tf_op jit(solution)/shard_map/ppermute | solution.py:306
  73.9 2.5 %collective-permute-done.16 = bf16[256,512]{1,0:T(8,128)(2,1)S(1)} collective-permute-done((bf16[256,512]{1,0:T(8,128)(2,1)S(1)}, bf16[256,512]{1,0:T(8,128)(2,1)S(1)}, u32[]{:S(2)}, u32[]{:S(2)}) %collective-permute-start.16) | collective-permute-done | bytes 262176 | tf_op jit(solution)/shard_map/ppermute | solution.py:315
  76.4 0.1 fusion.19
  76.6 0.3 fusion.25
  76.8 1.9 %collective-permute-done.19 = bf16[256,512]{1,0:T(8,128)(2,1)S(1)} collective-permute-done((bf16[256,512]{1,0:T(8,128)(2,1)S(1)}, bf16[256,512]{1,0:T(8,128)(2,1)S(1)}, u32[]{:S(2)}, u32[]{:S(2)}) %collective-permute-start.19) | collective-permute-done | bytes 262176 | tf_op jit(solution)/shard_map/ppermute | solution.py:306
  78.8 0.8 copy-done.14
  79.6 0.2 copy-done.15
  (92 shorter events, 1.3 us)
Async XLA Ops:
  0.6 4.8 %copy-start.3 = (bf16[128,2048]{1,0:T(8,128)(2,1)S(1)}, bf16[128,2048]{1,0:T(8,128)(2,1)}, u32[]{:S(2)}) copy-start(bf16[128,2048]{1,0:T(8,128)(2,1)} %v_own.3) | copy-start | bytes 1572868
  0.6 4.8 %copy-start.2 = (bf16[128,2048]{1,0:T(8,128)(2,1)S(1)}, bf16[128,2048]{1,0:T(8,128)(2,1)}, u32[]{:S(2)}) copy-start(bf16[128,2048]{1,0:T(8,128)(2,1)} %k_own.3) | copy-start | bytes 1572868
  2.5 13.0 %collective-permute-start.1 = (bf16[256,512]{1,0:T(8,128)(2,1)}, bf16[256,512]{1,0:T(8,128)(2,1)}, u32[]{:S(2)}, u32[]{:S(2)}) collective-permute-start(bf16[256,512]{1,0:T(8,128)(2,1)} %pad_maximum_fusion.10), channel_id=1, source_target_pairs={{0,1},{1,0},{2,3},{3,2},{4,5},{5,4},{6,7},{7,6},{8,9},{9,8},{10,11... | collective-permute-start | bytes 786440 | tf_op jit(solution)/shard_map/ppermute | solution.py:306
  5.4 6.9 %copy-start = (bf16[128,4096]{1,0:T(8,128)(2,1)S(1)}, bf16[128,4096]{1,0:T(8,128)(2,1)}, u32[]{:S(2)}) copy-start(bf16[128,4096]{1,0:T(8,128)(2,1)} %q_own.3) | copy-start | bytes 3145732
  5.5 6.9 %copy-start.1 = (bf16[128,4096]{1,0:T(8,128)(2,1)S(1)}, bf16[128,4096]{1,0:T(8,128)(2,1)}, u32[]{:S(2)}) copy-start(bf16[128,4096]{1,0:T(8,128)(2,1)} %g_own.3) | copy-start | bytes 3145732
  6.2 12.2 %collective-permute-start.8 = (bf16[256,512]{1,0:T(8,128)(2,1)}, bf16[256,512]{1,0:T(8,128)(2,1)S(1)}, u32[]{:S(2)}, u32[]{:S(2)}) collective-permute-start(bf16[256,512]{1,0:T(8,128)(2,1)} %pad_maximum_fusion.11), channel_id=1, source_target_pairs={{0,1},{1,0},{2,3},{3,2},{4,5},{5,4},{6,7},{7,6},{8,9},{9,8},{10,11... | collective-permute-start | bytes 786440 | tf_op jit(solution)/shard_map/ppermute | solution.py:306
  6.2 0.7 copy-start.7
  7.6 14.8 %collective-permute-start.2 = (bf16[256,512]{1,0:T(8,128)(2,1)}, bf16[256,512]{1,0:T(8,128)(2,1)}, u32[]{:S(2)}, u32[]{:S(2)}) collective-permute-start(bf16[256,512]{1,0:T(8,128)(2,1)} %pad_maximum_fusion.12), channel_id=1, source_target_pairs={{0,4},{2,6},{4,8},{6,10},{8,12},{10,14},{12,16},{14,18},{16,20},{1... | collective-permute-start | bytes 786440 | tf_op jit(solution)/shard_map/ppermute | solution.py:315
  13.2 16.5 %collective-permute-start = (bf16[256,1024]{1,0:T(8,128)(2,1)}, bf16[256,1024]{1,0:T(8,128)(2,1)}, u32[]{:S(2)}, u32[]{:S(2)}) collective-permute-start(bf16[256,1024]{1,0:T(8,128)(2,1)} %pad_maximum_fusion.4), channel_id=1, source_target_pairs={{0,1},{1,0},{2,3},{3,2},{4,5},{5,4},{6,7},{7,6},{8,9},{9,8},{10,11... | collective-permute-start | bytes 1572872 | tf_op jit(solution)/shard_map/ppermute | solution.py:306
  14.8 7.7 %copy-start.8 = (bf16[128,512]{1,0:T(8,128)(2,1)S(1)}, bf16[128,512]{1,0:T(8,128)(2,1)}, u32[]{:S(2)}) copy-start(bf16[128,512]{1,0:T(8,128)(2,1)} %copy-done.7) | copy-start | bytes 393220
  14.8 25.3 %collective-permute-start.5 = (bf16[256,1024]{1,0:T(8,128)(2,1)S(1)}, bf16[256,1024]{1,0:T(8,128)(2,1)}, u32[]{:S(2)}, u32[]{:S(2)}) collective-permute-start(bf16[256,1024]{1,0:T(8,128)(2,1)S(1)} %pad_maximum_fusion.6), channel_id=1, source_target_pairs={{0,1},{1,0},{2,3},{3,2},{4,5},{5,4},{6,7},{7,6},{8,9},{9,8},{10,11... | collective-permute-start | bytes 1572872 | tf_op jit(solution)/shard_map/ppermute | solution.py:306
  15.5 9.3 %collective-permute-start.3 = (bf16[256,512]{1,0:T(8,128)(2,1)}, bf16[256,512]{1,0:T(8,128)(2,1)S(1)}, u32[]{:S(2)}, u32[]{:S(2)}) collective-permute-start(bf16[256,512]{1,0:T(8,128)(2,1)} %collective-permute-done.1.kv_other), channel_id=1, source_target_pairs={{0,4},{2,6},{4,8},{6,10},{8,12},{10,14},{12,16},{14,18},{16,20},{1... | collective-permute-start | bytes 786440 | tf_op jit(solution)/shard_map/ppermute | solution.py:315
  18.4 23.9 %copy-start.4 = (bf16[256,512]{1,0:T(8,128)(2,1)}, bf16[256,512]{1,0:T(8,128)(2,1)S(1)}, u32[]{:S(2)}) copy-start(bf16[256,512]{1,0:T(8,128)(2,1)S(1)} %collective-permute-done.8.kv_other) | copy-start | bytes 786436
  18.4 22.2 %collective-permute-start.9 = (bf16[512,512]{1,0:T(8,128)(2,1)S(1)}, bf16[512,512]{1,0:T(8,128)(2,1)S(1)}, u32[]{:S(2)}, u32[]{:S(2)}) collective-permute-start(bf16[512,512]{1,0:T(8,128)(2,1)S(1)} %pad_maximum_fusion.8), channel_id=1, source_target_pairs={{0,4},{2,6},{4,8},{6,10},{8,12},{10,14},{12,16},{14,18},{16,20},{1... | collective-permute-start | bytes 1572872 | tf_op jit(solution)/shard_map/ppermute | solution.py:315
  22.5 3.5 %copy-start.24 = (s32[2,6]{1,0:T(2,128)S(1)}, s32[2,6]{1,0:T(2,128)}, u32[]{:S(2)}) copy-start(s32[2,6]{1,0:T(2,128)} %param.11) | copy-start | bytes 148
  22.5 3.5 %copy-start.25 = (s32[2,6]{1,0:T(2,128)S(1)}, s32[2,6]{1,0:T(2,128)}, u32[]{:S(2)}) copy-start(s32[2,6]{1,0:T(2,128)} %param.10) | copy-start | bytes 148
  24.8 4.9 %copy-start.9 = (bf16[256,512]{1,0:T(8,128)(2,1)}, bf16[256,512]{1,0:T(8,128)(2,1)S(1)}, u32[]{:S(2)}) copy-start(bf16[256,512]{1,0:T(8,128)(2,1)S(1)} %collective-permute-done.3.kv2_other) | copy-start | bytes 786436
  25.9 3.8 %collective-permute-start.4 = (bf16[512,512]{1,0:T(8,128)(2,1)S(1)}, bf16[512,512]{1,0:T(8,128)(2,1)S(1)}, u32[]{:S(2)}, u32[]{:S(2)}) collective-permute-start(bf16[512,512]{1,0:T(8,128)(2,1)S(1)} %pad_maximum_fusion.5), channel_id=1, source_target_pairs={{0,2},{2,0},{4,6},{6,4},{8,10},{10,8},{12,14},{14,12},{16,18},{18,... | collective-permute-start | bytes 1572872 | tf_op jit(solution)/shard_map/ppermute | solution.py:310
  29.7 0.8 copy-start.17
  40.1 1.7 %collective-permute-start.6 = (bf16[256,512]{1,0:T(8,128)(2,1)}, bf16[256,512]{1,0:T(8,128)(2,1)S(1)}, u32[]{:S(2)}, u32[]{:S(2)}) collective-permute-start(bf16[256,512]{1,0:T(8,128)(2,1)} %get-tuple-element.60), channel_id=1, source_target_pairs={{0,2},{2,0},{4,6},{6,4},{8,10},{10,8},{12,14},{14,12},{16,18},{18,... | collective-permute-start | bytes 786440 | tf_op jit(solution)/shard_map/ppermute | solution.py:310
  40.1 2.1 %collective-permute-start.7 = (bf16[256,512]{1,0:T(8,128)(2,1)}, bf16[256,512]{1,0:T(8,128)(2,1)S(1)}, u32[]{:S(2)}, u32[]{:S(2)}) collective-permute-start(bf16[256,512]{1,0:T(8,128)(2,1)} %get-tuple-element.62), channel_id=1, source_target_pairs={{0,2},{2,0},{4,6},{6,4},{8,10},{10,8},{12,14},{14,12},{16,18},{18,... | collective-permute-start | bytes 786440 | tf_op jit(solution)/shard_map/ppermute | solution.py:310
  40.7 1.8 %copy-start.5 = (bf16[256,512]{1,0:T(8,128)(2,1)}, bf16[256,512]{1,0:T(8,128)(2,1)S(1)}, u32[]{:S(2)}) copy-start(bf16[256,512]{1,0:T(8,128)(2,1)S(1)} %get-tuple-element.67.kv2_other) | copy-start | bytes 786436
  40.7 1.8 %copy-start.6 = (bf16[256,512]{1,0:T(8,128)(2,1)}, bf16[256,512]{1,0:T(8,128)(2,1)S(1)}, u32[]{:S(2)}) copy-start(bf16[256,512]{1,0:T(8,128)(2,1)S(1)} %get-tuple-element.66.kv2_own) | copy-start | bytes 786436
  42.3 1.0 %copy-start.22 = (bf16[256,512]{1,0:T(8,128)(2,1)S(1)}, bf16[256,512]{1,0:T(8,128)(2,1)}, u32[]{:S(2)}) copy-start(bf16[256,512]{1,0:T(8,128)(2,1)} %get-tuple-element.55) | copy-start | bytes 786436
  42.4 1.0 %copy-start.21 = (bf16[256,512]{1,0:T(8,128)(2,1)S(1)}, bf16[256,512]{1,0:T(8,128)(2,1)}, u32[]{:S(2)}) copy-start(bf16[256,512]{1,0:T(8,128)(2,1)} %get-tuple-element.61) | copy-start | bytes 786436
  42.4 4.2 %collective-permute-start.10 = (bf16[512,512]{1,0:T(8,128)(2,1)S(1)}, bf16[512,512]{1,0:T(8,128)(2,1)S(1)}, u32[]{:S(2)}, u32[]{:S(2)}) collective-permute-start(bf16[512,512]{1,0:T(8,128)(2,1)S(1)} %pad_maximum_fusion.9), channel_id=1, source_target_pairs={{0,2},{2,0},{4,6},{6,4},{8,10},{10,8},{12,14},{14,12},{16,18},{18,... | collective-permute-start | bytes 1572872 | tf_op jit(solution)/shard_map/ppermute | solution.py:310
  43.3 1.5 %copy-start.26 = (bf16[128,1024]{1,0:T(8,128)(2,1)S(1)}, bf16[128,1024]{1,0:T(8,128)(2,1)}, u32[]{:S(2)}) copy-start(bf16[128,1024]{1,0:T(8,128)(2,1)} %get-tuple-element.69) | copy-start | bytes 786436
  43.5 15.9 %collective-permute-start.14 = (bf16[512,512]{1,0:T(8,128)(2,1)S(1)}, bf16[512,512]{1,0:T(8,128)(2,1)S(1)}, u32[]{:S(2)}, u32[]{:S(2)}) collective-permute-start(bf16[512,512]{1,0:T(8,128)(2,1)S(1)} %pad_maximum_fusion.7), channel_id=1, source_target_pairs={{4,0},{6,2},{8,4},{10,6},{12,8},{14,10},{16,12},{18,14},{20,16},{2... | collective-permute-start | bytes 1572872 | tf_op jit(solution)/shard_map/ppermute | solution.py:315
  44.8 14.6 %copy-start.11 = (f32[256,512]{1,0:T(8,128)S(1)}, f32[256,512]{1,0:T(8,128)}, u32[]{:S(2)}) copy-start(f32[256,512]{1,0:T(8,128)} %get-tuple-element.80) | copy-start | bytes 1572868
  44.8 20.2 %collective-permute-start.11 = (bf16[128,1024]{1,0:T(8,128)(2,1)S(1)}, bf16[128,1024]{1,0:T(8,128)(2,1)S(1)}, u32[]{:S(2)}, u32[]{:S(2)}) collective-permute-start(bf16[128,1024]{1,0:T(8,128)(2,1)S(1)} %copy-done.26), channel_id=1, source_target_pairs={{0,1},{1,0},{2,3},{3,2},{4,5},{5,4},{6,7},{7,6},{8,9},{9,8},{10,11... | collective-permute-start | bytes 786440 | tf_op jit(solution)/shard_map/ppermute | solution.py:306
  46.6 0.8 copy-start.16
  56.6 9.3 %collective-permute-start.12 = (bf16[128,1024]{1,0:T(8,128)(2,1)}, bf16[128,1024]{1,0:T(8,128)(2,1)S(1)}, u32[]{:S(2)}, u32[]{:S(2)}) collective-permute-start(bf16[128,1024]{1,0:T(8,128)(2,1)} %get-tuple-element.70), channel_id=1, source_target_pairs={{0,1},{1,0},{2,3},{3,2},{4,5},{5,4},{6,7},{7,6},{8,9},{9,8},{10,11... | collective-permute-start | bytes 786440 | tf_op jit(solution)/shard_map/ppermute | solution.py:306
  57.0 2.6 %collective-permute-start.13 = (bf16[256,512]{1,0:T(8,128)(2,1)}, bf16[256,512]{1,0:T(8,128)(2,1)S(1)}, u32[]{:S(2)}, u32[]{:S(2)}) collective-permute-start(bf16[256,512]{1,0:T(8,128)(2,1)} %get-tuple-element.72), channel_id=1, source_target_pairs={{0,2},{2,0},{4,6},{6,4},{8,10},{10,8},{12,14},{14,12},{16,18},{18,... | collective-permute-start | bytes 786440 | tf_op jit(solution)/shard_map/ppermute | solution.py:310
  57.0 6.7 %collective-permute-start.15 = (bf16[256,512]{1,0:T(8,128)(2,1)}, bf16[256,512]{1,0:T(8,128)(2,1)S(1)}, u32[]{:S(2)}, u32[]{:S(2)}) collective-permute-start(bf16[256,512]{1,0:T(8,128)(2,1)} %get-tuple-element.75), channel_id=1, source_target_pairs={{0,2},{2,0},{4,6},{6,4},{8,10},{10,8},{12,14},{14,12},{16,18},{18,... | collective-permute-start | bytes 786440 | tf_op jit(solution)/shard_map/ppermute | solution.py:310
  59.4 1.0 %copy-start.23 = (bf16[256,512]{1,0:T(8,128)(2,1)S(1)}, bf16[256,512]{1,0:T(8,128)(2,1)}, u32[]{:S(2)}) copy-start(bf16[256,512]{1,0:T(8,128)(2,1)} %get-tuple-element.71) | copy-start | bytes 786436
  59.5 2.2 %copy-start.10 = (f32[256,512]{1,0:T(8,128)S(1)}, f32[256,512]{1,0:T(8,128)}, u32[]{:S(2)}) copy-start(f32[256,512]{1,0:T(8,128)} %get-tuple-element.82) | copy-start | bytes 1572868
  60.3 3.3 %copy-start.20 = (bf16[256,512]{1,0:T(8,128)(2,1)S(1)}, bf16[256,512]{1,0:T(8,128)(2,1)}, u32[]{:S(2)}) copy-start(bf16[256,512]{1,0:T(8,128)(2,1)} %get-tuple-element.74) | copy-start | bytes 786436
  60.4 11.7 %collective-permute-start.18 = (bf16[256,512]{1,0:T(8,128)(2,1)S(1)}, bf16[256,512]{1,0:T(8,128)(2,1)S(1)}, u32[]{:S(2)}, u32[]{:S(2)}) collective-permute-start(bf16[256,512]{1,0:T(8,128)(2,1)S(1)} %fusion.11), channel_id=1, source_target_pairs={{4,0},{6,2},{8,4},{10,6},{12,8},{14,10},{16,12},{18,14},{20,16},{2... | collective-permute-start | bytes 786440 | tf_op jit(solution)/shard_map/ppermute | solution.py:315
  61.7 4.2 %copy-start.18 = (bf16[128,1024]{1,0:T(8,128)(2,1)S(1)}, bf16[128,1024]{1,0:T(8,128)(2,1)}, u32[]{:S(2)}) copy-start(bf16[128,1024]{1,0:T(8,128)(2,1)} %get-tuple-element.76) | copy-start | bytes 786436
  61.7 4.2 %copy-start.19 = (bf16[128,1024]{1,0:T(8,128)(2,1)S(1)}, bf16[128,1024]{1,0:T(8,128)(2,1)}, u32[]{:S(2)}) copy-start(bf16[128,1024]{1,0:T(8,128)(2,1)} %get-tuple-element.77) | copy-start | bytes 786436
  61.9 14.6 %collective-permute-start.17 = (bf16[256,512]{1,0:T(8,128)(2,1)S(1)}, bf16[256,512]{1,0:T(8,128)(2,1)S(1)}, u32[]{:S(2)}, u32[]{:S(2)}) collective-permute-start(bf16[256,512]{1,0:T(8,128)(2,1)S(1)} %fusion.9), channel_id=1, source_target_pairs={{0,1},{1,0},{2,3},{3,2},{4,5},{5,4},{6,7},{7,6},{8,9},{9,8},{10,11... | collective-permute-start | bytes 786440 | tf_op jit(solution)/shard_map/ppermute | solution.py:306
  63.8 12.6 %collective-permute-start.16 = (bf16[256,512]{1,0:T(8,128)(2,1)S(1)}, bf16[256,512]{1,0:T(8,128)(2,1)S(1)}, u32[]{:S(2)}, u32[]{:S(2)}) collective-permute-start(bf16[256,512]{1,0:T(8,128)(2,1)S(1)} %fusion.16), channel_id=1, source_target_pairs={{4,0},{6,2},{8,4},{10,6},{12,8},{14,10},{16,12},{18,14},{20,16},{2... | collective-permute-start | bytes 786440 | tf_op jit(solution)/shard_map/ppermute | solution.py:315
  66.0 6.2 %copy-start.13 = (f32[256,512]{1,0:T(8,128)S(1)}, f32[256,512]{1,0:T(8,128)}, u32[]{:S(2)}) copy-start(f32[256,512]{1,0:T(8,128)} %get-tuple-element.85) | copy-start | bytes 1572868
  67.2 9.2 %copy-start.12 = (f32[256,512]{1,0:T(8,128)S(1)}, f32[256,512]{1,0:T(8,128)}, u32[]{:S(2)}) copy-start(f32[256,512]{1,0:T(8,128)} %get-tuple-element.81) | copy-start | bytes 1572868
  72.3 6.4 %collective-permute-start.19 = (bf16[256,512]{1,0:T(8,128)(2,1)S(1)}, bf16[256,512]{1,0:T(8,128)(2,1)S(1)}, u32[]{:S(2)}, u32[]{:S(2)}) collective-permute-start(bf16[256,512]{1,0:T(8,128)(2,1)S(1)} %fusion.14), channel_id=1, source_target_pairs={{0,1},{1,0},{2,3},{3,2},{4,5},{5,4},{6,7},{7,6},{8,9},{9,8},{10,11... | collective-permute-start | bytes 786440 | tf_op jit(solution)/shard_map/ppermute | solution.py:306
  78.8 0.8 copy-start.14
  78.8 1.0 %copy-start.15 = (bf16[128,2048]{1,0:T(8,128)(2,1)}, bf16[128,2048]{1,0:T(8,128)(2,1)S(1)}, u32[]{:S(2)}) copy-start(bf16[128,2048]{1,0:T(8,128)(2,1)S(1)} %get-tuple-element.92) | copy-start | bytes 1572868

commit v5 on v4

--- a/solution.py
+++ b/solution.py
@@ -14,7 +14,7 @@
 STEP_HEADS = 1
 HIDDEN = -1e30
 FAR = 1 << 20
-VMEM_BYTES = 57344 * 1024
+VMEM_BYTES = 53248 * 1024
 
 
 def shifted_2(block, axis, distance):

time: 80.1 us -> 79.4 us (level)
    unnamed x54 -> x30, local copies, waits for them, and re-layouts: 4.67 us -> 1.8 us
    dynamic_slice x11, local copies, waits for them, and re-layouts: 1.25 us -> 4.01 us  [packed(): lax.dynamic_slice_in_dim(a, start, width, 1)]
    ppermute x6, waiting for transfers between devices: 11.6 us -> 14.1 us  [moved(): lax.ppermute(block, 'tm', [(i, i + distance) for i in range(size) if 0 <=...]
    ppermute x8, waiting for transfers between devices: 6.37 us -> 4.64 us  [swap(): return lax.ppermute(block, 'space', [(0, 1), (1, 0)])]
    select_n x2, other arithmetic: 1.1 us -> 0.06 us  [attended(): jnp.where(odd, kv2_other[c], kv_other[c])]
  transfers between devices with their start and end apart: 20 -> 20, of which waited for: 11 -> 10; matrix products, arithmetic and copies ran while one was open for 9% -> 10% of each run, Pallas kernels for 23% -> 23%
where the time goes in v5:
time: 79.4 us; the launch traced here: 79 us
  starting transfers between devices  26.7 us (34%)
  waiting for transfers between devices  20.1 us (25%)
  Pallas kernels  18.5 us (23%)
  other arithmetic  6.57 us (8%)
  local copies, waits for them, and re-layouts  5.97 us (8%)
  between operations  1.1 us (1%)
    pallas_call x2, Pallas kernels, attend(): pl.pallas_call(attend_kernel, grid_spec=pltpu.PrefetchScalarGridSpec(num_...  18.5 us
    ppermute x6, starting transfers between devices, moved(): lax.ppermute(block, 'tm', [(i, i + distance) for i in range(size) if 0 <=...  14.7 us
    ppermute x6, waiting for transfers between devices, moved(): lax.ppermute(block, 'tm', [(i, i + distance) for i in range(size) if 0 <=...  14.1 us
    ppermute x8, starting transfers between devices, swap(): return lax.ppermute(block, 'space', [(0, 1), (1, 0)])  10.8 us
    ppermute x8, waiting for transfers between devices, swap(): return lax.ppermute(block, 'space', [(0, 1), (1, 0)])  4.64 us
    dynamic_slice x11, local copies, waits for them, and re-layouts, packed(): lax.dynamic_slice_in_dim(a, start, width, 1)  4.01 us
    concatenate x5, other arithmetic, packed(): jnp.concatenate([lax.dynamic_slice_in_dim(a, start, width, 1) for a in ar...  3.02 us
    unnamed x30, local copies, waits for them, and re-layouts  1.8 us
  transfers between devices with their start and end apart: 20, of which 10 were waited for; matrix products, arithmetic and copies ran while one was open for 10% of the time, Pallas kernels for 23%

profile of v5, /device:TPU:0, one launch (start us, length us, event | category | flops | bytes accessed | tf_op | source)
XLA Modules:
  0.0 79.0 jit_solution(13852007891834704120)
XLA Ops:
  0.6 1.0 %constant_dynamic-slice_fusion.10 = (bf16[128,512]{1,0:T(8,128)(2,1)S(1)}, bf16[128,512]{1,0:T(8,128)(2,1)S(1)}) fusion(bf16[128,2048]{1,0:T(8,128)(2,1)} %v_own.3, s32[]{:T(128)S(6)} %select_n.112, bf16[128,2048]{1,0:T(8,128)(2,1)} %k_own.3), kind=kLoop, calls=%fused_computation.64 | loop fusion | bytes 524292 | tf_op jit(solution)/shard_map/dynamic_slice | solution.py:142
  1.7 0.7 pad_maximum_fusion.10
  2.4 2.9 %collective-permute-start.1 = (bf16[256,512]{1,0:T(8,128)(2,1)}, bf16[256,512]{1,0:T(8,128)(2,1)S(1)}, u32[]{:S(2)}, u32[]{:S(2)}) collective-permute-start(bf16[256,512]{1,0:T(8,128)(2,1)} %pad_maximum_fusion.10), channel_id=1, source_target_pairs={{0,1},{1,0},{2,3},{3,2},{4,5},{5,4},{6,7},{7,6},{8,9},{9,8},{10,11... | collective-permute-start | bytes 786440 | tf_op jit(solution)/shard_map/ppermute | solution.py:306
  5.4 1.0 %constant_dynamic-slice_fusion.8 = bf16[128,512]{1,0:T(8,128)(2,1)S(1)} fusion(bf16[128,2048]{1,0:T(8,128)(2,1)} %v_own.3, s32[]{:T(128)S(6)} %select_n.113), kind=kLoop, calls=%fused_computation.62 | loop fusion | bytes 262148 | tf_op jit(solution)/shard_map/dynamic_slice | solution.py:142
  6.4 0.7 pad_maximum_fusion.11
  7.1 0.9 %constant_dynamic-slice_fusion.6 = bf16[128,512]{1,0:T(8,128)(2,1)S(1)} fusion(bf16[128,2048]{1,0:T(8,128)(2,1)} %v_own.3, s32[]{:T(128)S(6)} %select_n.114), kind=kLoop, calls=%fused_computation.60 | loop fusion | bytes 262148 | tf_op jit(solution)/shard_map/dynamic_slice | solution.py:142
  8.1 0.7 pad_maximum_fusion.12
  8.8 4.6 %collective-permute-start.2 = (bf16[256,512]{1,0:T(8,128)(2,1)}, bf16[256,512]{1,0:T(8,128)(2,1)}, u32[]{:S(2)}, u32[]{:S(2)}) collective-permute-start(bf16[256,512]{1,0:T(8,128)(2,1)} %pad_maximum_fusion.12), channel_id=1, source_target_pairs={{0,4},{2,6},{4,8},{6,10},{8,12},{10,14},{12,16},{14,18},{16,20},{1... | collective-permute-start | bytes 786440 | tf_op jit(solution)/shard_map/ppermute | solution.py:315
  13.5 0.8 %pad_maximum_fusion.4 = bf16[256,1024]{1,0:T(8,128)(2,1)} fusion(bf16[128,1024]{1,0:T(8,128)(2,1)S(1)} %constant_dynamic-slice_fusion.4, bf16[128,1024]{1,0:T(8,128)(2,1)S(1)} %constant_dynamic-slice_fusion.5), kind=kLoop, calls=%fused_computation.39 | loop fusion | flops 1048576 | bytes 1048576 | tf_op jit(solution)/shard_map/concatenate | solution.py:142
  14.3 1.5 %collective-permute-start = (bf16[256,1024]{1,0:T(8,128)(2,1)}, bf16[256,1024]{1,0:T(8,128)(2,1)}, u32[]{:S(2)}, u32[]{:S(2)}) collective-permute-start(bf16[256,1024]{1,0:T(8,128)(2,1)} %pad_maximum_fusion.4), channel_id=1, source_target_pairs={{0,1},{1,0},{2,3},{3,2},{4,5},{5,4},{6,7},{7,6},{8,9},{9,8},{10,11... | collective-permute-start | bytes 1572872 | tf_op jit(solution)/shard_map/ppermute | solution.py:306
  15.9 0.6 collective-permute-start.5
  16.5 0.9 %constant_dynamic-slice_fusion = bf16[128,512]{1,0:T(8,128)(2,1)S(1)} fusion(bf16[128,2048]{1,0:T(8,128)(2,1)} %v_own.3, s32[]{:T(128)S(6)} %select_n.123), kind=kLoop, calls=%fused_computation.54 | loop fusion | bytes 262148 | tf_op jit(solution)/shard_map/dynamic_slice | solution.py:142
  17.5 2.8 %collective-permute-start.3 = (bf16[256,512]{1,0:T(8,128)(2,1)S(1)}, bf16[256,512]{1,0:T(8,128)(2,1)S(1)}, u32[]{:S(2)}, u32[]{:S(2)}) collective-permute-start(bf16[256,512]{1,0:T(8,128)(2,1)S(1)} %collective-permute-done.1.kv_other), channel_id=1, source_target_pairs={{0,4},{2,6},{4,8},{6,10},{8,12},{10,14},{12,16},{14,18},{16,20},{1... | collective-permute-start | bytes 786440 | tf_op jit(solution)/shard_map/ppermute | solution.py:315
  20.3 3.4 %collective-permute-start.9 = (bf16[512,512]{1,0:T(8,128)(2,1)S(1)}, bf16[512,512]{1,0:T(8,128)(2,1)S(1)}, u32[]{:S(2)}, u32[]{:S(2)}) collective-permute-start(bf16[512,512]{1,0:T(8,128)(2,1)S(1)} %pad_maximum_fusion.8), channel_id=1, source_target_pairs={{0,4},{2,6},{4,8},{6,10},{8,12},{10,14},{12,16},{14,18},{16,20},{1... | collective-permute-start | bytes 1572872 | tf_op jit(solution)/shard_map/ppermute | solution.py:315
  23.9 2.9 %collective-permute-done.3.kv2_other = bf16[256,512]{1,0:T(8,128)(2,1)S(1)} collective-permute-done((bf16[256,512]{1,0:T(8,128)(2,1)S(1)}, bf16[256,512]{1,0:T(8,128)(2,1)S(1)}, u32[]{:S(2)}, u32[]{:S(2)}) %collective-permute-start.3) | collective-permute-done | bytes 262176 | tf_op jit(solution)/shard_map/ppermute | solution.py:315
  27.1 2.5 %collective-permute-done.qg_other = bf16[256,1024]{1,0:T(8,128)(2,1)} collective-permute-done((bf16[256,1024]{1,0:T(8,128)(2,1)}, bf16[256,1024]{1,0:T(8,128)(2,1)}, u32[]{:S(2)}, u32[]{:S(2)}) %collective-permute-start) | collective-permute-done | bytes 524320 | tf_op jit(solution)/shard_map/ppermute | solution.py:306
  29.7 0.8 copy-done.12
  30.5 9.3 %shard_map.85 = (bf16[128,1024]{1,0:T(8,128)(2,1)S(1)}, bf16[128,1024]{1,0:T(8,128)(2,1)S(1)}, f32[256,512]{1,0:T(8,128)}, f32[256,512]{1,0:T(8,128)}, bf16[256,...) custom-call(s32[1]{0:T(128)} %bitcast.side_ref, ...), custom_call_target="tpu_custom_call" | custom-call | tf_op jit(solution)/shard_map/pallas_call | solution.py:281
  39.7 0.3 collective-permute-done.5.qg_other
  40.1 0.5 collective-permute-start.7
  40.6 1.0 %collective-permute-done.6 = bf16[256,512]{1,0:T(8,128)(2,1)S(1)} collective-permute-done((bf16[256,512]{1,0:T(8,128)(2,1)S(1)}, bf16[256,512]{1,0:T(8,128)(2,1)S(1)}, u32[]{:S(2)}, u32[]{:S(2)}) %collective-permute-start.6) | collective-permute-done | bytes 262176 | tf_op jit(solution)/shard_map/ppermute | solution.py:310
  41.6 0.4 collective-permute-done.7
  42.1 0.8 %pad_maximum_fusion.9 = bf16[512,512]{1,0:T(8,128)(2,1)} fusion(bf16[256,512]{1,0:T(8,128)(2,1)S(1)} %broadcast_select_fusion, bf16[256,512]{1,0:T(8,128)(2,1)S(1)} %maximum_select_fusion.1), kind=kLoop, calls=%fused_computation.44 | loop fusion | flops 1048576 | bytes 1048576 | tf_op jit(solution)/shard_map/concatenate | solution.py:361
  42.9 0.1 collective-permute-start.10
  43.1 0.1 fusion.6
  43.3 1.3 %collective-permute-start.14 = (bf16[512,512]{1,0:T(8,128)(2,1)S(1)}, bf16[512,512]{1,0:T(8,128)(2,1)S(1)}, u32[]{:S(2)}, u32[]{:S(2)}) collective-permute-start(bf16[512,512]{1,0:T(8,128)(2,1)S(1)} %pad_maximum_fusion.7), channel_id=1, source_target_pairs={{4,0},{6,2},{8,4},{10,6},{12,8},{14,10},{16,12},{18,14},{20,16},{2... | collective-permute-start | bytes 1572872 | tf_op jit(solution)/shard_map/ppermute | solution.py:315
  44.6 1.9 %collective-permute-start.11 = (bf16[128,1024]{1,0:T(8,128)(2,1)S(1)}, bf16[128,1024]{1,0:T(8,128)(2,1)S(1)}, u32[]{:S(2)}, u32[]{:S(2)}) collective-permute-start(bf16[128,1024]{1,0:T(8,128)(2,1)S(1)} %get-tuple-element.69), channel_id=1, source_target_pairs={{0,1},{1,0},{2,3},{3,2},{4,5},{5,4},{6,7},{7,6},{8,9},{9,8},{10,11... | collective-permute-start | bytes 786440 | tf_op jit(solution)/shard_map/ppermute | solution.py:306
  46.5 9.3 %shard_map.86 = (bf16[128,1024]{1,0:T(8,128)(2,1)S(1)}, bf16[128,1024]{1,0:T(8,128)(2,1)S(1)}, f32[256,512]{1,0:T(8,128)}, f32[256,512]{1,0:T(8,128)}, bf16[256,...) custom-call(s32[1]{0:T(128)} %bitcast.side_ref, ...), custom_call_target="tpu_custom_call" | custom-call | tf_op jit(solution)/shard_map/pallas_call | solution.py:281
  55.7 0.5 collective-permute-start.12
  56.3 0.5 collective-permute-start.15
  56.8 2.7 %collective-permute-done.14 = bf16[512,512]{1,0:T(8,128)(2,1)S(1)} collective-permute-done((bf16[512,512]{1,0:T(8,128)(2,1)S(1)}, bf16[512,512]{1,0:T(8,128)(2,1)S(1)}, u32[]{:S(2)}, u32[]{:S(2)}) %collective-permute-start.14) | collective-permute-done | bytes 524320 | tf_op jit(solution)/shard_map/ppermute | solution.py:315
  59.5 0.1 fusion.4
  59.7 0.1 fusion.11
  59.8 1.3 %collective-permute-start.18 = (bf16[256,512]{1,0:T(8,128)(2,1)S(1)}, bf16[256,512]{1,0:T(8,128)(2,1)S(1)}, u32[]{:S(2)}, u32[]{:S(2)}) collective-permute-start(bf16[256,512]{1,0:T(8,128)(2,1)S(1)} %fusion.11), channel_id=1, source_target_pairs={{4,0},{6,2},{8,4},{10,6},{12,8},{14,10},{16,12},{18,14},{20,16},{2... | collective-permute-start | bytes 786440 | tf_op jit(solution)/shard_map/ppermute | solution.py:315
  61.1 0.1 fusion.9
  61.2 1.8 %collective-permute-start.17 = (bf16[256,512]{1,0:T(8,128)(2,1)S(1)}, bf16[256,512]{1,0:T(8,128)(2,1)S(1)}, u32[]{:S(2)}, u32[]{:S(2)}) collective-permute-start(bf16[256,512]{1,0:T(8,128)(2,1)S(1)} %fusion.9), channel_id=1, source_target_pairs={{0,1},{1,0},{2,3},{3,2},{4,5},{5,4},{6,7},{7,6},{8,9},{9,8},{10,11... | collective-permute-start | bytes 786440 | tf_op jit(solution)/shard_map/ppermute | solution.py:306
  63.1 1.3 %collective-permute-start.16 = (bf16[256,512]{1,0:T(8,128)(2,1)S(1)}, bf16[256,512]{1,0:T(8,128)(2,1)S(1)}, u32[]{:S(2)}, u32[]{:S(2)}) collective-permute-start(bf16[256,512]{1,0:T(8,128)(2,1)S(1)} %fusion.16), channel_id=1, source_target_pairs={{4,0},{6,2},{8,4},{10,6},{12,8},{14,10},{16,12},{18,14},{20,16},{2... | collective-permute-start | bytes 786440 | tf_op jit(solution)/shard_map/ppermute | solution.py:315
  64.4 0.2 collective-permute-done.12
  64.5 1.2 %maximum_select_fusion = bf16[128,4096]{1,0:T(8,128)(2,1)} fusion(bf16[128,1024]{1,0:T(8,128)(2,1)S(1)} %collective-permute-done.12, bf16[128,1024]{1,0:T(8,128)(2,1)S(1)} %collective-permute-done.11, bf16[128,1024]{1,0:T(8,128)(2,1)S(1)} %get-tuple-element.77, bf16[128,1024]{1,0:T(8,128)(2,1)S(1)} %get-tuple-element.76, pred[]{:T(512)S(6)} %eq.10), kind=kLoop, calls=%fused_computation | loop fusion | flops 8912896 | bytes 2097153 | tf_op jit(solution)/shard_map/jit(_where)/select_n | solution.py:409
  65.7 5.7 %collective-permute-done.18 = bf16[256,512]{1,0:T(8,128)(2,1)S(1)} collective-permute-done((bf16[256,512]{1,0:T(8,128)(2,1)S(1)}, bf16[256,512]{1,0:T(8,128)(2,1)S(1)}, u32[]{:S(2)}, u32[]{:S(2)}) %collective-permute-start.18) | collective-permute-done | bytes 262176 | tf_op jit(solution)/shard_map/ppermute | solution.py:315
  71.5 0.1 fusion.14
  71.6 1.6 %collective-permute-start.19 = (bf16[256,512]{1,0:T(8,128)(2,1)S(1)}, bf16[256,512]{1,0:T(8,128)(2,1)S(1)}, u32[]{:S(2)}, u32[]{:S(2)}) collective-permute-start(bf16[256,512]{1,0:T(8,128)(2,1)S(1)} %fusion.14), channel_id=1, source_target_pairs={{0,1},{1,0},{2,3},{3,2},{4,5},{5,4},{6,7},{7,6},{8,9},{9,8},{10,11... | collective-permute-start | bytes 786440 | tf_op jit(solution)/shard_map/ppermute | solution.py:306
  73.1 2.8 %collective-permute-done.16 = bf16[256,512]{1,0:T(8,128)(2,1)S(1)} collective-permute-done((bf16[256,512]{1,0:T(8,128)(2,1)S(1)}, bf16[256,512]{1,0:T(8,128)(2,1)S(1)}, u32[]{:S(2)}, u32[]{:S(2)}) %collective-permute-start.16) | collective-permute-done | bytes 262176 | tf_op jit(solution)/shard_map/ppermute | solution.py:315
  75.9 0.1 fusion.19
  76.2 0.3 fusion.25
  76.4 1.6 %collective-permute-done.19 = bf16[256,512]{1,0:T(8,128)(2,1)S(1)} collective-permute-done((bf16[256,512]{1,0:T(8,128)(2,1)S(1)}, bf16[256,512]{1,0:T(8,128)(2,1)S(1)}, u32[]{:S(2)}, u32[]{:S(2)}) %collective-permute-start.19) | collective-permute-done | bytes 262176 | tf_op jit(solution)/shard_map/ppermute | solution.py:306
  78.1 0.8 copy-done.10
  78.8 0.2 copy-done.11
  (68 shorter events, 1.0 us)
Async XLA Ops:
  0.6 4.7 %copy-start.2 = (bf16[128,2048]{1,0:T(8,128)(2,1)S(1)}, bf16[128,2048]{1,0:T(8,128)(2,1)}, u32[]{:S(2)}) copy-start(bf16[128,2048]{1,0:T(8,128)(2,1)} %k_own.3) | copy-start | bytes 1572868
  2.4 15.0 %collective-permute-start.1 = (bf16[256,512]{1,0:T(8,128)(2,1)}, bf16[256,512]{1,0:T(8,128)(2,1)S(1)}, u32[]{:S(2)}, u32[]{:S(2)}) collective-permute-start(bf16[256,512]{1,0:T(8,128)(2,1)} %pad_maximum_fusion.10), channel_id=1, source_target_pairs={{0,1},{1,0},{2,3},{3,2},{4,5},{5,4},{6,7},{7,6},{8,9},{9,8},{10,11... | collective-permute-start | bytes 786440 | tf_op jit(solution)/shard_map/ppermute | solution.py:306
  5.4 8.0 %copy-start = (bf16[128,4096]{1,0:T(8,128)(2,1)S(1)}, bf16[128,4096]{1,0:T(8,128)(2,1)}, u32[]{:S(2)}) copy-start(bf16[128,4096]{1,0:T(8,128)(2,1)} %q_own.3) | copy-start | bytes 3145732
  6.4 7.0 %copy-start.1 = (bf16[128,4096]{1,0:T(8,128)(2,1)S(1)}, bf16[128,4096]{1,0:T(8,128)(2,1)}, u32[]{:S(2)}) copy-start(bf16[128,4096]{1,0:T(8,128)(2,1)} %g_own.3) | copy-start | bytes 3145732
  7.1 13.1 %collective-permute-start.8 = (bf16[256,512]{1,0:T(8,128)(2,1)}, bf16[256,512]{1,0:T(8,128)(2,1)S(1)}, u32[]{:S(2)}, u32[]{:S(2)}) collective-permute-start(bf16[256,512]{1,0:T(8,128)(2,1)} %pad_maximum_fusion.11), channel_id=1, source_target_pairs={{0,1},{1,0},{2,3},{3,2},{4,5},{5,4},{6,7},{7,6},{8,9},{9,8},{10,11... | collective-permute-start | bytes 786440 | tf_op jit(solution)/shard_map/ppermute | solution.py:306
  8.8 15.0 %collective-permute-start.2 = (bf16[256,512]{1,0:T(8,128)(2,1)}, bf16[256,512]{1,0:T(8,128)(2,1)}, u32[]{:S(2)}, u32[]{:S(2)}) collective-permute-start(bf16[256,512]{1,0:T(8,128)(2,1)} %pad_maximum_fusion.12), channel_id=1, source_target_pairs={{0,4},{2,6},{4,8},{6,10},{8,12},{10,14},{12,16},{14,18},{16,20},{1... | collective-permute-start | bytes 786440 | tf_op jit(solution)/shard_map/ppermute | solution.py:315
  14.3 15.4 %collective-permute-start = (bf16[256,1024]{1,0:T(8,128)(2,1)}, bf16[256,1024]{1,0:T(8,128)(2,1)}, u32[]{:S(2)}, u32[]{:S(2)}) collective-permute-start(bf16[256,1024]{1,0:T(8,128)(2,1)} %pad_maximum_fusion.4), channel_id=1, source_target_pairs={{0,1},{1,0},{2,3},{3,2},{4,5},{5,4},{6,7},{7,6},{8,9},{9,8},{10,11... | collective-permute-start | bytes 1572872 | tf_op jit(solution)/shard_map/ppermute | solution.py:306
  15.9 24.2 %collective-permute-start.5 = (bf16[256,1024]{1,0:T(8,128)(2,1)S(1)}, bf16[256,1024]{1,0:T(8,128)(2,1)}, u32[]{:S(2)}, u32[]{:S(2)}) collective-permute-start(bf16[256,1024]{1,0:T(8,128)(2,1)S(1)} %pad_maximum_fusion.6), channel_id=1, source_target_pairs={{0,1},{1,0},{2,3},{3,2},{4,5},{5,4},{6,7},{7,6},{8,9},{9,8},{10,11... | collective-permute-start | bytes 1572872 | tf_op jit(solution)/shard_map/ppermute | solution.py:306
  17.5 9.4 %collective-permute-start.3 = (bf16[256,512]{1,0:T(8,128)(2,1)S(1)}, bf16[256,512]{1,0:T(8,128)(2,1)S(1)}, u32[]{:S(2)}, u32[]{:S(2)}) collective-permute-start(bf16[256,512]{1,0:T(8,128)(2,1)S(1)} %collective-permute-done.1.kv_other), channel_id=1, source_target_pairs={{0,4},{2,6},{4,8},{6,10},{8,12},{10,14},{12,16},{14,18},{16,20},{1... | collective-permute-start | bytes 786440 | tf_op jit(solution)/shard_map/ppermute | solution.py:315
  20.3 20.3 %collective-permute-start.9 = (bf16[512,512]{1,0:T(8,128)(2,1)S(1)}, bf16[512,512]{1,0:T(8,128)(2,1)S(1)}, u32[]{:S(2)}, u32[]{:S(2)}) collective-permute-start(bf16[512,512]{1,0:T(8,128)(2,1)S(1)} %pad_maximum_fusion.8), channel_id=1, source_target_pairs={{0,4},{2,6},{4,8},{6,10},{8,12},{10,14},{12,16},{14,18},{16,20},{1... | collective-permute-start | bytes 1572872 | tf_op jit(solution)/shard_map/ppermute | solution.py:315
  23.9 3.1 %copy-start.13 = (s32[2,6]{1,0:T(2,128)S(1)}, s32[2,6]{1,0:T(2,128)}, u32[]{:S(2)}) copy-start(s32[2,6]{1,0:T(2,128)} %param.11) | copy-start | bytes 148
  23.9 3.1 %copy-start.14 = (s32[2,6]{1,0:T(2,128)S(1)}, s32[2,6]{1,0:T(2,128)}, u32[]{:S(2)}) copy-start(s32[2,6]{1,0:T(2,128)} %param.10) | copy-start | bytes 148
  26.8 2.8 %copy-start.5 = (bf16[256,512]{1,0:T(8,128)(2,1)}, bf16[256,512]{1,0:T(8,128)(2,1)S(1)}, u32[]{:S(2)}) copy-start(bf16[256,512]{1,0:T(8,128)(2,1)S(1)} %collective-permute-done.3.kv2_other) | copy-start | bytes 786436
  26.9 2.7 %collective-permute-start.4 = (bf16[512,512]{1,0:T(8,128)(2,1)S(1)}, bf16[512,512]{1,0:T(8,128)(2,1)S(1)}, u32[]{:S(2)}, u32[]{:S(2)}) collective-permute-start(bf16[512,512]{1,0:T(8,128)(2,1)S(1)} %pad_maximum_fusion.5), channel_id=1, source_target_pairs={{0,2},{2,0},{4,6},{6,4},{8,10},{10,8},{12,14},{14,12},{16,18},{18,... | collective-permute-start | bytes 1572872 | tf_op jit(solution)/shard_map/ppermute | solution.py:310
  29.7 0.8 %copy-start.12 = (bf16[512,512]{1,0:T(8,128)(2,1)}, bf16[512,512]{1,0:T(8,128)(2,1)S(1)}, u32[]{:S(2)}) copy-start(bf16[512,512]{1,0:T(8,128)(2,1)S(1)} %collective-permute-done.4.kv1) | copy-start | bytes 1572868
  40.1 1.5 %collective-permute-start.6 = (bf16[256,512]{1,0:T(8,128)(2,1)S(1)}, bf16[256,512]{1,0:T(8,128)(2,1)S(1)}, u32[]{:S(2)}, u32[]{:S(2)}) collective-permute-start(bf16[256,512]{1,0:T(8,128)(2,1)S(1)} %get-tuple-element.60), channel_id=1, source_target_pairs={{0,2},{2,0},{4,6},{6,4},{8,10},{10,8},{12,14},{14,12},{16,18},{18,... | collective-permute-start | bytes 786440 | tf_op jit(solution)/shard_map/ppermute | solution.py:310
  40.1 1.9 %collective-permute-start.7 = (bf16[256,512]{1,0:T(8,128)(2,1)S(1)}, bf16[256,512]{1,0:T(8,128)(2,1)S(1)}, u32[]{:S(2)}, u32[]{:S(2)}) collective-permute-start(bf16[256,512]{1,0:T(8,128)(2,1)S(1)} %get-tuple-element.62), channel_id=1, source_target_pairs={{0,2},{2,0},{4,6},{6,4},{8,10},{10,8},{12,14},{14,12},{16,18},{18,... | collective-permute-start | bytes 786440 | tf_op jit(solution)/shard_map/ppermute | solution.py:310
  40.6 2.3 %copy-start.3 = (bf16[256,512]{1,0:T(8,128)(2,1)}, bf16[256,512]{1,0:T(8,128)(2,1)S(1)}, u32[]{:S(2)}) copy-start(bf16[256,512]{1,0:T(8,128)(2,1)S(1)} %get-tuple-element.67.kv2_other) | copy-start | bytes 786436
  40.6 2.3 %copy-start.4 = (bf16[256,512]{1,0:T(8,128)(2,1)}, bf16[256,512]{1,0:T(8,128)(2,1)S(1)}, u32[]{:S(2)}) copy-start(bf16[256,512]{1,0:T(8,128)(2,1)S(1)} %get-tuple-element.66.kv2_own) | copy-start | bytes 786436
  42.9 3.5 %collective-permute-start.10 = (bf16[512,512]{1,0:T(8,128)(2,1)}, bf16[512,512]{1,0:T(8,128)(2,1)}, u32[]{:S(2)}, u32[]{:S(2)}) collective-permute-start(bf16[512,512]{1,0:T(8,128)(2,1)} %pad_maximum_fusion.9), channel_id=1, source_target_pairs={{0,2},{2,0},{4,6},{6,4},{8,10},{10,8},{12,14},{14,12},{16,18},{18,... | collective-permute-start | bytes 1572872 | tf_op jit(solution)/shard_map/ppermute | solution.py:310
  43.3 16.2 %collective-permute-start.14 = (bf16[512,512]{1,0:T(8,128)(2,1)S(1)}, bf16[512,512]{1,0:T(8,128)(2,1)S(1)}, u32[]{:S(2)}, u32[]{:S(2)}) collective-permute-start(bf16[512,512]{1,0:T(8,128)(2,1)S(1)} %pad_maximum_fusion.7), channel_id=1, source_target_pairs={{4,0},{6,2},{8,4},{10,6},{12,8},{14,10},{16,12},{18,14},{20,16},{2... | collective-permute-start | bytes 1572872 | tf_op jit(solution)/shard_map/ppermute | solution.py:315
  44.6 14.9 %copy-start.7 = (f32[256,512]{1,0:T(8,128)S(1)}, f32[256,512]{1,0:T(8,128)}, u32[]{:S(2)}) copy-start(f32[256,512]{1,0:T(8,128)} %get-tuple-element.80) | copy-start | bytes 1572868
  44.6 19.8 %collective-permute-start.11 = (bf16[128,1024]{1,0:T(8,128)(2,1)S(1)}, bf16[128,1024]{1,0:T(8,128)(2,1)S(1)}, u32[]{:S(2)}, u32[]{:S(2)}) collective-permute-start(bf16[128,1024]{1,0:T(8,128)(2,1)S(1)} %get-tuple-element.69), channel_id=1, source_target_pairs={{0,1},{1,0},{2,3},{3,2},{4,5},{5,4},{6,7},{7,6},{8,9},{9,8},{10,11... | collective-permute-start | bytes 786440 | tf_op jit(solution)/shard_map/ppermute | solution.py:306
  55.7 8.8 %collective-permute-start.12 = (bf16[128,1024]{1,0:T(8,128)(2,1)S(1)}, bf16[128,1024]{1,0:T(8,128)(2,1)S(1)}, u32[]{:S(2)}, u32[]{:S(2)}) collective-permute-start(bf16[128,1024]{1,0:T(8,128)(2,1)S(1)} %get-tuple-element.70), channel_id=1, source_target_pairs={{0,1},{1,0},{2,3},{3,2},{4,5},{5,4},{6,7},{7,6},{8,9},{9,8},{10,11... | collective-permute-start | bytes 786440 | tf_op jit(solution)/shard_map/ppermute | solution.py:306
  56.3 3.4 %collective-permute-start.13 = (bf16[256,512]{1,0:T(8,128)(2,1)S(1)}, bf16[256,512]{1,0:T(8,128)(2,1)S(1)}, u32[]{:S(2)}, u32[]{:S(2)}) collective-permute-start(bf16[256,512]{1,0:T(8,128)(2,1)S(1)} %get-tuple-element.72), channel_id=1, source_target_pairs={{0,2},{2,0},{4,6},{6,4},{8,10},{10,8},{12,14},{14,12},{16,18},{18,... | collective-permute-start | bytes 786440 | tf_op jit(solution)/shard_map/ppermute | solution.py:310
  56.3 6.7 %collective-permute-start.15 = (bf16[256,512]{1,0:T(8,128)(2,1)S(1)}, bf16[256,512]{1,0:T(8,128)(2,1)S(1)}, u32[]{:S(2)}, u32[]{:S(2)}) collective-permute-start(bf16[256,512]{1,0:T(8,128)(2,1)S(1)} %get-tuple-element.75), channel_id=1, source_target_pairs={{0,2},{2,0},{4,6},{6,4},{8,10},{10,8},{12,14},{14,12},{16,18},{18,... | collective-permute-start | bytes 786440 | tf_op jit(solution)/shard_map/ppermute | solution.py:310
  59.6 1.5 %copy-start.6 = (f32[256,512]{1,0:T(8,128)S(1)}, f32[256,512]{1,0:T(8,128)}, u32[]{:S(2)}) copy-start(f32[256,512]{1,0:T(8,128)} %get-tuple-element.82) | copy-start | bytes 1572868
  59.8 11.7 %collective-permute-start.18 = (bf16[256,512]{1,0:T(8,128)(2,1)S(1)}, bf16[256,512]{1,0:T(8,128)(2,1)S(1)}, u32[]{:S(2)}, u32[]{:S(2)}) collective-permute-start(bf16[256,512]{1,0:T(8,128)(2,1)S(1)} %fusion.11), channel_id=1, source_target_pairs={{4,0},{6,2},{8,4},{10,6},{12,8},{14,10},{16,12},{18,14},{20,16},{2... | collective-permute-start | bytes 786440 | tf_op jit(solution)/shard_map/ppermute | solution.py:315
  61.2 14.9 %collective-permute-start.17 = (bf16[256,512]{1,0:T(8,128)(2,1)S(1)}, bf16[256,512]{1,0:T(8,128)(2,1)S(1)}, u32[]{:S(2)}, u32[]{:S(2)}) collective-permute-start(bf16[256,512]{1,0:T(8,128)(2,1)S(1)} %fusion.9), channel_id=1, source_target_pairs={{0,1},{1,0},{2,3},{3,2},{4,5},{5,4},{6,7},{7,6},{8,9},{9,8},{10,11... | collective-permute-start | bytes 786440 | tf_op jit(solution)/shard_map/ppermute | solution.py:306
  63.1 12.9 %collective-permute-start.16 = (bf16[256,512]{1,0:T(8,128)(2,1)S(1)}, bf16[256,512]{1,0:T(8,128)(2,1)S(1)}, u32[]{:S(2)}, u32[]{:S(2)}) collective-permute-start(bf16[256,512]{1,0:T(8,128)(2,1)S(1)} %fusion.16), channel_id=1, source_target_pairs={{4,0},{6,2},{8,4},{10,6},{12,8},{14,10},{16,12},{18,14},{20,16},{2... | collective-permute-start | bytes 786440 | tf_op jit(solution)/shard_map/ppermute | solution.py:315
  64.5 6.9 %copy-start.9 = (f32[256,512]{1,0:T(8,128)S(1)}, f32[256,512]{1,0:T(8,128)}, u32[]{:S(2)}) copy-start(f32[256,512]{1,0:T(8,128)} %get-tuple-element.85) | copy-start | bytes 1572868
  65.7 10.2 %copy-start.8 = (f32[256,512]{1,0:T(8,128)S(1)}, f32[256,512]{1,0:T(8,128)}, u32[]{:S(2)}) copy-start(f32[256,512]{1,0:T(8,128)} %get-tuple-element.81) | copy-start | bytes 1572868
  71.6 6.4 %collective-permute-start.19 = (bf16[256,512]{1,0:T(8,128)(2,1)S(1)}, bf16[256,512]{1,0:T(8,128)(2,1)S(1)}, u32[]{:S(2)}, u32[]{:S(2)}) collective-permute-start(bf16[256,512]{1,0:T(8,128)(2,1)S(1)} %fusion.14), channel_id=1, source_target_pairs={{0,1},{1,0},{2,3},{3,2},{4,5},{5,4},{6,7},{7,6},{8,9},{9,8},{10,11... | collective-permute-start | bytes 786440 | tf_op jit(solution)/shard_map/ppermute | solution.py:306
  78.1 0.8 %copy-start.10 = (bf16[128,2048]{1,0:T(8,128)(2,1)}, bf16[128,2048]{1,0:T(8,128)(2,1)S(1)}, u32[]{:S(2)}) copy-start(bf16[128,2048]{1,0:T(8,128)(2,1)S(1)} %get-tuple-element.91) | copy-start | bytes 1572868
  78.1 1.0 %copy-start.11 = (bf16[128,2048]{1,0:T(8,128)(2,1)}, bf16[128,2048]{1,0:T(8,128)(2,1)S(1)}, u32[]{:S(2)}) copy-start(bf16[128,2048]{1,0:T(8,128)(2,1)S(1)} %get-tuple-element.92) | copy-start | bytes 1572868

commit v6 on v5

--- a/solution.py
+++ b/solution.py
@@ -11,7 +11,7 @@
 BLOCK_TOKENS = 128
 MAXT = 6
 REACH = 2
-STEP_HEADS = 1
+STEP_HEADS = 2
 HIDDEN = -1e30
 FAR = 1 << 20
 VMEM_BYTES = 53248 * 1024
@@ -435,7 +435,7 @@
         and tiles.shape[0] == 2
         and queries.shape[0] == BLOCK_TOKENS
         and queries.shape[1] == 2 * keys.shape[1]
-        and keys.shape[1] % (4 * HEAD_SIZE) == 0
+        and keys.shape[1] % (4 * STEP_HEADS * HEAD_SIZE) == 0
     )
     run = pair_body if pair else general_body
     return run(queries, keys, values, output_gradient, tiles, kinds)

time: 79.4 us -> 79.4 us (level)
  Pallas kernels: 18.5 us -> 17.6 us
  waiting for transfers between devices: 20.1 us -> 21 us
    pallas_call x2, Pallas kernels: 18.5 us -> 17.6 us  [attend(): pl.pallas_call(attend_kernel, grid_spec=pltpu.PrefetchScalarGridSpec(num_...]
  transfers between devices with their start and end apart: 20 -> 20, of which waited for: 10 -> 9; matrix products, arithmetic and copies ran while one was open for 10% -> 10% of each run, Pallas kernels for 23% -> 22%
where the time goes in v6:
time: 79.4 us; the launch traced here: 79 us
  starting transfers between devices  26.7 us (34%)
  waiting for transfers between devices  21 us (26%)
  Pallas kernels  17.6 us (22%)
  other arithmetic  6.57 us (8%)
  local copies, waits for them, and re-layouts  5.97 us (8%)
  between operations  1.12 us (1%)
    pallas_call x2, Pallas kernels, attend(): pl.pallas_call(attend_kernel, grid_spec=pltpu.PrefetchScalarGridSpec(num_...  17.6 us
    ppermute x6, waiting for transfers between devices, moved(): lax.ppermute(block, 'tm', [(i, i + distance) for i in range(size) if 0 <=...  14.8 us
    ppermute x6, starting transfers between devices, moved(): lax.ppermute(block, 'tm', [(i, i + distance) for i in range(size) if 0 <=...  14.7 us
    ppermute x8, starting transfers between devices, swap(): return lax.ppermute(block, 'space', [(0, 1), (1, 0)])  10.7 us
    ppermute x8, waiting for transfers between devices, swap(): return lax.ppermute(block, 'space', [(0, 1), (1, 0)])  4.93 us
    dynamic_slice x11, local copies, waits for them, and re-layouts, packed(): lax.dynamic_slice_in_dim(a, start, width, 1)  4.01 us
    concatenate x5, other arithmetic, packed(): jnp.concatenate([lax.dynamic_slice_in_dim(a, start, width, 1) for a in ar...  3.02 us
    unnamed x30, local copies, waits for them, and re-layouts  1.8 us
  transfers between devices with their start and end apart: 20, of which 9 were waited for; matrix products, arithmetic and copies ran while one was open for 10% of the time, Pallas kernels for 22%

profile of v6, /device:TPU:0, one launch (start us, length us, event | category | flops | bytes accessed | tf_op | source)
XLA Modules:
  0.0 79.0 jit_solution(15853189105955485929)
XLA Ops:
  0.6 1.0 %constant_dynamic-slice_fusion.10 = (bf16[128,512]{1,0:T(8,128)(2,1)S(1)}, bf16[128,512]{1,0:T(8,128)(2,1)S(1)}) fusion(bf16[128,2048]{1,0:T(8,128)(2,1)} %v_own.3, s32[]{:T(128)S(6)} %select_n.112, bf16[128,2048]{1,0:T(8,128)(2,1)} %k_own.3), kind=kLoop, calls=%fused_computation.64 | loop fusion | bytes 524292 | tf_op jit(solution)/shard_map/dynamic_slice | solution.py:142
  1.7 0.7 pad_maximum_fusion.10
  2.4 2.9 %collective-permute-start.1 = (bf16[256,512]{1,0:T(8,128)(2,1)}, bf16[256,512]{1,0:T(8,128)(2,1)S(1)}, u32[]{:S(2)}, u32[]{:S(2)}) collective-permute-start(bf16[256,512]{1,0:T(8,128)(2,1)} %pad_maximum_fusion.10), channel_id=1, source_target_pairs={{0,1},{1,0},{2,3},{3,2},{4,5},{5,4},{6,7},{7,6},{8,9},{9,8},{10,11... | collective-permute-start | bytes 786440 | tf_op jit(solution)/shard_map/ppermute | solution.py:306
  5.4 1.0 %constant_dynamic-slice_fusion.8 = bf16[128,512]{1,0:T(8,128)(2,1)S(1)} fusion(bf16[128,2048]{1,0:T(8,128)(2,1)} %v_own.3, s32[]{:T(128)S(6)} %select_n.113), kind=kLoop, calls=%fused_computation.62 | loop fusion | bytes 262148 | tf_op jit(solution)/shard_map/dynamic_slice | solution.py:142
  6.4 0.7 pad_maximum_fusion.11
  7.1 0.9 %constant_dynamic-slice_fusion.6 = bf16[128,512]{1,0:T(8,128)(2,1)S(1)} fusion(bf16[128,2048]{1,0:T(8,128)(2,1)} %v_own.3, s32[]{:T(128)S(6)} %select_n.114), kind=kLoop, calls=%fused_computation.60 | loop fusion | bytes 262148 | tf_op jit(solution)/shard_map/dynamic_slice | solution.py:142
  8.1 0.7 pad_maximum_fusion.12
  8.8 4.6 %collective-permute-start.2 = (bf16[256,512]{1,0:T(8,128)(2,1)}, bf16[256,512]{1,0:T(8,128)(2,1)}, u32[]{:S(2)}, u32[]{:S(2)}) collective-permute-start(bf16[256,512]{1,0:T(8,128)(2,1)} %pad_maximum_fusion.12), channel_id=1, source_target_pairs={{0,4},{2,6},{4,8},{6,10},{8,12},{10,14},{12,16},{14,18},{16,20},{1... | collective-permute-start | bytes 786440 | tf_op jit(solution)/shard_map/ppermute | solution.py:315
  13.5 0.8 %pad_maximum_fusion.4 = bf16[256,1024]{1,0:T(8,128)(2,1)} fusion(bf16[128,1024]{1,0:T(8,128)(2,1)S(1)} %constant_dynamic-slice_fusion.4, bf16[128,1024]{1,0:T(8,128)(2,1)S(1)} %constant_dynamic-slice_fusion.5), kind=kLoop, calls=%fused_computation.39 | loop fusion | flops 1048576 | bytes 1048576 | tf_op jit(solution)/shard_map/concatenate | solution.py:142
  14.3 1.5 %collective-permute-start = (bf16[256,1024]{1,0:T(8,128)(2,1)}, bf16[256,1024]{1,0:T(8,128)(2,1)}, u32[]{:S(2)}, u32[]{:S(2)}) collective-permute-start(bf16[256,1024]{1,0:T(8,128)(2,1)} %pad_maximum_fusion.4), channel_id=1, source_target_pairs={{0,1},{1,0},{2,3},{3,2},{4,5},{5,4},{6,7},{7,6},{8,9},{9,8},{10,11... | collective-permute-start | bytes 1572872 | tf_op jit(solution)/shard_map/ppermute | solution.py:306
  15.9 0.6 collective-permute-start.5
  16.5 0.9 %constant_dynamic-slice_fusion = bf16[128,512]{1,0:T(8,128)(2,1)S(1)} fusion(bf16[128,2048]{1,0:T(8,128)(2,1)} %v_own.3, s32[]{:T(128)S(6)} %select_n.123), kind=kLoop, calls=%fused_computation.54 | loop fusion | bytes 262148 | tf_op jit(solution)/shard_map/dynamic_slice | solution.py:142
  17.5 2.8 %collective-permute-start.3 = (bf16[256,512]{1,0:T(8,128)(2,1)S(1)}, bf16[256,512]{1,0:T(8,128)(2,1)S(1)}, u32[]{:S(2)}, u32[]{:S(2)}) collective-permute-start(bf16[256,512]{1,0:T(8,128)(2,1)S(1)} %collective-permute-done.1.kv_other), channel_id=1, source_target_pairs={{0,4},{2,6},{4,8},{6,10},{8,12},{10,14},{12,16},{14,18},{16,20},{1... | collective-permute-start | bytes 786440 | tf_op jit(solution)/shard_map/ppermute | solution.py:315
  20.3 3.4 %collective-permute-start.9 = (bf16[512,512]{1,0:T(8,128)(2,1)S(1)}, bf16[512,512]{1,0:T(8,128)(2,1)S(1)}, u32[]{:S(2)}, u32[]{:S(2)}) collective-permute-start(bf16[512,512]{1,0:T(8,128)(2,1)S(1)} %pad_maximum_fusion.8), channel_id=1, source_target_pairs={{0,4},{2,6},{4,8},{6,10},{8,12},{10,14},{12,16},{14,18},{16,20},{1... | collective-permute-start | bytes 1572872 | tf_op jit(solution)/shard_map/ppermute | solution.py:315
  23.9 2.9 %collective-permute-done.3.kv2_other = bf16[256,512]{1,0:T(8,128)(2,1)S(1)} collective-permute-done((bf16[256,512]{1,0:T(8,128)(2,1)S(1)}, bf16[256,512]{1,0:T(8,128)(2,1)S(1)}, u32[]{:S(2)}, u32[]{:S(2)}) %collective-permute-start.3) | collective-permute-done | bytes 262176 | tf_op jit(solution)/shard_map/ppermute | solution.py:315
  27.1 2.5 %collective-permute-done.qg_other = bf16[256,1024]{1,0:T(8,128)(2,1)} collective-permute-done((bf16[256,1024]{1,0:T(8,128)(2,1)}, bf16[256,1024]{1,0:T(8,128)(2,1)}, u32[]{:S(2)}, u32[]{:S(2)}) %collective-permute-start) | collective-permute-done | bytes 524320 | tf_op jit(solution)/shard_map/ppermute | solution.py:306
  29.7 0.8 copy-done.12
  30.5 8.8 %shard_map.85 = (bf16[128,1024]{1,0:T(8,128)(2,1)S(1)}, bf16[128,1024]{1,0:T(8,128)(2,1)S(1)}, f32[256,512]{1,0:T(8,128)}, f32[256,512]{1,0:T(8,128)}, bf16[256,...) custom-call(s32[1]{0:T(128)} %bitcast.side_ref, ...), custom_call_target="tpu_custom_call" | custom-call | tf_op jit(solution)/shard_map/pallas_call | solution.py:281
  39.3 0.8 %collective-permute-done.5.qg_other = bf16[256,1024]{1,0:T(8,128)(2,1)} collective-permute-done((bf16[256,1024]{1,0:T(8,128)(2,1)S(1)}, bf16[256,1024]{1,0:T(8,128)(2,1)}, u32[]{:S(2)}, u32[]{:S(2)}) %collective-permute-start.5) | collective-permute-done | bytes 524320 | tf_op jit(solution)/shard_map/ppermute | solution.py:306
  40.1 0.5 collective-permute-start.7
  40.6 1.0 %collective-permute-done.6 = bf16[256,512]{1,0:T(8,128)(2,1)S(1)} collective-permute-done((bf16[256,512]{1,0:T(8,128)(2,1)S(1)}, bf16[256,512]{1,0:T(8,128)(2,1)S(1)}, u32[]{:S(2)}, u32[]{:S(2)}) %collective-permute-start.6) | collective-permute-done | bytes 262176 | tf_op jit(solution)/shard_map/ppermute | solution.py:310
  41.6 0.4 collective-permute-done.7
  42.1 0.8 %pad_maximum_fusion.9 = bf16[512,512]{1,0:T(8,128)(2,1)} fusion(bf16[256,512]{1,0:T(8,128)(2,1)S(1)} %broadcast_select_fusion, bf16[256,512]{1,0:T(8,128)(2,1)S(1)} %maximum_select_fusion.1), kind=kLoop, calls=%fused_computation.44 | loop fusion | flops 1048576 | bytes 1048576 | tf_op jit(solution)/shard_map/concatenate | solution.py:361
  42.9 0.1 collective-permute-start.10
  43.1 0.1 fusion.1
  43.1 0.1 fusion.6
  43.3 1.3 %collective-permute-start.14 = (bf16[512,512]{1,0:T(8,128)(2,1)S(1)}, bf16[512,512]{1,0:T(8,128)(2,1)S(1)}, u32[]{:S(2)}, u32[]{:S(2)}) collective-permute-start(bf16[512,512]{1,0:T(8,128)(2,1)S(1)} %pad_maximum_fusion.7), channel_id=1, source_target_pairs={{4,0},{6,2},{8,4},{10,6},{12,8},{14,10},{16,12},{18,14},{20,16},{2... | collective-permute-start | bytes 1572872 | tf_op jit(solution)/shard_map/ppermute | solution.py:315
  44.6 1.8 %collective-permute-start.11 = (bf16[128,1024]{1,0:T(8,128)(2,1)S(1)}, bf16[128,1024]{1,0:T(8,128)(2,1)S(1)}, u32[]{:S(2)}, u32[]{:S(2)}) collective-permute-start(bf16[128,1024]{1,0:T(8,128)(2,1)S(1)} %get-tuple-element.69), channel_id=1, source_target_pairs={{0,1},{1,0},{2,3},{3,2},{4,5},{5,4},{6,7},{7,6},{8,9},{9,8},{10,11... | collective-permute-start | bytes 786440 | tf_op jit(solution)/shard_map/ppermute | solution.py:306
  46.4 8.8 %shard_map.86 = (bf16[128,1024]{1,0:T(8,128)(2,1)S(1)}, bf16[128,1024]{1,0:T(8,128)(2,1)S(1)}, f32[256,512]{1,0:T(8,128)}, f32[256,512]{1,0:T(8,128)}, bf16[256,...) custom-call(s32[1]{0:T(128)} %bitcast.side_ref, ...), custom_call_target="tpu_custom_call" | custom-call | tf_op jit(solution)/shard_map/pallas_call | solution.py:281
  55.2 0.5 collective-permute-start.12
  55.7 0.5 collective-permute-start.15
  56.2 3.2 %collective-permute-done.14 = bf16[512,512]{1,0:T(8,128)(2,1)S(1)} collective-permute-done((bf16[512,512]{1,0:T(8,128)(2,1)S(1)}, bf16[512,512]{1,0:T(8,128)(2,1)S(1)}, u32[]{:S(2)}, u32[]{:S(2)}) %collective-permute-start.14) | collective-permute-done | bytes 524320 | tf_op jit(solution)/shard_map/ppermute | solution.py:315
  59.4 0.1 fusion.4
  59.6 0.1 fusion.11
  59.7 1.3 %collective-permute-start.18 = (bf16[256,512]{1,0:T(8,128)(2,1)S(1)}, bf16[256,512]{1,0:T(8,128)(2,1)S(1)}, u32[]{:S(2)}, u32[]{:S(2)}) collective-permute-start(bf16[256,512]{1,0:T(8,128)(2,1)S(1)} %fusion.11), channel_id=1, source_target_pairs={{4,0},{6,2},{8,4},{10,6},{12,8},{14,10},{16,12},{18,14},{20,16},{2... | collective-permute-start | bytes 786440 | tf_op jit(solution)/shard_map/ppermute | solution.py:315
  61.0 0.1 fusion.9
  61.2 1.8 %collective-permute-start.17 = (bf16[256,512]{1,0:T(8,128)(2,1)S(1)}, bf16[256,512]{1,0:T(8,128)(2,1)S(1)}, u32[]{:S(2)}, u32[]{:S(2)}) collective-permute-start(bf16[256,512]{1,0:T(8,128)(2,1)S(1)} %fusion.9), channel_id=1, source_target_pairs={{0,1},{1,0},{2,3},{3,2},{4,5},{5,4},{6,7},{7,6},{8,9},{9,8},{10,11... | collective-permute-start | bytes 786440 | tf_op jit(solution)/shard_map/ppermute | solution.py:306
  63.0 1.3 %collective-permute-start.16 = (bf16[256,512]{1,0:T(8,128)(2,1)S(1)}, bf16[256,512]{1,0:T(8,128)(2,1)S(1)}, u32[]{:S(2)}, u32[]{:S(2)}) collective-permute-start(bf16[256,512]{1,0:T(8,128)(2,1)S(1)} %fusion.16), channel_id=1, source_target_pairs={{4,0},{6,2},{8,4},{10,6},{12,8},{14,10},{16,12},{18,14},{20,16},{2... | collective-permute-start | bytes 786440 | tf_op jit(solution)/shard_map/ppermute | solution.py:315
  64.3 1.2 %maximum_select_fusion = bf16[128,4096]{1,0:T(8,128)(2,1)} fusion(bf16[128,1024]{1,0:T(8,128)(2,1)S(1)} %collective-permute-done.12, bf16[128,1024]{1,0:T(8,128)(2,1)S(1)} %collective-permute-done.11, bf16[128,1024]{1,0:T(8,128)(2,1)S(1)} %get-tuple-element.77, bf16[128,1024]{1,0:T(8,128)(2,1)S(1)} %get-tuple-element.76, pred[]{:T(512)S(6)} %eq.10), kind=kLoop, calls=%fused_computation | loop fusion | flops 8912896 | bytes 2097153 | tf_op jit(solution)/shard_map/jit(_where)/select_n | solution.py:409
  65.6 5.9 %collective-permute-done.18 = bf16[256,512]{1,0:T(8,128)(2,1)S(1)} collective-permute-done((bf16[256,512]{1,0:T(8,128)(2,1)S(1)}, bf16[256,512]{1,0:T(8,128)(2,1)S(1)}, u32[]{:S(2)}, u32[]{:S(2)}) %collective-permute-start.18) | collective-permute-done | bytes 262176 | tf_op jit(solution)/shard_map/ppermute | solution.py:315
  71.4 0.1 fusion.14
  71.5 1.6 %collective-permute-start.19 = (bf16[256,512]{1,0:T(8,128)(2,1)S(1)}, bf16[256,512]{1,0:T(8,128)(2,1)S(1)}, u32[]{:S(2)}, u32[]{:S(2)}) collective-permute-start(bf16[256,512]{1,0:T(8,128)(2,1)S(1)} %fusion.14), channel_id=1, source_target_pairs={{0,1},{1,0},{2,3},{3,2},{4,5},{5,4},{6,7},{7,6},{8,9},{9,8},{10,11... | collective-permute-start | bytes 786440 | tf_op jit(solution)/shard_map/ppermute | solution.py:306
  73.1 2.8 %collective-permute-done.16 = bf16[256,512]{1,0:T(8,128)(2,1)S(1)} collective-permute-done((bf16[256,512]{1,0:T(8,128)(2,1)S(1)}, bf16[256,512]{1,0:T(8,128)(2,1)S(1)}, u32[]{:S(2)}, u32[]{:S(2)}) %collective-permute-start.16) | collective-permute-done | bytes 262176 | tf_op jit(solution)/shard_map/ppermute | solution.py:315
  75.9 0.1 fusion.19
  76.1 0.3 fusion.25
  76.4 1.6 %collective-permute-done.19 = bf16[256,512]{1,0:T(8,128)(2,1)S(1)} collective-permute-done((bf16[256,512]{1,0:T(8,128)(2,1)S(1)}, bf16[256,512]{1,0:T(8,128)(2,1)S(1)}, u32[]{:S(2)}, u32[]{:S(2)}) %collective-permute-start.19) | collective-permute-done | bytes 262176 | tf_op jit(solution)/shard_map/ppermute | solution.py:306
  78.0 0.8 copy-done.10
  78.8 0.2 copy-done.11
  (68 shorter events, 1.0 us)
Async XLA Ops:
  0.6 4.7 %copy-start.2 = (bf16[128,2048]{1,0:T(8,128)(2,1)S(1)}, bf16[128,2048]{1,0:T(8,128)(2,1)}, u32[]{:S(2)}) copy-start(bf16[128,2048]{1,0:T(8,128)(2,1)} %k_own.3) | copy-start | bytes 1572868
  2.4 15.0 %collective-permute-start.1 = (bf16[256,512]{1,0:T(8,128)(2,1)}, bf16[256,512]{1,0:T(8,128)(2,1)S(1)}, u32[]{:S(2)}, u32[]{:S(2)}) collective-permute-start(bf16[256,512]{1,0:T(8,128)(2,1)} %pad_maximum_fusion.10), channel_id=1, source_target_pairs={{0,1},{1,0},{2,3},{3,2},{4,5},{5,4},{6,7},{7,6},{8,9},{9,8},{10,11... | collective-permute-start | bytes 786440 | tf_op jit(solution)/shard_map/ppermute | solution.py:306
  5.4 8.0 %copy-start = (bf16[128,4096]{1,0:T(8,128)(2,1)S(1)}, bf16[128,4096]{1,0:T(8,128)(2,1)}, u32[]{:S(2)}) copy-start(bf16[128,4096]{1,0:T(8,128)(2,1)} %q_own.3) | copy-start | bytes 3145732
  6.4 7.0 %copy-start.1 = (bf16[128,4096]{1,0:T(8,128)(2,1)S(1)}, bf16[128,4096]{1,0:T(8,128)(2,1)}, u32[]{:S(2)}) copy-start(bf16[128,4096]{1,0:T(8,128)(2,1)} %g_own.3) | copy-start | bytes 3145732
  7.1 13.1 %collective-permute-start.8 = (bf16[256,512]{1,0:T(8,128)(2,1)}, bf16[256,512]{1,0:T(8,128)(2,1)S(1)}, u32[]{:S(2)}, u32[]{:S(2)}) collective-permute-start(bf16[256,512]{1,0:T(8,128)(2,1)} %pad_maximum_fusion.11), channel_id=1, source_target_pairs={{0,1},{1,0},{2,3},{3,2},{4,5},{5,4},{6,7},{7,6},{8,9},{9,8},{10,11... | collective-permute-start | bytes 786440 | tf_op jit(solution)/shard_map/ppermute | solution.py:306
  8.8 15.0 %collective-permute-start.2 = (bf16[256,512]{1,0:T(8,128)(2,1)}, bf16[256,512]{1,0:T(8,128)(2,1)}, u32[]{:S(2)}, u32[]{:S(2)}) collective-permute-start(bf16[256,512]{1,0:T(8,128)(2,1)} %pad_maximum_fusion.12), channel_id=1, source_target_pairs={{0,4},{2,6},{4,8},{6,10},{8,12},{10,14},{12,16},{14,18},{16,20},{1... | collective-permute-start | bytes 786440 | tf_op jit(solution)/shard_map/ppermute | solution.py:315
  14.3 15.4 %collective-permute-start = (bf16[256,1024]{1,0:T(8,128)(2,1)}, bf16[256,1024]{1,0:T(8,128)(2,1)}, u32[]{:S(2)}, u32[]{:S(2)}) collective-permute-start(bf16[256,1024]{1,0:T(8,128)(2,1)} %pad_maximum_fusion.4), channel_id=1, source_target_pairs={{0,1},{1,0},{2,3},{3,2},{4,5},{5,4},{6,7},{7,6},{8,9},{9,8},{10,11... | collective-permute-start | bytes 1572872 | tf_op jit(solution)/shard_map/ppermute | solution.py:306
  15.9 24.2 %collective-permute-start.5 = (bf16[256,1024]{1,0:T(8,128)(2,1)S(1)}, bf16[256,1024]{1,0:T(8,128)(2,1)}, u32[]{:S(2)}, u32[]{:S(2)}) collective-permute-start(bf16[256,1024]{1,0:T(8,128)(2,1)S(1)} %pad_maximum_fusion.6), channel_id=1, source_target_pairs={{0,1},{1,0},{2,3},{3,2},{4,5},{5,4},{6,7},{7,6},{8,9},{9,8},{10,11... | collective-permute-start | bytes 1572872 | tf_op jit(solution)/shard_map/ppermute | solution.py:306
  17.5 9.4 %collective-permute-start.3 = (bf16[256,512]{1,0:T(8,128)(2,1)S(1)}, bf16[256,512]{1,0:T(8,128)(2,1)S(1)}, u32[]{:S(2)}, u32[]{:S(2)}) collective-permute-start(bf16[256,512]{1,0:T(8,128)(2,1)S(1)} %collective-permute-done.1.kv_other), channel_id=1, source_target_pairs={{0,4},{2,6},{4,8},{6,10},{8,12},{10,14},{12,16},{14,18},{16,20},{1... | collective-permute-start | bytes 786440 | tf_op jit(solution)/shard_map/ppermute | solution.py:315
  20.3 20.3 %collective-permute-start.9 = (bf16[512,512]{1,0:T(8,128)(2,1)S(1)}, bf16[512,512]{1,0:T(8,128)(2,1)S(1)}, u32[]{:S(2)}, u32[]{:S(2)}) collective-permute-start(bf16[512,512]{1,0:T(8,128)(2,1)S(1)} %pad_maximum_fusion.8), channel_id=1, source_target_pairs={{0,4},{2,6},{4,8},{6,10},{8,12},{10,14},{12,16},{14,18},{16,20},{1... | collective-permute-start | bytes 1572872 | tf_op jit(solution)/shard_map/ppermute | solution.py:315
  23.9 3.1 %copy-start.13 = (s32[2,6]{1,0:T(2,128)S(1)}, s32[2,6]{1,0:T(2,128)}, u32[]{:S(2)}) copy-start(s32[2,6]{1,0:T(2,128)} %param.11) | copy-start | bytes 148
  23.9 3.1 %copy-start.14 = (s32[2,6]{1,0:T(2,128)S(1)}, s32[2,6]{1,0:T(2,128)}, u32[]{:S(2)}) copy-start(s32[2,6]{1,0:T(2,128)} %param.10) | copy-start | bytes 148
  26.8 2.8 %copy-start.5 = (bf16[256,512]{1,0:T(8,128)(2,1)}, bf16[256,512]{1,0:T(8,128)(2,1)S(1)}, u32[]{:S(2)}) copy-start(bf16[256,512]{1,0:T(8,128)(2,1)S(1)} %collective-permute-done.3.kv2_other) | copy-start | bytes 786436
  26.9 2.7 %collective-permute-start.4 = (bf16[512,512]{1,0:T(8,128)(2,1)S(1)}, bf16[512,512]{1,0:T(8,128)(2,1)S(1)}, u32[]{:S(2)}, u32[]{:S(2)}) collective-permute-start(bf16[512,512]{1,0:T(8,128)(2,1)S(1)} %pad_maximum_fusion.5), channel_id=1, source_target_pairs={{0,2},{2,0},{4,6},{6,4},{8,10},{10,8},{12,14},{14,12},{16,18},{18,... | collective-permute-start | bytes 1572872 | tf_op jit(solution)/shard_map/ppermute | solution.py:310
  29.7 0.8 %copy-start.12 = (bf16[512,512]{1,0:T(8,128)(2,1)}, bf16[512,512]{1,0:T(8,128)(2,1)S(1)}, u32[]{:S(2)}) copy-start(bf16[512,512]{1,0:T(8,128)(2,1)S(1)} %collective-permute-done.4.kv1) | copy-start | bytes 1572868
  40.1 1.5 %collective-permute-start.6 = (bf16[256,512]{1,0:T(8,128)(2,1)S(1)}, bf16[256,512]{1,0:T(8,128)(2,1)S(1)}, u32[]{:S(2)}, u32[]{:S(2)}) collective-permute-start(bf16[256,512]{1,0:T(8,128)(2,1)S(1)} %get-tuple-element.60), channel_id=1, source_target_pairs={{0,2},{2,0},{4,6},{6,4},{8,10},{10,8},{12,14},{14,12},{16,18},{18,... | collective-permute-start | bytes 786440 | tf_op jit(solution)/shard_map/ppermute | solution.py:310
  40.1 1.9 %collective-permute-start.7 = (bf16[256,512]{1,0:T(8,128)(2,1)S(1)}, bf16[256,512]{1,0:T(8,128)(2,1)S(1)}, u32[]{:S(2)}, u32[]{:S(2)}) collective-permute-start(bf16[256,512]{1,0:T(8,128)(2,1)S(1)} %get-tuple-element.62), channel_id=1, source_target_pairs={{0,2},{2,0},{4,6},{6,4},{8,10},{10,8},{12,14},{14,12},{16,18},{18,... | collective-permute-start | bytes 786440 | tf_op jit(solution)/shard_map/ppermute | solution.py:310
  40.6 2.3 %copy-start.3 = (bf16[256,512]{1,0:T(8,128)(2,1)}, bf16[256,512]{1,0:T(8,128)(2,1)S(1)}, u32[]{:S(2)}) copy-start(bf16[256,512]{1,0:T(8,128)(2,1)S(1)} %get-tuple-element.67.kv2_other) | copy-start | bytes 786436
  40.6 2.3 %copy-start.4 = (bf16[256,512]{1,0:T(8,128)(2,1)}, bf16[256,512]{1,0:T(8,128)(2,1)S(1)}, u32[]{:S(2)}) copy-start(bf16[256,512]{1,0:T(8,128)(2,1)S(1)} %get-tuple-element.66.kv2_own) | copy-start | bytes 786436
  42.9 3.5 %collective-permute-start.10 = (bf16[512,512]{1,0:T(8,128)(2,1)}, bf16[512,512]{1,0:T(8,128)(2,1)}, u32[]{:S(2)}, u32[]{:S(2)}) collective-permute-start(bf16[512,512]{1,0:T(8,128)(2,1)} %pad_maximum_fusion.9), channel_id=1, source_target_pairs={{0,2},{2,0},{4,6},{6,4},{8,10},{10,8},{12,14},{14,12},{16,18},{18,... | collective-permute-start | bytes 1572872 | tf_op jit(solution)/shard_map/ppermute | solution.py:310
  43.3 16.1 %collective-permute-start.14 = (bf16[512,512]{1,0:T(8,128)(2,1)S(1)}, bf16[512,512]{1,0:T(8,128)(2,1)S(1)}, u32[]{:S(2)}, u32[]{:S(2)}) collective-permute-start(bf16[512,512]{1,0:T(8,128)(2,1)S(1)} %pad_maximum_fusion.7), channel_id=1, source_target_pairs={{4,0},{6,2},{8,4},{10,6},{12,8},{14,10},{16,12},{18,14},{20,16},{2... | collective-permute-start | bytes 1572872 | tf_op jit(solution)/shard_map/ppermute | solution.py:315
  44.6 14.8 %copy-start.7 = (f32[256,512]{1,0:T(8,128)S(1)}, f32[256,512]{1,0:T(8,128)}, u32[]{:S(2)}) copy-start(f32[256,512]{1,0:T(8,128)} %get-tuple-element.80) | copy-start | bytes 1572868
  44.6 19.7 %collective-permute-start.11 = (bf16[128,1024]{1,0:T(8,128)(2,1)S(1)}, bf16[128,1024]{1,0:T(8,128)(2,1)S(1)}, u32[]{:S(2)}, u32[]{:S(2)}) collective-permute-start(bf16[128,1024]{1,0:T(8,128)(2,1)S(1)} %get-tuple-element.69), channel_id=1, source_target_pairs={{0,1},{1,0},{2,3},{3,2},{4,5},{5,4},{6,7},{7,6},{8,9},{9,8},{10,11... | collective-permute-start | bytes 786440 | tf_op jit(solution)/shard_map/ppermute | solution.py:306
  55.2 9.1 %collective-permute-start.12 = (bf16[128,1024]{1,0:T(8,128)(2,1)S(1)}, bf16[128,1024]{1,0:T(8,128)(2,1)S(1)}, u32[]{:S(2)}, u32[]{:S(2)}) collective-permute-start(bf16[128,1024]{1,0:T(8,128)(2,1)S(1)} %get-tuple-element.70), channel_id=1, source_target_pairs={{0,1},{1,0},{2,3},{3,2},{4,5},{5,4},{6,7},{7,6},{8,9},{9,8},{10,11... | collective-permute-start | bytes 786440 | tf_op jit(solution)/shard_map/ppermute | solution.py:306
  55.7 3.9 %collective-permute-start.13 = (bf16[256,512]{1,0:T(8,128)(2,1)S(1)}, bf16[256,512]{1,0:T(8,128)(2,1)S(1)}, u32[]{:S(2)}, u32[]{:S(2)}) collective-permute-start(bf16[256,512]{1,0:T(8,128)(2,1)S(1)} %get-tuple-element.72), channel_id=1, source_target_pairs={{0,2},{2,0},{4,6},{6,4},{8,10},{10,8},{12,14},{14,12},{16,18},{18,... | collective-permute-start | bytes 786440 | tf_op jit(solution)/shard_map/ppermute | solution.py:310
  55.7 7.2 %collective-permute-start.15 = (bf16[256,512]{1,0:T(8,128)(2,1)S(1)}, bf16[256,512]{1,0:T(8,128)(2,1)S(1)}, u32[]{:S(2)}, u32[]{:S(2)}) collective-permute-start(bf16[256,512]{1,0:T(8,128)(2,1)S(1)} %get-tuple-element.75), channel_id=1, source_target_pairs={{0,2},{2,0},{4,6},{6,4},{8,10},{10,8},{12,14},{14,12},{16,18},{18,... | collective-permute-start | bytes 786440 | tf_op jit(solution)/shard_map/ppermute | solution.py:310
  59.5 1.5 %copy-start.6 = (f32[256,512]{1,0:T(8,128)S(1)}, f32[256,512]{1,0:T(8,128)}, u32[]{:S(2)}) copy-start(f32[256,512]{1,0:T(8,128)} %get-tuple-element.82) | copy-start | bytes 1572868
  59.7 11.7 %collective-permute-start.18 = (bf16[256,512]{1,0:T(8,128)(2,1)S(1)}, bf16[256,512]{1,0:T(8,128)(2,1)S(1)}, u32[]{:S(2)}, u32[]{:S(2)}) collective-permute-start(bf16[256,512]{1,0:T(8,128)(2,1)S(1)} %fusion.11), channel_id=1, source_target_pairs={{4,0},{6,2},{8,4},{10,6},{12,8},{14,10},{16,12},{18,14},{20,16},{2... | collective-permute-start | bytes 786440 | tf_op jit(solution)/shard_map/ppermute | solution.py:315
  61.2 14.9 %collective-permute-start.17 = (bf16[256,512]{1,0:T(8,128)(2,1)S(1)}, bf16[256,512]{1,0:T(8,128)(2,1)S(1)}, u32[]{:S(2)}, u32[]{:S(2)}) collective-permute-start(bf16[256,512]{1,0:T(8,128)(2,1)S(1)} %fusion.9), channel_id=1, source_target_pairs={{0,1},{1,0},{2,3},{3,2},{4,5},{5,4},{6,7},{7,6},{8,9},{9,8},{10,11... | collective-permute-start | bytes 786440 | tf_op jit(solution)/shard_map/ppermute | solution.py:306
  63.0 12.9 %collective-permute-start.16 = (bf16[256,512]{1,0:T(8,128)(2,1)S(1)}, bf16[256,512]{1,0:T(8,128)(2,1)S(1)}, u32[]{:S(2)}, u32[]{:S(2)}) collective-permute-start(bf16[256,512]{1,0:T(8,128)(2,1)S(1)} %fusion.16), channel_id=1, source_target_pairs={{4,0},{6,2},{8,4},{10,6},{12,8},{14,10},{16,12},{18,14},{20,16},{2... | collective-permute-start | bytes 786440 | tf_op jit(solution)/shard_map/ppermute | solution.py:315
  64.3 7.1 %copy-start.9 = (f32[256,512]{1,0:T(8,128)S(1)}, f32[256,512]{1,0:T(8,128)}, u32[]{:S(2)}) copy-start(f32[256,512]{1,0:T(8,128)} %get-tuple-element.85) | copy-start | bytes 1572868
  65.6 10.3 %copy-start.8 = (f32[256,512]{1,0:T(8,128)S(1)}, f32[256,512]{1,0:T(8,128)}, u32[]{:S(2)}) copy-start(f32[256,512]{1,0:T(8,128)} %get-tuple-element.81) | copy-start | bytes 1572868
  71.5 6.4 %collective-permute-start.19 = (bf16[256,512]{1,0:T(8,128)(2,1)S(1)}, bf16[256,512]{1,0:T(8,128)(2,1)S(1)}, u32[]{:S(2)}, u32[]{:S(2)}) collective-permute-start(bf16[256,512]{1,0:T(8,128)(2,1)S(1)} %fusion.14), channel_id=1, source_target_pairs={{0,1},{1,0},{2,3},{3,2},{4,5},{5,4},{6,7},{7,6},{8,9},{9,8},{10,11... | collective-permute-start | bytes 786440 | tf_op jit(solution)/shard_map/ppermute | solution.py:306
  78.0 0.8 %copy-start.10 = (bf16[128,2048]{1,0:T(8,128)(2,1)}, bf16[128,2048]{1,0:T(8,128)(2,1)S(1)}, u32[]{:S(2)}) copy-start(bf16[128,2048]{1,0:T(8,128)(2,1)S(1)} %get-tuple-element.91) | copy-start | bytes 1572868
  78.0 1.0 %copy-start.11 = (bf16[128,2048]{1,0:T(8,128)(2,1)}, bf16[128,2048]{1,0:T(8,128)(2,1)S(1)}, u32[]{:S(2)}) copy-start(bf16[128,2048]{1,0:T(8,128)(2,1)S(1)} %get-tuple-element.92) | copy-start | bytes 1572868

commit v7 on v5

--- a/solution.py
+++ b/solution.py
@@ -383,6 +383,7 @@
 
     dq_own0, dq_away0, e0_own, e0_other, e1_own, e1_other, e2_own, e2_other = attended(0)
     e1_own, e1_other = after([e1_own, e1_other], qg_other[1])
+    e1_own, e1_other = after([e1_own, e1_other], late)
     dq_other0 = swap(dq_away0)
     e1_own, e1_other = mate(e1_own), mate(e1_other)
     ship0 = [jnp.concatenate([back_sum(e2_own, e1_own), back_sum(e2_other, e1_other)], axis=0)]

time: 79.4 us -> 79.4 us (level)
  no operation moved by 1% of the time
where the time goes in v7:
time: 79.4 us; the launch traced here: 79 us
  starting transfers between devices  26.7 us (34%)
  waiting for transfers between devices  20.1 us (25%)
  Pallas kernels  18.5 us (23%)
  other arithmetic  6.57 us (8%)
  local copies, waits for them, and re-layouts  5.97 us (8%)
  between operations  1.1 us (1%)
    pallas_call x2, Pallas kernels, attend(): pl.pallas_call(attend_kernel, grid_spec=pltpu.PrefetchScalarGridSpec(num_...  18.5 us
    ppermute x6, starting transfers between devices, moved(): lax.ppermute(block, 'tm', [(i, i + distance) for i in range(size) if 0 <=...  14.7 us
    ppermute x6, waiting for transfers between devices, moved(): lax.ppermute(block, 'tm', [(i, i + distance) for i in range(size) if 0 <=...  14.2 us
    ppermute x8, starting transfers between devices, swap(): return lax.ppermute(block, 'space', [(0, 1), (1, 0)])  10.8 us
    ppermute x8, waiting for transfers between devices, swap(): return lax.ppermute(block, 'space', [(0, 1), (1, 0)])  4.62 us
    dynamic_slice x11, local copies, waits for them, and re-layouts, packed(): lax.dynamic_slice_in_dim(a, start, width, 1)  4.01 us
    concatenate x5, other arithmetic, packed(): jnp.concatenate([lax.dynamic_slice_in_dim(a, start, width, 1) for a in ar...  3.02 us
    unnamed x30, local copies, waits for them, and re-layouts  1.8 us
  transfers between devices with their start and end apart: 20, of which 10 were waited for; matrix products, arithmetic and copies ran while one was open for 10% of the time, Pallas kernels for 23%

profile of v7, /device:TPU:0, one launch (start us, length us, event | category | flops | bytes accessed | tf_op | source)
XLA Modules:
  0.0 79.0 jit_solution(18367957094391982414)
XLA Ops:
  0.6 1.0 %constant_dynamic-slice_fusion.10 = (bf16[128,512]{1,0:T(8,128)(2,1)S(1)}, bf16[128,512]{1,0:T(8,128)(2,1)S(1)}) fusion(bf16[128,2048]{1,0:T(8,128)(2,1)} %v_own.3, s32[]{:T(128)S(6)} %select_n.112, bf16[128,2048]{1,0:T(8,128)(2,1)} %k_own.3), kind=kLoop, calls=%fused_computation.64 | loop fusion | bytes 524292 | tf_op jit(solution)/shard_map/dynamic_slice | solution.py:142
  1.7 0.7 pad_maximum_fusion.10
  2.4 2.9 %collective-permute-start.1 = (bf16[256,512]{1,0:T(8,128)(2,1)}, bf16[256,512]{1,0:T(8,128)(2,1)S(1)}, u32[]{:S(2)}, u32[]{:S(2)}) collective-permute-start(bf16[256,512]{1,0:T(8,128)(2,1)} %pad_maximum_fusion.10), channel_id=1, source_target_pairs={{0,1},{1,0},{2,3},{3,2},{4,5},{5,4},{6,7},{7,6},{8,9},{9,8},{10,11... | collective-permute-start | bytes 786440 | tf_op jit(solution)/shard_map/ppermute | solution.py:306
  5.4 1.0 %constant_dynamic-slice_fusion.8 = bf16[128,512]{1,0:T(8,128)(2,1)S(1)} fusion(bf16[128,2048]{1,0:T(8,128)(2,1)} %v_own.3, s32[]{:T(128)S(6)} %select_n.113), kind=kLoop, calls=%fused_computation.62 | loop fusion | bytes 262148 | tf_op jit(solution)/shard_map/dynamic_slice | solution.py:142
  6.4 0.7 pad_maximum_fusion.11
  7.1 0.9 %constant_dynamic-slice_fusion.6 = bf16[128,512]{1,0:T(8,128)(2,1)S(1)} fusion(bf16[128,2048]{1,0:T(8,128)(2,1)} %v_own.3, s32[]{:T(128)S(6)} %select_n.114), kind=kLoop, calls=%fused_computation.60 | loop fusion | bytes 262148 | tf_op jit(solution)/shard_map/dynamic_slice | solution.py:142
  8.1 0.7 pad_maximum_fusion.12
  8.8 4.6 %collective-permute-start.2 = (bf16[256,512]{1,0:T(8,128)(2,1)}, bf16[256,512]{1,0:T(8,128)(2,1)}, u32[]{:S(2)}, u32[]{:S(2)}) collective-permute-start(bf16[256,512]{1,0:T(8,128)(2,1)} %pad_maximum_fusion.12), channel_id=1, source_target_pairs={{0,4},{2,6},{4,8},{6,10},{8,12},{10,14},{12,16},{14,18},{16,20},{1... | collective-permute-start | bytes 786440 | tf_op jit(solution)/shard_map/ppermute | solution.py:315
  13.5 0.8 %pad_maximum_fusion.4 = bf16[256,1024]{1,0:T(8,128)(2,1)} fusion(bf16[128,1024]{1,0:T(8,128)(2,1)S(1)} %constant_dynamic-slice_fusion.4, bf16[128,1024]{1,0:T(8,128)(2,1)S(1)} %constant_dynamic-slice_fusion.5), kind=kLoop, calls=%fused_computation.39 | loop fusion | flops 1048576 | bytes 1048576 | tf_op jit(solution)/shard_map/concatenate | solution.py:142
  14.3 1.5 %collective-permute-start = (bf16[256,1024]{1,0:T(8,128)(2,1)}, bf16[256,1024]{1,0:T(8,128)(2,1)}, u32[]{:S(2)}, u32[]{:S(2)}) collective-permute-start(bf16[256,1024]{1,0:T(8,128)(2,1)} %pad_maximum_fusion.4), channel_id=1, source_target_pairs={{0,1},{1,0},{2,3},{3,2},{4,5},{5,4},{6,7},{7,6},{8,9},{9,8},{10,11... | collective-permute-start | bytes 1572872 | tf_op jit(solution)/shard_map/ppermute | solution.py:306
  15.9 0.6 collective-permute-start.5
  16.5 0.9 %constant_dynamic-slice_fusion = bf16[128,512]{1,0:T(8,128)(2,1)S(1)} fusion(bf16[128,2048]{1,0:T(8,128)(2,1)} %v_own.3, s32[]{:T(128)S(6)} %select_n.121), kind=kLoop, calls=%fused_computation.54 | loop fusion | bytes 262148 | tf_op jit(solution)/shard_map/dynamic_slice | solution.py:142
  17.5 2.8 %collective-permute-start.3 = (bf16[256,512]{1,0:T(8,128)(2,1)S(1)}, bf16[256,512]{1,0:T(8,128)(2,1)S(1)}, u32[]{:S(2)}, u32[]{:S(2)}) collective-permute-start(bf16[256,512]{1,0:T(8,128)(2,1)S(1)} %collective-permute-done.1.kv_other), channel_id=1, source_target_pairs={{0,4},{2,6},{4,8},{6,10},{8,12},{10,14},{12,16},{14,18},{16,20},{1... | collective-permute-start | bytes 786440 | tf_op jit(solution)/shard_map/ppermute | solution.py:315
  20.3 3.4 %collective-permute-start.7 = (bf16[512,512]{1,0:T(8,128)(2,1)S(1)}, bf16[512,512]{1,0:T(8,128)(2,1)S(1)}, u32[]{:S(2)}, u32[]{:S(2)}) collective-permute-start(bf16[512,512]{1,0:T(8,128)(2,1)S(1)} %pad_maximum_fusion.7), channel_id=1, source_target_pairs={{0,4},{2,6},{4,8},{6,10},{8,12},{10,14},{12,16},{14,18},{16,20},{1... | collective-permute-start | bytes 1572872 | tf_op jit(solution)/shard_map/ppermute | solution.py:315
  23.9 2.9 %collective-permute-done.3.kv2_other = bf16[256,512]{1,0:T(8,128)(2,1)S(1)} collective-permute-done((bf16[256,512]{1,0:T(8,128)(2,1)S(1)}, bf16[256,512]{1,0:T(8,128)(2,1)S(1)}, u32[]{:S(2)}, u32[]{:S(2)}) %collective-permute-start.3) | collective-permute-done | bytes 262176 | tf_op jit(solution)/shard_map/ppermute | solution.py:315
  27.1 2.5 %collective-permute-done.qg_other = bf16[256,1024]{1,0:T(8,128)(2,1)} collective-permute-done((bf16[256,1024]{1,0:T(8,128)(2,1)}, bf16[256,1024]{1,0:T(8,128)(2,1)}, u32[]{:S(2)}, u32[]{:S(2)}) %collective-permute-start) | collective-permute-done | bytes 524320 | tf_op jit(solution)/shard_map/ppermute | solution.py:306
  29.7 0.8 copy-done.12
  30.5 9.3 %shard_map.85 = (bf16[128,1024]{1,0:T(8,128)(2,1)S(1)}, bf16[128,1024]{1,0:T(8,128)(2,1)S(1)}, f32[256,512]{1,0:T(8,128)}, f32[256,512]{1,0:T(8,128)}, bf16[256,...) custom-call(s32[1]{0:T(128)} %bitcast.side_ref, ...), custom_call_target="tpu_custom_call" | custom-call | tf_op jit(solution)/shard_map/pallas_call | solution.py:281
  39.7 0.3 collective-permute-done.5.qg_other
  40.1 0.5 collective-permute-start.9
  40.6 1.0 %collective-permute-done.8 = bf16[256,512]{1,0:T(8,128)(2,1)S(1)} collective-permute-done((bf16[256,512]{1,0:T(8,128)(2,1)S(1)}, bf16[256,512]{1,0:T(8,128)(2,1)S(1)}, u32[]{:S(2)}, u32[]{:S(2)}) %collective-permute-start.8) | collective-permute-done | bytes 262176 | tf_op jit(solution)/shard_map/ppermute | solution.py:310
  41.6 0.4 collective-permute-done.9
  42.1 0.8 %pad_maximum_fusion.9 = bf16[512,512]{1,0:T(8,128)(2,1)} fusion(bf16[256,512]{1,0:T(8,128)(2,1)S(1)} %broadcast_select_fusion, bf16[256,512]{1,0:T(8,128)(2,1)S(1)} %maximum_select_fusion.1), kind=kLoop, calls=%fused_computation.44 | loop fusion | flops 1048576 | bytes 1048576 | tf_op jit(solution)/shard_map/concatenate | solution.py:361
  42.9 0.1 collective-permute-start.10
  43.1 0.1 fusion.6
  43.3 1.3 %collective-permute-start.14 = (bf16[512,512]{1,0:T(8,128)(2,1)S(1)}, bf16[512,512]{1,0:T(8,128)(2,1)S(1)}, u32[]{:S(2)}, u32[]{:S(2)}) collective-permute-start(bf16[512,512]{1,0:T(8,128)(2,1)S(1)} %pad_maximum_fusion.8), channel_id=1, source_target_pairs={{4,0},{6,2},{8,4},{10,6},{12,8},{14,10},{16,12},{18,14},{20,16},{2... | collective-permute-start | bytes 1572872 | tf_op jit(solution)/shard_map/ppermute | solution.py:315
  44.6 1.9 %collective-permute-start.11 = (bf16[128,1024]{1,0:T(8,128)(2,1)S(1)}, bf16[128,1024]{1,0:T(8,128)(2,1)S(1)}, u32[]{:S(2)}, u32[]{:S(2)}) collective-permute-start(bf16[128,1024]{1,0:T(8,128)(2,1)S(1)} %get-tuple-element.73), channel_id=1, source_target_pairs={{0,1},{1,0},{2,3},{3,2},{4,5},{5,4},{6,7},{7,6},{8,9},{9,8},{10,11... | collective-permute-start | bytes 786440 | tf_op jit(solution)/shard_map/ppermute | solution.py:306
  46.5 9.3 %shard_map.86 = (bf16[128,1024]{1,0:T(8,128)(2,1)S(1)}, bf16[128,1024]{1,0:T(8,128)(2,1)S(1)}, f32[256,512]{1,0:T(8,128)}, f32[256,512]{1,0:T(8,128)}, bf16[256,...) custom-call(s32[1]{0:T(128)} %bitcast.side_ref, ...), custom_call_target="tpu_custom_call" | custom-call | tf_op jit(solution)/shard_map/pallas_call | solution.py:281
  55.7 0.5 collective-permute-start.12
  56.3 0.5 collective-permute-start.15
  56.8 2.7 %collective-permute-done.14 = bf16[512,512]{1,0:T(8,128)(2,1)S(1)} collective-permute-done((bf16[512,512]{1,0:T(8,128)(2,1)S(1)}, bf16[512,512]{1,0:T(8,128)(2,1)S(1)}, u32[]{:S(2)}, u32[]{:S(2)}) %collective-permute-start.14) | collective-permute-done | bytes 524320 | tf_op jit(solution)/shard_map/ppermute | solution.py:315
  59.5 0.1 fusion.4
  59.7 0.1 fusion.11
  59.8 1.3 %collective-permute-start.18 = (bf16[256,512]{1,0:T(8,128)(2,1)S(1)}, bf16[256,512]{1,0:T(8,128)(2,1)S(1)}, u32[]{:S(2)}, u32[]{:S(2)}) collective-permute-start(bf16[256,512]{1,0:T(8,128)(2,1)S(1)} %fusion.11), channel_id=1, source_target_pairs={{4,0},{6,2},{8,4},{10,6},{12,8},{14,10},{16,12},{18,14},{20,16},{2... | collective-permute-start | bytes 786440 | tf_op jit(solution)/shard_map/ppermute | solution.py:315
  61.1 0.1 fusion.9
  61.2 1.8 %collective-permute-start.17 = (bf16[256,512]{1,0:T(8,128)(2,1)S(1)}, bf16[256,512]{1,0:T(8,128)(2,1)S(1)}, u32[]{:S(2)}, u32[]{:S(2)}) collective-permute-start(bf16[256,512]{1,0:T(8,128)(2,1)S(1)} %fusion.9), channel_id=1, source_target_pairs={{0,1},{1,0},{2,3},{3,2},{4,5},{5,4},{6,7},{7,6},{8,9},{9,8},{10,11... | collective-permute-start | bytes 786440 | tf_op jit(solution)/shard_map/ppermute | solution.py:306
  63.1 1.3 %collective-permute-start.16 = (bf16[256,512]{1,0:T(8,128)(2,1)S(1)}, bf16[256,512]{1,0:T(8,128)(2,1)S(1)}, u32[]{:S(2)}, u32[]{:S(2)}) collective-permute-start(bf16[256,512]{1,0:T(8,128)(2,1)S(1)} %fusion.16), channel_id=1, source_target_pairs={{4,0},{6,2},{8,4},{10,6},{12,8},{14,10},{16,12},{18,14},{20,16},{2... | collective-permute-start | bytes 786440 | tf_op jit(solution)/shard_map/ppermute | solution.py:315
  64.4 0.1 collective-permute-done.12
  64.5 1.2 %maximum_select_fusion = bf16[128,4096]{1,0:T(8,128)(2,1)} fusion(bf16[128,1024]{1,0:T(8,128)(2,1)S(1)} %collective-permute-done.12, bf16[128,1024]{1,0:T(8,128)(2,1)S(1)} %collective-permute-done.11, bf16[128,1024]{1,0:T(8,128)(2,1)S(1)} %get-tuple-element.81, bf16[128,1024]{1,0:T(8,128)(2,1)S(1)} %get-tuple-element.80, pred[]{:T(512)S(6)} %eq.10), kind=kLoop, calls=%fused_computation | loop fusion | flops 8912896 | bytes 2097153 | tf_op jit(solution)/shard_map/jit(_where)/select_n | solution.py:410
  65.7 5.7 %collective-permute-done.18 = bf16[256,512]{1,0:T(8,128)(2,1)S(1)} collective-permute-done((bf16[256,512]{1,0:T(8,128)(2,1)S(1)}, bf16[256,512]{1,0:T(8,128)(2,1)S(1)}, u32[]{:S(2)}, u32[]{:S(2)}) %collective-permute-start.18) | collective-permute-done | bytes 262176 | tf_op jit(solution)/shard_map/ppermute | solution.py:315
  71.5 0.1 fusion.14
  71.6 1.6 %collective-permute-start.19 = (bf16[256,512]{1,0:T(8,128)(2,1)S(1)}, bf16[256,512]{1,0:T(8,128)(2,1)S(1)}, u32[]{:S(2)}, u32[]{:S(2)}) collective-permute-start(bf16[256,512]{1,0:T(8,128)(2,1)S(1)} %fusion.14), channel_id=1, source_target_pairs={{0,1},{1,0},{2,3},{3,2},{4,5},{5,4},{6,7},{7,6},{8,9},{9,8},{10,11... | collective-permute-start | bytes 786440 | tf_op jit(solution)/shard_map/ppermute | solution.py:306
  73.1 2.8 %collective-permute-done.16 = bf16[256,512]{1,0:T(8,128)(2,1)S(1)} collective-permute-done((bf16[256,512]{1,0:T(8,128)(2,1)S(1)}, bf16[256,512]{1,0:T(8,128)(2,1)S(1)}, u32[]{:S(2)}, u32[]{:S(2)}) %collective-permute-start.16) | collective-permute-done | bytes 262176 | tf_op jit(solution)/shard_map/ppermute | solution.py:315
  75.9 0.1 fusion.19
  76.2 0.3 fusion.25
  76.5 1.6 %collective-permute-done.19 = bf16[256,512]{1,0:T(8,128)(2,1)S(1)} collective-permute-done((bf16[256,512]{1,0:T(8,128)(2,1)S(1)}, bf16[256,512]{1,0:T(8,128)(2,1)S(1)}, u32[]{:S(2)}, u32[]{:S(2)}) %collective-permute-start.19) | collective-permute-done | bytes 262176 | tf_op jit(solution)/shard_map/ppermute | solution.py:306
  78.1 0.8 copy-done.10
  78.9 0.2 copy-done.11
  (68 shorter events, 1.0 us)
Async XLA Ops:
  0.6 4.7 %copy-start.2 = (bf16[128,2048]{1,0:T(8,128)(2,1)S(1)}, bf16[128,2048]{1,0:T(8,128)(2,1)}, u32[]{:S(2)}) copy-start(bf16[128,2048]{1,0:T(8,128)(2,1)} %k_own.3) | copy-start | bytes 1572868
  2.4 15.0 %collective-permute-start.1 = (bf16[256,512]{1,0:T(8,128)(2,1)}, bf16[256,512]{1,0:T(8,128)(2,1)S(1)}, u32[]{:S(2)}, u32[]{:S(2)}) collective-permute-start(bf16[256,512]{1,0:T(8,128)(2,1)} %pad_maximum_fusion.10), channel_id=1, source_target_pairs={{0,1},{1,0},{2,3},{3,2},{4,5},{5,4},{6,7},{7,6},{8,9},{9,8},{10,11... | collective-permute-start | bytes 786440 | tf_op jit(solution)/shard_map/ppermute | solution.py:306
  5.4 8.0 %copy-start = (bf16[128,4096]{1,0:T(8,128)(2,1)S(1)}, bf16[128,4096]{1,0:T(8,128)(2,1)}, u32[]{:S(2)}) copy-start(bf16[128,4096]{1,0:T(8,128)(2,1)} %q_own.3) | copy-start | bytes 3145732
  6.4 7.0 %copy-start.1 = (bf16[128,4096]{1,0:T(8,128)(2,1)S(1)}, bf16[128,4096]{1,0:T(8,128)(2,1)}, u32[]{:S(2)}) copy-start(bf16[128,4096]{1,0:T(8,128)(2,1)} %g_own.3) | copy-start | bytes 3145732
  7.1 13.1 %collective-permute-start.6 = (bf16[256,512]{1,0:T(8,128)(2,1)}, bf16[256,512]{1,0:T(8,128)(2,1)S(1)}, u32[]{:S(2)}, u32[]{:S(2)}) collective-permute-start(bf16[256,512]{1,0:T(8,128)(2,1)} %pad_maximum_fusion.11), channel_id=1, source_target_pairs={{0,1},{1,0},{2,3},{3,2},{4,5},{5,4},{6,7},{7,6},{8,9},{9,8},{10,11... | collective-permute-start | bytes 786440 | tf_op jit(solution)/shard_map/ppermute | solution.py:306
  8.8 15.0 %collective-permute-start.2 = (bf16[256,512]{1,0:T(8,128)(2,1)}, bf16[256,512]{1,0:T(8,128)(2,1)}, u32[]{:S(2)}, u32[]{:S(2)}) collective-permute-start(bf16[256,512]{1,0:T(8,128)(2,1)} %pad_maximum_fusion.12), channel_id=1, source_target_pairs={{0,4},{2,6},{4,8},{6,10},{8,12},{10,14},{12,16},{14,18},{16,20},{1... | collective-permute-start | bytes 786440 | tf_op jit(solution)/shard_map/ppermute | solution.py:315
  14.3 15.4 %collective-permute-start = (bf16[256,1024]{1,0:T(8,128)(2,1)}, bf16[256,1024]{1,0:T(8,128)(2,1)}, u32[]{:S(2)}, u32[]{:S(2)}) collective-permute-start(bf16[256,1024]{1,0:T(8,128)(2,1)} %pad_maximum_fusion.4), channel_id=1, source_target_pairs={{0,1},{1,0},{2,3},{3,2},{4,5},{5,4},{6,7},{7,6},{8,9},{9,8},{10,11... | collective-permute-start | bytes 1572872 | tf_op jit(solution)/shard_map/ppermute | solution.py:306
  15.9 24.2 %collective-permute-start.5 = (bf16[256,1024]{1,0:T(8,128)(2,1)S(1)}, bf16[256,1024]{1,0:T(8,128)(2,1)}, u32[]{:S(2)}, u32[]{:S(2)}) collective-permute-start(bf16[256,1024]{1,0:T(8,128)(2,1)S(1)} %pad_maximum_fusion.6), channel_id=1, source_target_pairs={{0,1},{1,0},{2,3},{3,2},{4,5},{5,4},{6,7},{7,6},{8,9},{9,8},{10,11... | collective-permute-start | bytes 1572872 | tf_op jit(solution)/shard_map/ppermute | solution.py:306
  17.5 9.4 %collective-permute-start.3 = (bf16[256,512]{1,0:T(8,128)(2,1)S(1)}, bf16[256,512]{1,0:T(8,128)(2,1)S(1)}, u32[]{:S(2)}, u32[]{:S(2)}) collective-permute-start(bf16[256,512]{1,0:T(8,128)(2,1)S(1)} %collective-permute-done.1.kv_other), channel_id=1, source_target_pairs={{0,4},{2,6},{4,8},{6,10},{8,12},{10,14},{12,16},{14,18},{16,20},{1... | collective-permute-start | bytes 786440 | tf_op jit(solution)/shard_map/ppermute | solution.py:315
  20.3 19.7 %collective-permute-start.7 = (bf16[512,512]{1,0:T(8,128)(2,1)S(1)}, bf16[512,512]{1,0:T(8,128)(2,1)S(1)}, u32[]{:S(2)}, u32[]{:S(2)}) collective-permute-start(bf16[512,512]{1,0:T(8,128)(2,1)S(1)} %pad_maximum_fusion.7), channel_id=1, source_target_pairs={{0,4},{2,6},{4,8},{6,10},{8,12},{10,14},{12,16},{14,18},{16,20},{1... | collective-permute-start | bytes 1572872 | tf_op jit(solution)/shard_map/ppermute | solution.py:315
  23.9 3.1 %copy-start.13 = (s32[2,6]{1,0:T(2,128)S(1)}, s32[2,6]{1,0:T(2,128)}, u32[]{:S(2)}) copy-start(s32[2,6]{1,0:T(2,128)} %param.11) | copy-start | bytes 148
  23.9 3.1 %copy-start.14 = (s32[2,6]{1,0:T(2,128)S(1)}, s32[2,6]{1,0:T(2,128)}, u32[]{:S(2)}) copy-start(s32[2,6]{1,0:T(2,128)} %param.10) | copy-start | bytes 148
  26.8 2.8 %copy-start.5 = (bf16[256,512]{1,0:T(8,128)(2,1)}, bf16[256,512]{1,0:T(8,128)(2,1)S(1)}, u32[]{:S(2)}) copy-start(bf16[256,512]{1,0:T(8,128)(2,1)S(1)} %collective-permute-done.3.kv2_other) | copy-start | bytes 786436
  26.9 2.7 %collective-permute-start.4 = (bf16[512,512]{1,0:T(8,128)(2,1)S(1)}, bf16[512,512]{1,0:T(8,128)(2,1)S(1)}, u32[]{:S(2)}, u32[]{:S(2)}) collective-permute-start(bf16[512,512]{1,0:T(8,128)(2,1)S(1)} %pad_maximum_fusion.5), channel_id=1, source_target_pairs={{0,2},{2,0},{4,6},{6,4},{8,10},{10,8},{12,14},{14,12},{16,18},{18,... | collective-permute-start | bytes 1572872 | tf_op jit(solution)/shard_map/ppermute | solution.py:310
  29.7 0.8 %copy-start.12 = (bf16[512,512]{1,0:T(8,128)(2,1)}, bf16[512,512]{1,0:T(8,128)(2,1)S(1)}, u32[]{:S(2)}) copy-start(bf16[512,512]{1,0:T(8,128)(2,1)S(1)} %collective-permute-done.4.kv1) | copy-start | bytes 1572868
  40.1 1.5 %collective-permute-start.8 = (bf16[256,512]{1,0:T(8,128)(2,1)S(1)}, bf16[256,512]{1,0:T(8,128)(2,1)S(1)}, u32[]{:S(2)}, u32[]{:S(2)}) collective-permute-start(bf16[256,512]{1,0:T(8,128)(2,1)S(1)} %get-tuple-element.66), channel_id=1, source_target_pairs={{0,2},{2,0},{4,6},{6,4},{8,10},{10,8},{12,14},{14,12},{16,18},{18,... | collective-permute-start | bytes 786440 | tf_op jit(solution)/shard_map/ppermute | solution.py:310
  40.1 1.9 %collective-permute-start.9 = (bf16[256,512]{1,0:T(8,128)(2,1)S(1)}, bf16[256,512]{1,0:T(8,128)(2,1)S(1)}, u32[]{:S(2)}, u32[]{:S(2)}) collective-permute-start(bf16[256,512]{1,0:T(8,128)(2,1)S(1)} %get-tuple-element.68), channel_id=1, source_target_pairs={{0,2},{2,0},{4,6},{6,4},{8,10},{10,8},{12,14},{14,12},{16,18},{18,... | collective-permute-start | bytes 786440 | tf_op jit(solution)/shard_map/ppermute | solution.py:310
  40.6 2.3 %copy-start.3 = (bf16[256,512]{1,0:T(8,128)(2,1)}, bf16[256,512]{1,0:T(8,128)(2,1)S(1)}, u32[]{:S(2)}) copy-start(bf16[256,512]{1,0:T(8,128)(2,1)S(1)} %get-tuple-element.71.kv2_other) | copy-start | bytes 786436
  40.6 2.3 %copy-start.4 = (bf16[256,512]{1,0:T(8,128)(2,1)}, bf16[256,512]{1,0:T(8,128)(2,1)S(1)}, u32[]{:S(2)}) copy-start(bf16[256,512]{1,0:T(8,128)(2,1)S(1)} %get-tuple-element.70.kv2_own) | copy-start | bytes 786436
  42.9 3.6 %collective-permute-start.10 = (bf16[512,512]{1,0:T(8,128)(2,1)}, bf16[512,512]{1,0:T(8,128)(2,1)}, u32[]{:S(2)}, u32[]{:S(2)}) collective-permute-start(bf16[512,512]{1,0:T(8,128)(2,1)} %pad_maximum_fusion.9), channel_id=1, source_target_pairs={{0,2},{2,0},{4,6},{6,4},{8,10},{10,8},{12,14},{14,12},{16,18},{18,... | collective-permute-start | bytes 1572872 | tf_op jit(solution)/shard_map/ppermute | solution.py:310
  43.3 16.2 %collective-permute-start.14 = (bf16[512,512]{1,0:T(8,128)(2,1)S(1)}, bf16[512,512]{1,0:T(8,128)(2,1)S(1)}, u32[]{:S(2)}, u32[]{:S(2)}) collective-permute-start(bf16[512,512]{1,0:T(8,128)(2,1)S(1)} %pad_maximum_fusion.8), channel_id=1, source_target_pairs={{4,0},{6,2},{8,4},{10,6},{12,8},{14,10},{16,12},{18,14},{20,16},{2... | collective-permute-start | bytes 1572872 | tf_op jit(solution)/shard_map/ppermute | solution.py:315
  44.6 14.9 %copy-start.7 = (f32[256,512]{1,0:T(8,128)S(1)}, f32[256,512]{1,0:T(8,128)}, u32[]{:S(2)}) copy-start(f32[256,512]{1,0:T(8,128)} %get-tuple-element.84) | copy-start | bytes 1572868
  44.6 19.8 %collective-permute-start.11 = (bf16[128,1024]{1,0:T(8,128)(2,1)S(1)}, bf16[128,1024]{1,0:T(8,128)(2,1)S(1)}, u32[]{:S(2)}, u32[]{:S(2)}) collective-permute-start(bf16[128,1024]{1,0:T(8,128)(2,1)S(1)} %get-tuple-element.73), channel_id=1, source_target_pairs={{0,1},{1,0},{2,3},{3,2},{4,5},{5,4},{6,7},{7,6},{8,9},{9,8},{10,11... | collective-permute-start | bytes 786440 | tf_op jit(solution)/shard_map/ppermute | solution.py:306
  55.7 8.8 %collective-permute-start.12 = (bf16[128,1024]{1,0:T(8,128)(2,1)S(1)}, bf16[128,1024]{1,0:T(8,128)(2,1)S(1)}, u32[]{:S(2)}, u32[]{:S(2)}) collective-permute-start(bf16[128,1024]{1,0:T(8,128)(2,1)S(1)} %get-tuple-element.74), channel_id=1, source_target_pairs={{0,1},{1,0},{2,3},{3,2},{4,5},{5,4},{6,7},{7,6},{8,9},{9,8},{10,11... | collective-permute-start | bytes 786440 | tf_op jit(solution)/shard_map/ppermute | solution.py:306
  56.3 3.4 %collective-permute-start.13 = (bf16[256,512]{1,0:T(8,128)(2,1)S(1)}, bf16[256,512]{1,0:T(8,128)(2,1)S(1)}, u32[]{:S(2)}, u32[]{:S(2)}) collective-permute-start(bf16[256,512]{1,0:T(8,128)(2,1)S(1)} %get-tuple-element.76), channel_id=1, source_target_pairs={{0,2},{2,0},{4,6},{6,4},{8,10},{10,8},{12,14},{14,12},{16,18},{18,... | collective-permute-start | bytes 786440 | tf_op jit(solution)/shard_map/ppermute | solution.py:310
  56.3 6.7 %collective-permute-start.15 = (bf16[256,512]{1,0:T(8,128)(2,1)S(1)}, bf16[256,512]{1,0:T(8,128)(2,1)S(1)}, u32[]{:S(2)}, u32[]{:S(2)}) collective-permute-start(bf16[256,512]{1,0:T(8,128)(2,1)S(1)} %get-tuple-element.79), channel_id=1, source_target_pairs={{0,2},{2,0},{4,6},{6,4},{8,10},{10,8},{12,14},{14,12},{16,18},{18,... | collective-permute-start | bytes 786440 | tf_op jit(solution)/shard_map/ppermute | solution.py:310
  59.6 1.5 %copy-start.6 = (f32[256,512]{1,0:T(8,128)S(1)}, f32[256,512]{1,0:T(8,128)}, u32[]{:S(2)}) copy-start(f32[256,512]{1,0:T(8,128)} %get-tuple-element.86) | copy-start | bytes 1572868
  59.8 11.7 %collective-permute-start.18 = (bf16[256,512]{1,0:T(8,128)(2,1)S(1)}, bf16[256,512]{1,0:T(8,128)(2,1)S(1)}, u32[]{:S(2)}, u32[]{:S(2)}) collective-permute-start(bf16[256,512]{1,0:T(8,128)(2,1)S(1)} %fusion.11), channel_id=1, source_target_pairs={{4,0},{6,2},{8,4},{10,6},{12,8},{14,10},{16,12},{18,14},{20,16},{2... | collective-permute-start | bytes 786440 | tf_op jit(solution)/shard_map/ppermute | solution.py:315
  61.2 14.9 %collective-permute-start.17 = (bf16[256,512]{1,0:T(8,128)(2,1)S(1)}, bf16[256,512]{1,0:T(8,128)(2,1)S(1)}, u32[]{:S(2)}, u32[]{:S(2)}) collective-permute-start(bf16[256,512]{1,0:T(8,128)(2,1)S(1)} %fusion.9), channel_id=1, source_target_pairs={{0,1},{1,0},{2,3},{3,2},{4,5},{5,4},{6,7},{7,6},{8,9},{9,8},{10,11... | collective-permute-start | bytes 786440 | tf_op jit(solution)/shard_map/ppermute | solution.py:306
  63.1 12.9 %collective-permute-start.16 = (bf16[256,512]{1,0:T(8,128)(2,1)S(1)}, bf16[256,512]{1,0:T(8,128)(2,1)S(1)}, u32[]{:S(2)}, u32[]{:S(2)}) collective-permute-start(bf16[256,512]{1,0:T(8,128)(2,1)S(1)} %fusion.16), channel_id=1, source_target_pairs={{4,0},{6,2},{8,4},{10,6},{12,8},{14,10},{16,12},{18,14},{20,16},{2... | collective-permute-start | bytes 786440 | tf_op jit(solution)/shard_map/ppermute | solution.py:315
  64.5 7.0 %copy-start.9 = (f32[256,512]{1,0:T(8,128)S(1)}, f32[256,512]{1,0:T(8,128)}, u32[]{:S(2)}) copy-start(f32[256,512]{1,0:T(8,128)} %get-tuple-element.89) | copy-start | bytes 1572868
  65.7 10.2 %copy-start.8 = (f32[256,512]{1,0:T(8,128)S(1)}, f32[256,512]{1,0:T(8,128)}, u32[]{:S(2)}) copy-start(f32[256,512]{1,0:T(8,128)} %get-tuple-element.85) | copy-start | bytes 1572868
  71.6 6.4 %collective-permute-start.19 = (bf16[256,512]{1,0:T(8,128)(2,1)S(1)}, bf16[256,512]{1,0:T(8,128)(2,1)S(1)}, u32[]{:S(2)}, u32[]{:S(2)}) collective-permute-start(bf16[256,512]{1,0:T(8,128)(2,1)S(1)} %fusion.14), channel_id=1, source_target_pairs={{0,1},{1,0},{2,3},{3,2},{4,5},{5,4},{6,7},{7,6},{8,9},{9,8},{10,11... | collective-permute-start | bytes 786440 | tf_op jit(solution)/shard_map/ppermute | solution.py:306
  78.1 0.8 %copy-start.10 = (bf16[128,2048]{1,0:T(8,128)(2,1)}, bf16[128,2048]{1,0:T(8,128)(2,1)S(1)}, u32[]{:S(2)}) copy-start(bf16[128,2048]{1,0:T(8,128)(2,1)S(1)} %get-tuple-element.95) | copy-start | bytes 1572868
  78.1 1.0 %copy-start.11 = (bf16[128,2048]{1,0:T(8,128)(2,1)}, bf16[128,2048]{1,0:T(8,128)(2,1)S(1)}, u32[]{:S(2)}) copy-start(bf16[128,2048]{1,0:T(8,128)(2,1)S(1)} %get-tuple-element.96) | copy-start | bytes 1572868
